TPU v7x, 32 devices: a whole 2x2x4 slice. The times are simulated.
32 devices in a mesh: lat: 8 (over z, y), lon: 4 (over x, core).
Axes of the slice: x: 2, y: 2, z: 4, core: 2. Of those that a mesh axis runs over, the one named last changes fastest.
Arguments:
- grid_state: bfloat16 [16, 720, 640], P('lat', 'lon'), may hold values from -6 to 6
- conv_weight: float32 [3, 3, 640], replicated, may hold values from -2.4 to 2.4
- spectral_gain: float32 [2, 256, 640], P(None, None, 'lon'), may hold values from -4 to 4
- spectral_weight: bfloat16 [2, 640, 640], P(None, None, 'lon'), may hold values from -0.125 to 0.125
- norm_gain: float32 [640], replicated, may hold values from 0.1 to 1.9
- expand_weight: bfloat16 [640, 1280], replicated, may hold values from -0.25 to 0.25
- reduce_weight: bfloat16 [1280, 640], replicated, may hold values from -0.15625 to 0.15625
Outputs:
- block_output: bfloat16 [16, 720, 640], P('lat', 'lon')
All inputs are finite; a program needn't handle non-finite values.
Results may differ from a plain program's by a relative error of at most 0.015.
Values may be sent and summed in bfloat16 or wider, within the bound.
No kernel may reach another device: no remote copies, remote signals or barrier semaphores. Data moves between devices by JAX's collectives and lax.ppermute only.
A program may use at most 128 MiB of HBM per device.

v0:
```python
import math

import jax
import jax.numpy as jnp
from jax import lax
from jax.sharding import PartitionSpec as P

M = 256


norm_eps = 1e-06
underflow_cut = -60.0
degree_block = 16


def padded_2(value, sides, width, wrap):
    for axis, dim in sides:
        count, length = (lax.axis_size(axis), value.shape[dim])
        up = [(i, (i + 1) % count) for i in range(count if wrap else count - 1)]
        down = [(j, i) for i, j in up]
        last = lax.slice_in_dim(value, length - width, length, axis=dim)
        initial = lax.slice_in_dim(value, 0, width, axis=dim)
        before = lax.ppermute(last, axis, up)
        after = lax.ppermute(initial, axis, down)
        value = jnp.concatenate([before, value, after], axis=dim)
    return value


def legendre_table(orders, lat_total, degree_count):
    colatitude = (jnp.arange(lat_total, dtype=jnp.float32) + 0.5) * (math.pi / lat_total)
    cosines = jnp.cos(colatitude)
    sine_values = jnp.sin(colatitude)
    rank_values = jnp.arange(1, degree_count + 1, dtype=jnp.int32)
    rank_float = rank_values.astype(jnp.float32)
    log_terms = 0.5 * jnp.log((2.0 * rank_float + 1.0) / (2.0 * rank_float))
    log_norm = jnp.sum(
        jnp.where(rank_values[None, :] <= orders[:, None], log_terms[None, :], jnp.float32(0.0)),
        axis=1,
    )
    order_float = orders.astype(jnp.float32)[:, None]
    log_start = (
        -0.5 * math.log(4.0 * math.pi)
        + log_norm[:, None]
        + order_float * jnp.log(sine_values)[None, :]
    )
    start_value = jnp.where(
        log_start > underflow_cut, jnp.exp(jnp.maximum(log_start, underflow_cut)), jnp.float32(0.0)
    )

    def advance_block(totals, block_start):
        previous, earlier = totals
        rows_out = []
        for inner in range(degree_block):
            degree = block_start + inner
            degree_float = degree.astype(jnp.float32)
            raise_coef = jnp.sqrt(
                jnp.maximum(4.0 * degree_float * degree_float - 1.0, 0.0)
                / jnp.maximum(degree_float * degree_float - order_float * order_float, 1.0)
            )
            lower_coef = jnp.sqrt(
                jnp.maximum((degree_float - 1.0) ** 2 - order_float * order_float, 0.0)
                / jnp.maximum(4.0 * (degree_float - 1.0) ** 2 - 1.0, 1.0)
            )
            recurred = raise_coef * (cosines[None, :] * previous - lower_coef * earlier)
            current = jnp.where(
                degree < orders[:, None],
                jnp.float32(0.0),
                jnp.where(degree == orders[:, None], start_value, recurred),
            )
            earlier = previous
            previous = current
            rows_out.append(current)
        return ((previous, earlier), jnp.stack(rows_out, axis=0))

    blank = jnp.zeros((orders.shape[0], lat_total), jnp.float32)
    starts = jnp.arange(0, degree_count, degree_block, dtype=jnp.int32)
    unused, table_blocks = lax.scan(advance_block, (blank, blank), starts)
    return table_blocks.reshape(degree_count, orders.shape[0], lat_total)


def quadrature(lat_total):
    colatitude = (jnp.arange(lat_total, dtype=jnp.float32) + 0.5) * (math.pi / lat_total)
    return 2.0 * math.pi * math.pi / lat_total * jnp.sin(colatitude)


def fourier_table(longitudes, lon_total, mode_count):
    mode_index = jnp.arange(mode_count, dtype=jnp.int32)
    phase_index = longitudes[:, None] * mode_index[None, :] % lon_total
    angles = phase_index.astype(jnp.float32) * (2.0 * math.pi / lon_total)
    return (jnp.stack([jnp.cos(angles), -jnp.sin(angles)], axis=1) / lon_total).astype(jnp.bfloat16)


def synthesis_table(longitudes, lon_total, mode_count):
    mode_index = jnp.arange(mode_count, dtype=jnp.int32)
    phase_index = mode_index[:, None] * longitudes[None, :] % lon_total
    angles = phase_index.astype(jnp.float32) * (2.0 * math.pi / lon_total)
    doubling = jnp.where(mode_index == 0, 1.0, 2.0).astype(jnp.float32)[:, None]
    return jnp.stack([doubling * jnp.cos(angles), -doubling * jnp.sin(angles)], axis=0).astype(
        jnp.bfloat16
    )


def shards(
    grid_state, conv_weight, spectral_gain, spectral_weight, norm_gain, expand_weight, reduce_weight
):
    lat_rows, sector_width, channel_total = grid_state.shape
    lat_count = lax.axis_size("lat")
    lon_count = lax.axis_size("lon")
    lat_total = lat_rows * lat_count
    lon_total = sector_width * lon_count
    mode_count = M
    order_share = mode_count // lat_count
    channel_share = channel_total // lon_count
    lat_position = lax.axis_index("lat")
    wrapped = padded_2(grid_state, (("lon", 1),), 1, True)
    padded = padded_2(wrapped, (("lat", 0),), 1, False)
    padded_wide = padded.astype(jnp.float32)
    filtered = jnp.zeros((lat_rows, sector_width, channel_total), jnp.float32)
    for row_shift in range(3):
        for col_shift in range(3):
            filtered = (
                filtered
                + conv_weight[row_shift, col_shift]
                * padded_wide[
                    row_shift : row_shift + lat_rows, col_shift : col_shift + sector_width
                ]
            )
    first_section = (grid_state.astype(jnp.float32) + jax.nn.gelu(filtered)).astype(jnp.bfloat16)
    gathered = lax.all_to_all(first_section, "lon", split_axis=2, concat_axis=1, tiled=True)
    forward_table = fourier_table(jnp.arange(lon_total, dtype=jnp.int32), lon_total, mode_count)
    spectrum = jnp.einsum(
        "tpc,prm->tmrc", gathered, forward_table, preferred_element_type=jnp.float32
    ).astype(jnp.bfloat16)
    cycle_spectrum = lax.all_to_all(spectrum, "lat", split_axis=1, concat_axis=0, tiled=True)
    orders = lat_position * order_share + jnp.arange(order_share, dtype=jnp.int32)
    legendre = legendre_table(orders, lat_total, mode_count)
    analysis_table = (legendre * quadrature(lat_total)[None, None, :]).astype(jnp.bfloat16)
    coefficients = jnp.einsum(
        "lmt,tmrc->lmrc", analysis_table, cycle_spectrum, preferred_element_type=jnp.float32
    )
    gain_real = spectral_gain[0][:, None, :]
    gain_imag = spectral_gain[1][:, None, :]
    coef_real = coefficients[:, :, 0, :]
    coef_imag = coefficients[:, :, 1, :]
    gained = jnp.stack(
        [
            gain_real * coef_real - gain_imag * coef_imag,
            gain_real * coef_imag + gain_imag * coef_real,
        ],
        axis=2,
    ).astype(jnp.bfloat16)
    blank = jnp.zeros((mode_count * order_share, channel_share), jnp.float32)
    portion = lax.all_gather(gained, "lon", axis=3, tiled=True)
    width_part = portion.shape[3]
    weight_rows = lax.slice_in_dim(spectral_weight, 0, width_part, axis=1)
    real_part = portion[:, :, 0, :].reshape(-1, width_part)
    imag_part = portion[:, :, 1, :].reshape(-1, width_part)
    real_sum = (
        blank
        + jnp.dot(real_part, weight_rows[0], preferred_element_type=jnp.float32)
        - jnp.dot(imag_part, weight_rows[1], preferred_element_type=jnp.float32)
    )
    imag_sum = (
        blank
        + jnp.dot(real_part, weight_rows[1], preferred_element_type=jnp.float32)
        + jnp.dot(imag_part, weight_rows[0], preferred_element_type=jnp.float32)
    )
    mixed = jnp.stack(
        [
            real_sum.reshape(mode_count, order_share, channel_share),
            imag_sum.reshape(mode_count, order_share, channel_share),
        ],
        axis=2,
    ).astype(jnp.bfloat16)
    synthesis_legendre = legendre.astype(jnp.bfloat16)
    cycle_modes = jnp.einsum(
        "lmt,lmrc->tmrc", synthesis_legendre, mixed, preferred_element_type=jnp.float32
    ).astype(jnp.bfloat16)
    band_modes = lax.all_to_all(cycle_modes, "lat", split_axis=0, concat_axis=1, tiled=True)
    inverse_table = synthesis_table(jnp.arange(lon_total, dtype=jnp.int32), lon_total, mode_count)
    all_lons = jnp.einsum(
        "tmrc,rmp->tpc", band_modes, inverse_table, preferred_element_type=jnp.float32
    )
    spectral_out = lax.all_to_all(
        all_lons.astype(jnp.bfloat16), "lon", split_axis=1, concat_axis=2, tiled=True
    ).astype(all_lons.dtype)
    second_section = (first_section.astype(jnp.float32) + spectral_out).astype(jnp.bfloat16)
    second_wide = second_section.astype(jnp.float32)
    scale_values = lax.rsqrt(jnp.mean(second_wide * second_wide, axis=-1, keepdims=True) + norm_eps)
    normed = (second_wide * norm_gain * scale_values).astype(jnp.bfloat16)
    flat_rows = normed.reshape(-1, channel_total)
    hidden = jax.nn.gelu(
        jnp.dot(flat_rows, expand_weight, preferred_element_type=jnp.float32)
    ).astype(jnp.bfloat16)
    update = jnp.dot(hidden, reduce_weight, preferred_element_type=jnp.float32)
    block_output = (second_wide.reshape(-1, channel_total) + update).astype(jnp.bfloat16)
    return block_output.reshape(lat_rows, sector_width, channel_total)


def solution(mesh):
    return jax.shard_map(
        shards,
        mesh=mesh,
        in_specs=(
            P("lat", "lon", None),
            P(),
            P(None, None, "lon"),
            P(None, None, "lon"),
            P(),
            P(),
            P(),
        ),
        out_specs=P("lat", "lon", None),
        check_vma=False,
    )
```

profile of v0, /device:TPU:0, one launch (start us, length us, event | category | flops | bytes accessed | tf_op | source)
XLA Modules:
  0.0 599.7 jit_solution(16794127039909674058)
XLA Ops:
  6.5 1.2 copy.61
  8.3 2.0 collective-permute-start.1
  10.3 0.9 slice_reduce_fusion.8
  11.8 4.3 collective-permute-start.2
  16.1 1.3 collective-permute-start.3
  17.5 4.3 sine_negate_fusion
  21.7 4.6 collective-permute-done.3
  26.4 1.1 fusion.108
  27.6 1.8 copy.65
  29.3 3.5 all-to-all-start
  33.1 10.0 %all-to-all-done = bf16[2,180,640]{1,0,2:T(2,128)(2,1)S(1)} async-done(((bf16[2,180,640]{1,0,2:T(2,128)(2,1)}), bf16[2,180,640]{1,0,2:T(2,128)(2,1)S(1)}, u32[]{:S(2)}, u32[]{:S(2)}) %all-to-all-start) | async-done | bytes 460832 | tf_op jit(solution)/shard_map/all_to_all | solution.py:129
  44.0 1.8 fusion.99
  45.8 1.2 copy.68
  46.9 7.7 %all-to-all-start.1 = ((bf16[2,256,2,160]{3,0,2,1:T(2,128)(2,1)}), bf16[2,256,2,160]{3,0,2,1:T(2,128)(2,1)S(1)}, u32[]{:S(2)}, u32[]{:S(2)}) async-start(bf16[2,256,2,160]{3,0,2,1:T(2,128)(2,1)} %copy.68), calls=%async_computation.1 | async-start | bytes 1048576 | tf_op jit(solution)/shard_map/all_to_all | solution.py:134
  54.8 231.6 %while.21 = (s32[]{:T(128)}, f32[32,16]{0,1:T(8,128)S(1)}, f32[32,16]{0,1:T(8,128)S(1)}, f32[16,16,32,16]{2,3,1,0:T(8,128)}, s32[16]{0:T(128)S(1)}, /*index=5*/s...) while((s32[]{:T(128)}, f32[32,16]{0,1:T(8,128)S(1)}, ...), condition=%wide.region_2.3_spmd.clone.clone.clone.clone, body=%wide.region_1.2_spmd.clone.clone.clone.clone.sunk | while | flops 140513 | bytes 765066 | solution.py:77
  68.7 0.7 bitcast_dynamic-update-slice_fusion.2
  71.3 0.6 fusion.209
  83.1 0.7 bitcast_dynamic-update-slice_fusion.2
  97.6 0.7 bitcast_dynamic-update-slice_fusion.2
  100.2 0.6 fusion.209
  112.1 0.7 bitcast_dynamic-update-slice_fusion.2
  126.6 0.7 bitcast_dynamic-update-slice_fusion.2
  129.2 0.6 fusion.209
  141.0 0.7 bitcast_dynamic-update-slice_fusion.2
  143.7 0.6 fusion.209
  155.5 0.7 bitcast_dynamic-update-slice_fusion.2
  170.0 0.7 bitcast_dynamic-update-slice_fusion.2
  184.5 0.7 bitcast_dynamic-update-slice_fusion.2
  199.0 0.7 bitcast_dynamic-update-slice_fusion.2
  213.4 0.7 bitcast_dynamic-update-slice_fusion.2
  227.9 0.7 bitcast_dynamic-update-slice_fusion.2
  242.4 0.7 bitcast_dynamic-update-slice_fusion.2
  256.9 0.7 bitcast_dynamic-update-slice_fusion.2
  271.3 0.7 bitcast_dynamic-update-slice_fusion.2
  285.8 0.7 bitcast_dynamic-update-slice_fusion.2
  286.5 2.7 copy.71
  290.4 1.6 convolution_bitcast_fusion
  292.0 1.7 subtract_convert_fusion
  293.7 2.8 pad_maximum_fusion
  296.5 132.0 %all-gather.2.cloned.1.call-done = bf16[256,32,2,640]{0,3,2,1:T(8,128)(2,1)} async-done(((bf16[256,32,2,160]{0,3,2,1:T(8,128)(2,1)}), bf16[256,32,2,640]{0,3,2,1:T(8,128)(2,1)}) %all-gather.2.cloned.1.call-update) | async-done | bytes 20971536 | tf_op jit(solution)/shard_map/all_gather | solution.py:153
  428.5 16.3 %fusion.178 = (bf16[256,32,1,640]{0,3,2,1:T(8,128)(2,1)}, bf16[256,32,1,640]{0,3,2,1:T(8,128)(2,1)}) fusion(bf16[256,32,2,640]{0,3,2,1:T(8,128)(2,1)} %all-gather.2.cloned.1.call-done), kind=kLoop, calls=%fused_computation.269 | loop fusion | bytes 41943040 | tf_op jit(solution)/shard_map/slice | solution.py:157
  444.9 16.5 %copy.72 = bf16[256,32,1,640]{3,1,0,2:T(8,128)(2,1)} copy(bf16[256,32,1,640]{0,3,2,1:T(8,128)(2,1)} %get-tuple-element.516) | data formatting | bytes 20971520 | tf_op jit(solution)/shard_map/slice | solution.py:156
  461.4 10.0 %fusion.148 = f32[8192,160]{0,1:T(8,128)} fusion(bf16[8192,640]{1,0:T(8,128)(2,1)} %bitcast.250, bf16[2,640,160]{1,2,0:T(8,128)(2,1)S(1)} %copy-done.4), kind=kOutput, calls=%fused_computation.229 | convolution fusion | flops 1677721600 | bytes 15933440 | tf_op jit(solution)/shard_map/dot_general | solution.py:160
  471.4 5.8 fusion.144
  477.2 16.5 %copy.73 = bf16[256,32,1,640]{3,1,0,2:T(8,128)(2,1)} copy(bf16[256,32,1,640]{0,3,2,1:T(8,128)(2,1)} %get-tuple-element.515) | data formatting | bytes 20971520 | tf_op jit(solution)/shard_map/slice | solution.py:157
  493.7 10.5 %fusion.76 = bf16[8192,160]{0,1:T(8,128)(2,1)} fusion(f32[8192,160]{0,1:T(8,128)} %fusion.148, bf16[8192,640]{1,0:T(8,128)(2,1)} %bitcast.252, bf16[2,640,160]{1,2,0:T(8,128)(2,1)S(1)} %copy-done.4), kind=kOutput, calls=%fused_computation.129 | convolution fusion | flops 1680343040 | bytes 18554880 | tf_op jit(solution)/shard_map/dot_general | solution.py:161
  504.2 5.7 copy.74
  509.9 7.6 %copy.76 = bf16[256,32,1,160]{0,3,2,1:T(8,128)(2,1)} copy(bf16[256,32,1,160]{3,1,0,2:T(8,128)(2,1)} %bitcast.254) | data formatting | bytes 5242880 | tf_op jit(solution)/shard_map/stack;reshape | solution.py:168
  517.6 10.5 %fusion.75 = bf16[8192,160]{0,1:T(8,128)(2,1)} fusion(f32[8192,160]{0,1:T(8,128)} %fusion.144, bf16[8192,640]{1,0:T(8,128)(2,1)} %bitcast.253, bf16[2,640,160]{1,2,0:T(8,128)(2,1)S(1)} %copy-done.4), kind=kOutput, calls=%fused_computation.127 | convolution fusion | flops 1680343040 | bytes 18554880 | tf_op jit(solution)/shard_map/dot_general | solution.py:166
  528.1 5.7 copy.75
  533.8 7.6 %copy.77 = bf16[256,32,1,160]{0,3,2,1:T(8,128)(2,1)} copy(bf16[256,32,1,160]{3,1,0,2:T(8,128)(2,1)} %bitcast.255) | data formatting | bytes 5242880 | tf_op jit(solution)/shard_map/stack;reshape | solution.py:168
  541.3 4.0 fusion.95
  545.3 1.3 copy.79
  546.6 5.5 all-to-all-start.2
  552.2 4.1 multiply_convert_fusion.1
  556.3 10.8 %all-to-all-done.2 = bf16[16,32,2,160]{3,2,1,0:T(2,128)(2,1)S(1)} async-done(((bf16[16,32,2,160]{3,2,1,0:T(2,128)(2,1)}), bf16[16,32,2,160]{3,2,1,0:T(2,128)(2,1)S(1)}, u32[]{:S(2)}, u32[]{:S(2)}) %all-to-all-start.2) | async-done | bytes 327712 | tf_op jit(solution)/shard_map/all_to_all | solution.py:179
  567.2 1.5 fusion.98
  568.6 1.0 copy.82
  569.6 13.5 %all_to_all.63 = bf16[2,720,160]{2,0,1:T(2,128)(2,1)S(1)} all-to-all(bf16[2,720,160]{2,0,1:T(2,128)(2,1)S(1)} %copy.82), channel_id=1, replica_groups=mesh['lat'=8,'lon'=4] {'lon'}, dimensions={1} | all-to-all | bytes 921600 | tf_op jit(solution)/shard_map/all_to_all | solution.py:184
  583.4 1.9 reshape.1009
  585.4 1.5 multiply_reduce_fusion
  586.9 1.0 reshape.1006
  588.2 3.4 fusion.94
  591.7 1.1 copy.84
  (846 shorter events, 52.0 us)
Async XLA Ops:
  6.5 581.6 %copy-start = (bf16[1280,640]{1,0:T(8,128)(2,1)S(1)}, bf16[1280,640]{1,0:T(8,128)(2,1)}, u32[]{:S(2)}) copy-start(bf16[1280,640]{1,0:T(8,128)(2,1)} %param.15) | copy-start | bytes 4915204
  7.8 3.7 collective-permute-start
  8.3 3.3 collective-permute-start.1
  11.7 14.7 %copy-start.3 = (bf16[2,180,640]{2,0,1:T(2,128)(2,1)S(1)}, bf16[2,180,640]{2,0,1:T(2,128)(2,1)}, u32[]{:S(2)}) copy-start(bf16[2,180,640]{2,0,1:T(2,128)(2,1)} %param.9) | copy-start | bytes 1382404
  11.8 9.9 %collective-permute-start.2 = (bf16[1,182,640]{2,1,0:T(8,128)(2,1)S(1)}, bf16[1,182,640]{2,1,0:T(8,128)(2,1)S(1)}, u32[]{:S(2)}, u32[]{:S(2)}) collective-permute-start(bf16[1,182,640]{2,1,0:T(8,128)(2,1)S(1)} %get-tuple-element.519), channel_id=1, source_target_pairs={{0,4},{4,8},{8,12},{12,16},{16,20},{20,24},{24,28},{1,5},{5,9},{9,... | collective-permute-start | bytes 698888 | tf_op jit(solution)/shard_map/ppermute | solution.py:23
  16.1 10.2 %collective-permute-start.3 = (bf16[1,182,640]{2,1,0:T(8,128)(2,1)S(1)}, bf16[1,182,640]{2,1,0:T(8,128)(2,1)S(1)}, u32[]{:S(2)}, u32[]{:S(2)}) collective-permute-start(bf16[1,182,640]{2,1,0:T(8,128)(2,1)S(1)} %get-tuple-element.520), channel_id=1, source_target_pairs={{4,0},{8,4},{12,8},{16,12},{20,16},{24,20},{28,24},{5,1},{9,5},{13... | collective-permute-start | bytes 698888 | tf_op jit(solution)/shard_map/ppermute | solution.py:24
  27.6 5.3 copy-start.2
  29.3 13.7 %all-to-all-start = ((bf16[2,180,640]{1,0,2:T(2,128)(2,1)}), bf16[2,180,640]{1,0,2:T(2,128)(2,1)S(1)}, u32[]{:S(2)}, u32[]{:S(2)}) async-start(bf16[2,180,640]{1,0,2:T(2,128)(2,1)} %copy.65), calls=%async_computation | async-start | bytes 1310720 | tf_op jit(solution)/shard_map/all_to_all | solution.py:129
  46.9 242.4 %all-to-all-start.1 = ((bf16[2,256,2,160]{3,0,2,1:T(2,128)(2,1)}), bf16[2,256,2,160]{3,0,2,1:T(2,128)(2,1)S(1)}, u32[]{:S(2)}, u32[]{:S(2)}) async-start(bf16[2,256,2,160]{3,0,2,1:T(2,128)(2,1)} %copy.68), calls=%async_computation.1 | async-start | bytes 1048576 | tf_op jit(solution)/shard_map/all_to_all | solution.py:134
  54.6 373.9 %all-gather.2.cloned.1.call-start = ((), (), s32[]{:S(2)}) async-start(), calls=%async_computation.4 | async-start | bytes 26214400 | tf_op jit(solution)/shard_map/all_gather | solution.py:153
  286.5 2.8 copy-start.5
  444.9 16.6 %copy-start.4 = (bf16[2,640,160]{1,2,0:T(8,128)(2,1)S(1)}, bf16[2,640,160]{1,2,0:T(8,128)(2,1)}, u32[]{:S(2)}) copy-start(bf16[2,640,160]{1,2,0:T(8,128)(2,1)} %param.12) | copy-start | bytes 1228804
  461.4 10.0 %copy-start.1 = (bf16[256,32,1,640]{3,1,0,2:T(8,128)(2,1)S(1)}, bf16[256,32,1,640]{3,1,0,2:T(8,128)(2,1)}, u32[]{:S(2)}) copy-start(bf16[256,32,1,640]{3,1,0,2:T(8,128)(2,1)} %copy.72) | copy-start | bytes 31457284
  546.6 20.4 %all-to-all-start.2 = ((bf16[16,32,2,160]{3,2,1,0:T(2,128)(2,1)}), bf16[16,32,2,160]{3,2,1,0:T(2,128)(2,1)S(1)}, u32[]{:S(2)}, u32[]{:S(2)}) async-start(bf16[16,32,2,160]{3,2,1,0:T(2,128)(2,1)} %copy.79), calls=%async_computation.2 | async-start | bytes 1048576 | tf_op jit(solution)/shard_map/all_to_all | solution.py:179
  585.4 2.6 copy-start.6
Sparse Core Ops, SparseCore 0:
  296.6 131.8 all-gather.1
where the time goes:
time: 605 us; the launch traced here: 600 us
  loops' own time  171 us (28%)
  waiting for transfers between devices  158 us (26%)
  local copies, waits for them, and re-layouts  113 us (19%)
  other arithmetic  56.4 us (9%)
  matrix products  49.1 us (8%)
  starting transfers between devices  25 us (4%)
  between operations  13.7 us (2%)
  blocking collectives  13.5 us (2%)
    another operation x1, loops' own time, legendre_table(): unused, table_blocks = lax.scan(advance_block, (blank, blank), starts)  171 us
    all_gather x1, waiting for transfers between devices, shards(): portion = lax.all_gather(gained, 'lon', axis=3, tiled=True)  132 us
    slice x2, local copies, waits for them, and re-layouts, shards(): imag_part = portion[:, :, 1, :].reshape(-1, width_part)  32.8 us
    while x240, other arithmetic  21.3 us
    slice x1, local copies, waits for them, and re-layouts, shards(): real_part = portion[:, :, 0, :].reshape(-1, width_part)  16.5 us
    another operation x2, local copies, waits for them, and re-layouts, shards(): jnp.stack([real_sum.reshape(mode_count, order_share, channel_share), imag...  15.2 us
    all_to_all x1, blocking collectives, shards(): lax.all_to_all(all_lons.astype(jnp.bfloat16), 'lon', split_axis=1, concat...  13.5 us
    eq x256, other arithmetic, advance_block(): degree == orders[:, None]  12.8 us
  transfers between devices with their start and end apart: 8, of which 6 were waited for; matrix products, arithmetic and copies ran while one was open for 12% of the time, Pallas kernels for 0%

commit v1 on v0

--- a/solution.py
+++ b/solution.py
@@ -1,11 +1,17 @@
+import functools
 import math
 
 import jax
 import jax.numpy as jnp
+import numpy as np
 from jax import lax
+from jax.experimental import pallas as pl
+from jax.experimental.pallas import tpu as pltpu
+from jax.sharding import Mesh
 from jax.sharding import PartitionSpec as P
 
 M = 256
+LANES = 128
 
 
 norm_eps = 1e-06
@@ -100,7 +106,7 @@
     )
 
 
-def shards(
+def banded_shards(
     grid_state, conv_weight, spectral_gain, spectral_weight, norm_gain, expand_weight, reduce_weight
 ):
     lat_rows, sector_width, channel_total = grid_state.shape
@@ -197,19 +203,399 @@
     return block_output.reshape(lat_rows, sector_width, channel_total)
 
 
+def legendre_constant(lat_total, mode_count):
+    colatitude = (np.arange(lat_total // 2) + 0.5) * (math.pi / lat_total)
+    cosines, sines = np.cos(colatitude)[:, None], np.sin(colatitude)[:, None]
+    orders = np.arange(mode_count, dtype=np.float64)
+    ranks = np.arange(1, mode_count, dtype=np.float64)
+    log_terms = 0.5 * np.log((2.0 * ranks + 1.0) / (2.0 * ranks))
+    log_norm = np.concatenate([np.zeros(1), np.cumsum(log_terms)])
+    log_start = -0.5 * math.log(4.0 * math.pi) + log_norm + orders * np.log(sines)
+    start = np.where(
+        log_start > underflow_cut, np.exp(np.maximum(log_start, underflow_cut)), 0.0
+    )
+    table = np.zeros((lat_total // 2, mode_count, mode_count))
+    previous = np.zeros_like(start)
+    earlier = np.zeros_like(start)
+    for degree in range(mode_count):
+        raised = np.sqrt(
+            np.maximum(4.0 * degree * degree - 1.0, 0.0)
+            / np.maximum(degree * degree - orders * orders, 1.0)
+        )
+        lowered = np.sqrt(
+            np.maximum((degree - 1.0) ** 2 - orders * orders, 0.0)
+            / max(4.0 * (degree - 1.0) ** 2 - 1.0, 1.0)
+        )
+        recurred = raised * (cosines * previous - lowered * earlier)
+        current = np.where(degree < orders, 0.0, np.where(degree == orders, start, recurred))
+        earlier, previous = previous, current
+        table[:, degree, :] = current
+    return table
+
+
+def parity_tables(lat_total, mode_count):
+    table = legendre_constant(lat_total, mode_count)
+    return np.stack([table[:, :, 0::2], table[:, :, 1::2]]).astype(jnp.bfloat16)
+
+
+def analysis_constant(sectors, width, span, mode_count):
+    lon_total = sectors * width
+    out = np.zeros((2, sectors, span, 2, mode_count // 2))
+    for parity in range(2):
+        modes = np.arange(parity, mode_count, 2)
+        for sector in range(sectors):
+            longitudes = sector * width + np.arange(width)
+            angles = (longitudes[:, None] * modes[None, :] % lon_total) * (2 * math.pi / lon_total)
+            out[parity, sector, :width, 0] = np.cos(angles) / lon_total
+            out[parity, sector, :width, 1] = -np.sin(angles) / lon_total
+    return out.reshape(2, sectors, span, mode_count).astype(jnp.bfloat16)
+
+
+def synthesis_constant(sectors, width, padded, mode_count):
+    lon_total = sectors * width
+    out = np.zeros((sectors, 2, 2, padded, 2, mode_count // 2))
+    for sector in range(sectors):
+        longitudes = sector * width + np.arange(width)
+        for half in range(2):
+            modes = np.arange((sector + half) % 2, mode_count, 2)
+            doubling = np.where(modes == 0, 1.0, 2.0)[None, :]
+            angles = (longitudes[:, None] * modes[None, :] % lon_total) * (2 * math.pi / lon_total)
+            cosine, sine = doubling * np.cos(angles), doubling * np.sin(angles)
+            out[sector, half, 0, :width, 0] = cosine
+            out[sector, half, 0, :width, 1] = -sine
+            out[sector, half, 1, :width, 0] = sine
+            out[sector, half, 1, :width, 1] = cosine
+    return out.reshape(sectors, 2, 2 * padded, mode_count).astype(jnp.bfloat16)
+
+
+def gelu(value):
+    inner = value * (0.7978845608028654 + (0.7978845608028654 * 0.044715) * (value * value))
+    half = 0.5 * value
+    return half + half * jnp.tanh(inner)
+
+
+def pack_body(chips, share, width, grid_ref, out_ref, wide_ref):
+    span = wide_ref.shape[1]
+    tail = width // 8 * 8
+    flipped = []
+    for row in range(2):
+        wide_ref[row, tail:span, :] = jnp.zeros((span - tail, chips * share), jnp.float32)
+        wide_ref[row, 0:width, :] = grid_ref[row].astype(jnp.float32)
+        flipped.append(wide_ref[row].T)
+    rest = flipped[0][:, LANES:] + pltpu.roll(flipped[1][:, LANES:], width - LANES, axis=1)
+    for chip in range(chips):
+        at = slice(chip * share, (chip + 1) * share)
+        block = jnp.concatenate(
+            [flipped[0][at, :LANES], flipped[1][at, :LANES], rest[at]], axis=0
+        )
+        out_ref[chip] = block.astype(jnp.bfloat16)
+
+
+def spectral_body(
+    lat_count, columns, share, width,
+    parity_ref, own_ref, other_ref, gain_ref, tap_ref, legendre_ref, table_ref, out_ref,
+    field_ref, first_ref, modes_ref,
+):
+    lat_total = 2 * lat_count
+    north = lat_total // 2
+    sectors = 2 * columns
+    edge = width - LANES
+    orders = legendre_ref.shape[2]
+    parity = parity_ref[0]
+    for source, core in ((own_ref, parity), (other_ref, 1 - parity)):
+        for column in range(columns):
+            sector = 2 * column + core
+            for band in range(lat_count):
+                block = source[column * lat_count + band].astype(jnp.float32)
+                rest = block[2 * share :]
+                field_ref[sector, 2 * band, :, 0:LANES] = block[:share]
+                field_ref[sector, 2 * band, :, LANES:] = rest
+                field_ref[sector, 2 * band + 1, :, 0:LANES] = block[share : 2 * share]
+                field_ref[sector, 2 * band + 1, :, LANES:] = pltpu.roll(rest, LANES - edge, axis=1)
+
+    lane = lax.broadcasted_iota(jnp.int32, (8, LANES), 1)
+
+    def filter_sector(sector, unused):
+        after = lax.rem(sector + 1, sectors)
+        before = lax.rem(sector + sectors - 1, sectors)
+
+        def filter_rows(tile, unused):
+            rows = pl.ds(pl.multiple_of(tile * 8, 8), 8)
+            taps = []
+            for k in range(9):
+                tap = tap_ref[k, rows, :]
+                taps.append(jnp.concatenate([tap, tap], axis=1))
+            held, total, ahead = None, None, None
+
+            def finish(t, value, sum_):
+                first_ref[sector, pl.ds(pl.multiple_of(t * share + tile * 8, 8), 8), :] = value + gelu(sum_)
+
+            for t in range(lat_total):
+                low = field_ref[sector, t, rows, 0:LANES]
+                high = field_ref[sector, t, rows, LANES:]
+                right = pltpu.roll(field_ref[after, t, rows, 0:LANES], edge, axis=1)
+                left = pltpu.roll(field_ref[before, t, rows, LANES:], LANES - edge, axis=1)
+                high = jnp.where(lane == edge, right, jnp.where(lane == LANES - 1, left, high))
+                value = jnp.concatenate([low, high], axis=1)
+                west = pltpu.roll(value, 1, axis=1)
+                east = pltpu.roll(value, 2 * LANES - 1, axis=1)
+
+                def weigh(row):
+                    return (
+                        taps[3 * row] * west + taps[3 * row + 1] * value + taps[3 * row + 2] * east
+                    )
+
+                if t > 0:
+                    finish(t - 1, held, total + weigh(2))
+                total = weigh(1) if t == 0 else ahead + weigh(1)
+                ahead = weigh(0)
+                held = value
+            finish(lat_total - 1, held, total)
+            return unused
+
+        return lax.fori_loop(0, share // 8, filter_rows, unused)
+
+    lax.fori_loop(0, sectors, filter_sector, 0)
+
+    modes = None
+    for sector in range(sectors):
+        part = jnp.dot(
+            first_ref[sector].astype(jnp.bfloat16),
+            table_ref[sector],
+            preferred_element_type=jnp.float32,
+        )
+        modes = part if modes is None else modes + part
+    modes_ref[...] = modes
+
+    sign = (1 - 2 * parity).astype(jnp.float32)
+    folded = [[], []]
+    for t in range(north):
+        weight = 2.0 * math.pi * math.pi / lat_total * math.sin(math.pi * (t + 0.5) / lat_total)
+        upper = weight * modes_ref[t * share : (t + 1) * share, :]
+        mirror = lat_total - 1 - t
+        lower = (weight * sign) * modes_ref[mirror * share : (mirror + 1) * share, :]
+        folded[0].append(upper + lower)
+        folded[1].append(upper - lower)
+
+    sums = [[None] * north, [None] * north]
+
+    def add(half, t, kernel, value):
+        real = kernel[0] * value[:, :orders] - kernel[1] * value[:, orders:]
+        imag = kernel[0] * value[:, orders:] + kernel[1] * value[:, :orders]
+        had = sums[half][t]
+        sums[half][t] = (real, imag) if had is None else (had[0] + real, had[1] + imag)
+
+    for t in range(north):
+        products = jnp.concatenate(
+            [legendre_ref[t] * legendre_ref[s] for s in range(t, north)], axis=1
+        )
+        kernels = jnp.dot(gain_ref[...], products, preferred_element_type=jnp.float32)
+        for s in range(t, north):
+            at = slice((s - t) * orders, (s - t + 1) * orders)
+            for half in range(2):
+                base = 2 * half * share
+                kernel = (kernels[base : base + share, at], kernels[base + share : base + 2 * share, at])
+                add(half, t, kernel, folded[half][s])
+                if s != t:
+                    add(half, s, kernel, folded[half][t])
+
+    for t in range(north):
+        for part in range(2):
+            even, odd = sums[0][t][part], sums[1][t][part]
+            for place, value in ((t, even + odd), (lat_total - 1 - t, sign * (even - odd))):
+                at = (place % 2) * 2 * orders + part * orders
+                value = value.astype(jnp.bfloat16)
+                for column in range(columns):
+                    out_ref[column, place // 2, :, at : at + orders] = value
+
+
+def finish_body(
+    width, padded,
+    own_ref, other_ref, table_ref, mix_ref, first_ref, gain_ref, expand_ref, reduce_ref, out_ref,
+):
+    contract_last = (((1,), (1,)), ((), ()))
+    modes = table_ref.shape[2]
+    real, imag = [], []
+    for row in range(2):
+        at = slice(row * modes, (row + 1) * modes)
+        field = lax.dot_general(
+            table_ref[0], own_ref[:, at], contract_last, preferred_element_type=jnp.float32
+        ) + lax.dot_general(
+            table_ref[1], other_ref[:, at], contract_last, preferred_element_type=jnp.float32
+        )
+        real.append(field[:padded])
+        imag.append(field[padded:])
+    real = jnp.concatenate(real, axis=0).astype(jnp.bfloat16)
+    imag = jnp.concatenate(imag, axis=0).astype(jnp.bfloat16)
+    spectral_out = jnp.dot(real, mix_ref[0], preferred_element_type=jnp.float32) - jnp.dot(
+        imag, mix_ref[1], preferred_element_type=jnp.float32
+    )
+    second = (first_ref[...].astype(jnp.float32) + spectral_out).astype(jnp.bfloat16)
+    wide = second.astype(jnp.float32)
+    scale = lax.rsqrt(jnp.mean(wide * wide, axis=-1, keepdims=True) + norm_eps)
+    normed = (wide * gain_ref[...] * scale).astype(jnp.bfloat16)
+    hidden = gelu(jnp.dot(normed, expand_ref[...], preferred_element_type=jnp.float32))
+    update = jnp.dot(
+        hidden.astype(jnp.bfloat16), reduce_ref[...], preferred_element_type=jnp.float32
+    )
+    result = wide + update
+    for row in range(2):
+        out_ref[row] = result[row * padded : row * padded + width].astype(jnp.bfloat16)
+
+
+def in_vmem(count):
+    return [pl.BlockSpec(memory_space=pltpu.VMEM)] * count
+
+
+def chip_shards(
+    grid_state, conv_weight, spectral_gain, spectral_weight, norm_gain, expand_weight, reduce_weight
+):
+    lat_rows, width, channels = grid_state.shape
+    lat_count, columns = lax.axis_size("lat"), lax.axis_size("x")
+    chips, sectors = lat_count * columns, 2 * columns
+    share = channels // chips
+    lat_total = lat_rows * lat_count
+    orders = M // 2
+    span = 2 * LANES
+    padded = -(-width // 8) * 8
+    lat_at, column, core = lax.axis_index("lat"), lax.axis_index("x"), lax.axis_index("core")
+    swap = [(0, 1), (1, 0)]
+    over_chips = ("x", "lat")
+
+    packed = pl.pallas_call(
+        functools.partial(pack_body, chips, share, width),
+        out_shape=jax.ShapeDtypeStruct((chips, 3 * share, LANES), jnp.bfloat16),
+        in_specs=in_vmem(1),
+        out_specs=in_vmem(1)[0],
+        scratch_shapes=[pltpu.VMEM((2, span, channels), jnp.float32)],
+        compiler_params=pltpu.CompilerParams(vmem_limit_bytes=24 << 20),
+        name="pack",
+    )(grid_state)
+    own = lax.all_to_all(packed, over_chips, split_axis=0, concat_axis=0, tiled=True)
+    other = lax.ppermute(own, "core", swap)
+
+    lons = ("x", "core")
+    wrapped = padded_2(grid_state, ((lons, 1),), 1, True)
+    halo = padded_2(wrapped, (("lat", 0),), 1, False).astype(jnp.float32)
+    filtered = jnp.zeros(grid_state.shape, jnp.float32)
+    for row_shift in range(3):
+        for col_shift in range(3):
+            filtered = (
+                filtered
+                + conv_weight[row_shift, col_shift]
+                * halo[row_shift : row_shift + lat_rows, col_shift : col_shift + width]
+            )
+    first_section = (grid_state.astype(jnp.float32) + jax.nn.gelu(filtered)).astype(jnp.bfloat16)
+    first_rows = jnp.pad(first_section, ((0, 0), (0, padded - width), (0, 0))).reshape(-1, channels)
+
+    held = spectral_weight.shape[2]
+    across = lax.ppermute(spectral_weight, "x", [(i, (i + 1) % columns) for i in range(columns)])
+    pair = jnp.where(
+        column == 0, jnp.stack([spectral_weight, across]), jnp.stack([across, spectral_weight])
+    )
+    pair_other = lax.ppermute(pair, "core", swap)
+    quad = jnp.where(
+        core == 0,
+        jnp.stack([pair, pair_other], axis=1),
+        jnp.stack([pair_other, pair], axis=1),
+    )
+    mixing = jnp.concatenate(
+        [quad[i, j] for i in range(columns) for j in range(2)], axis=2
+    )
+
+    blocks = held // share
+    piece = lax.dynamic_slice_in_dim(
+        spectral_gain, (lat_at % blocks) * share, share, axis=2
+    ).transpose(0, 2, 1)
+    piece_other = lax.ppermute(piece, "core", swap)
+    gains = jnp.where(core == lat_at // blocks, piece, piece_other)
+    even = (jnp.arange(M) % 2 == 0)[None, :]
+    gain_rows = jnp.concatenate(
+        [
+            jnp.where(even, gains[0], 0.0),
+            jnp.where(even, gains[1], 0.0),
+            jnp.where(even, 0.0, gains[0]),
+            jnp.where(even, 0.0, gains[1]),
+        ],
+        axis=0,
+    ).astype(jnp.bfloat16)
+    chip = column * lat_count + lat_at
+    taps = lax.dynamic_slice_in_dim(conv_weight.reshape(9, channels), chip * share, share, axis=1)
+    taps = jnp.broadcast_to(taps[:, :, None], (9, share, LANES))
+
+    legendre = lax.dynamic_index_in_dim(
+        jnp.asarray(parity_tables(lat_total, M)), core, 0, keepdims=False
+    )
+    analysis = lax.dynamic_index_in_dim(
+        jnp.asarray(analysis_constant(sectors, width, span, M)), core, 0, keepdims=False
+    )
+    synthesis = lax.dynamic_index_in_dim(
+        jnp.asarray(synthesis_constant(sectors, width, padded, M)),
+        2 * column + core, 0, keepdims=False,
+    )
+
+    bands = pl.pallas_call(
+        functools.partial(spectral_body, lat_count, columns, share, width),
+        out_shape=jax.ShapeDtypeStruct((columns, lat_count, share, 2 * M), jnp.bfloat16),
+        in_specs=[pl.BlockSpec(memory_space=pltpu.SMEM)] + in_vmem(6),
+        out_specs=in_vmem(1)[0],
+        scratch_shapes=[
+            pltpu.VMEM((sectors, lat_total, share, span), jnp.float32),
+            pltpu.VMEM((sectors, lat_total * share, span), jnp.float32),
+            pltpu.VMEM((lat_total * share, M), jnp.float32),
+        ],
+        compiler_params=pltpu.CompilerParams(vmem_limit_bytes=40 << 20),
+        name="spectral",
+    )(core[None], own, other, gain_rows, taps, legendre, analysis)
+    back = lax.all_to_all(
+        bands.reshape(chips, share, 2 * M), over_chips, split_axis=0, concat_axis=0, tiled=True
+    ).reshape(channels, 2 * M)
+    back_other = lax.ppermute(back, "core", swap)
+
+    return pl.pallas_call(
+        functools.partial(finish_body, width, padded),
+        out_shape=jax.ShapeDtypeStruct(grid_state.shape, jnp.bfloat16),
+        in_specs=in_vmem(8),
+        out_specs=in_vmem(1)[0],
+        compiler_params=pltpu.CompilerParams(vmem_limit_bytes=40 << 20),
+        name="finish",
+    )(
+        back, back_other, synthesis, mixing, first_rows, norm_gain[None, :],
+        expand_weight, reduce_weight,
+    )
+
+
 def solution(mesh):
-    return jax.shard_map(
-        shards,
-        mesh=mesh,
-        in_specs=(
-            P("lat", "lon", None),
-            P(),
-            P(None, None, "lon"),
-            P(None, None, "lon"),
-            P(),
-            P(),
-            P(),
-        ),
-        out_specs=P("lat", "lon", None),
-        check_vma=False,
-    )
+    lat_count, lon_count = mesh.shape["lat"], mesh.shape["lon"]
+    columns = lon_count // 2
+    cored = Mesh(mesh.devices.reshape(lat_count, columns, 2), ("lat", "x", "core"))
+
+    def run(grid_state, *rest):
+        lat_total, lon_total, channels = grid_state.shape
+        chips = lat_count * columns
+        width = lon_total // lon_count
+        fits = (
+            columns == 2
+            and lat_total == 2 * lat_count
+            and lat_total <= 32
+            and channels % (8 * chips) == 0
+            and lat_count % 2 == 0
+            and (channels // lon_count) * 2 == (channels // chips) * lat_count
+            and LANES + 2 <= width
+            and 2 * (width - LANES) <= LANES
+        )
+        if fits:
+            body, on, lat, lon = chip_shards, cored, "lat", ("x", "core")
+        else:
+            body, on, lat, lon = banded_shards, mesh, "lat", "lon"
+        return jax.shard_map(
+            body,
+            mesh=on,
+            in_specs=(
+                P(lat, lon, None), P(), P(None, None, lon), P(None, None, lon), P(), P(), P(),
+            ),
+            out_specs=P(lat, lon, None),
+            check_vma=False,
+        )(grid_state, *rest)
+
+    return run

time: 605 us -> 105 us (0.17)
  loops' own time: 171 us -> 0 us
  waiting for transfers between devices: 158 us -> 22.6 us
  local copies, waits for them, and re-layouts: 113 us -> 17.9 us
  matrix products: 49.1 us -> 0 us
  other arithmetic: 56.4 us -> 26 us
  blocking collectives: 13.5 us -> 0 us
  between operations: 13.7 us -> 0.38 us
  Pallas kernels: 0 us -> 12.5 us
    another operation x1 -> x0, loops' own time: 171 us -> none  [legendre_table(): unused, table_blocks = lax.scan(advance_block, (blank, blank), starts)]
    all_gather x1 -> x0, waiting for transfers between devices: 132 us -> none  [shards(): portion = lax.all_gather(gained, 'lon', axis=3, tiled=True)]
    dot_general x9 -> x0, matrix products: 49.1 us -> none  [the longest x1 10.5 us: shards(): jnp.dot(imag_part, weight_rows[0], preferred_element_type=jnp.float32)]
    slice x4 -> x2, local copies, waits for them, and re-layouts: 50.3 us -> 1.25 us  [the longest x1 0.65 us: chip_shards(): conv_weight[row_shift, col_shift]]
    another operation x4 -> x0, local copies, waits for them, and re-layouts: 26.6 us -> none  [the longest x2 15.2 us: shards(): jnp.stack([real_sum.reshape(mode_count, order_share, channel_share), imag...]
    ppermute x2, waiting for transfers between devices: 0.27 us -> 22.5 us  [padded_2(): before = lax.ppermute(last, axis, up)]
    while x240 -> x0, other arithmetic: 21.3 us -> none
    all_to_all x3 -> x2, waiting for transfers between devices: 20.8 us -> 0.01 us  [the longest x1 0.01 us: chip_shards(): lax.all_to_all(packed, over_chips, split_axis=0, concat_axis=0, tiled=True)]
  transfers between devices with their start and end apart: 8 -> 11, of which waited for: 6 -> 2; matrix products, arithmetic and copies ran while one was open for 12% -> 40% of each run, Pallas kernels for 0% -> 9%
where the time goes in v1:
time: 105 us; the launch traced here: 104 us
  other arithmetic  26 us (25%)
  starting transfers between devices  24.4 us (23%)
  waiting for transfers between devices  22.6 us (22%)
  local copies, waits for them, and re-layouts  17.9 us (17%)
  Pallas kernels  12.5 us (12%)
    ppermute x2, waiting for transfers between devices, padded_2(): before = lax.ppermute(last, axis, up)  22.5 us
    convert_element_type x1, other arithmetic, chip_shards(): (grid_state.astype(jnp.float32) + jax.nn.gelu(filtered)).astype(jnp.bfloa...  12 us
    pallas_call x1, Pallas kernels, chip_shards(): pl.pallas_call(functools.partial(spectral_body, lat_count, columns, share...  7.98 us
    all_to_all x1, starting transfers between devices, chip_shards(): lax.all_to_all(packed, over_chips, split_axis=0, concat_axis=0, tiled=True)  7.87 us
    all_to_all x1, starting transfers between devices, chip_shards(): lax.all_to_all(bands.reshape(chips, share, 2 * M), over_chips, split_axis...  6.58 us
    select_n x2, other arithmetic, chip_shards(): jnp.where(column == 0, jnp.stack([spectral_weight, across]), jnp.stack([a...  4.27 us
    unnamed x33, local copies, waits for them, and re-layouts  4.21 us
    ppermute x2, starting transfers between devices, padded_2(): before = lax.ppermute(last, axis, up)  4.2 us
  transfers between devices with their start and end apart: 11, of which 2 were waited for; matrix products, arithmetic and copies ran while one was open for 40% of the time, Pallas kernels for 9%

profile of v1, /device:TPU:0, one launch (start us, length us, event | category | flops | bytes accessed | tf_op | source)
XLA Modules:
  0.0 103.7 jit_solution(12835430953785639404)
XLA Ops:
  0.0 0.9 dynamic-slice_bitcast_fusion.3
  1.0 0.5 collective-permute-start.1
  1.4 1.1 %copy.17.grid_ref = bf16[2,180,640]{2,1,0:T(8,128)(2,1)S(1)} copy(bf16[2,180,640]{2,0,1:T(2,128)(2,1)} %param.10) | data formatting | bytes 921600 | tf_op args[0]
  2.5 1.1 %pack.1 = bf16[16,120,128]{2,1,0:T(8,128)(2,1)} custom-call(bf16[2,180,640]{2,1,0:T(8,128)(2,1)S(1)} %copy.17.grid_ref), custom_call_target="tpu_custom_call" | custom-call | tf_op jit(solution)/shard_map/pack/pallas_call | solution.py:465
  3.6 7.9 %all-to-all-start = ((bf16[16,120,128]{2,1,0:T(8,128)(2,1)}), bf16[16,120,128]{2,1,0:T(8,128)(2,1)S(1)}, u32[]{:S(2)}, u32[]{:S(2)}) async-start(bf16[16,120,128]{2,1,0:T(8,128)(2,1)} %pack.1), calls=%async_computation | async-start | bytes 983040 | tf_op jit(solution)/shard_map/all_to_all | solution.py:474
  11.5 2.0 %collective-permute-start.3 = (bf16[2,640,160]{1,2,0:T(8,128)(2,1)}, bf16[2,640,160]{1,2,0:T(8,128)(2,1)}, u32[]{:S(2)}, u32[]{:S(2)}) collective-permute-start(bf16[2,640,160]{1,2,0:T(8,128)(2,1)} %param.13), channel_id=1, source_target_pairs={{0,2},{2,0},{1,3},{3,1},{4,6},{6,4},{5,7},{7,5},{8,10},{10,8},{9,1... | collective-permute-start | bytes 1228808 | tf_op jit(solution)/shard_map/ppermute | solution.py:492
  13.4 0.0 copy-done.2
  13.4 0.6 fusion.19
  14.0 0.0 collective-permute-start.5
  14.0 1.7 %collective-permute-start.6 = (bf16[2,1,640]{2,0,1:T(2,128)(2,1)}, bf16[2,1,640]{2,0,1:T(2,128)(2,1)}, u32[]{:S(2)}, u32[]{:S(2)}) collective-permute-start(bf16[2,1,640]{2,0,1:T(2,128)(2,1)} %get-tuple-element.20), channel_id=1, source_target_pairs={{1,0},{2,1},{3,2},{0,3},{5,4},{6,5},{7,6},{4,7},{9,8},{10,9},{11,1... | collective-permute-start | bytes 7688 | tf_op jit(solution)/shard_map/ppermute | solution.py:30
  15.8 0.0 copy-done.3
  15.8 0.7 slice_reduce_fusion.8
  16.5 1.1 %dynamic-slice_bitcast_fusion.table_ref = bf16[4,256,256]{2,1,0:T(8,128)(2,1)S(1)} fusion(bf16[2,4,256,256]{3,2,1,0:T(8,128)(2,1)} %constant.92.clone, s32[]{:T(128)S(6)} %select_n.103), kind=kLoop, calls=%fused_computation.36 | loop fusion | bytes 1048580 | tf_op jit(solution)/shard_map/jit(dynamic_index_in_dim)/squeeze | solution.py:529
  17.5 1.1 %dynamic-slice_bitcast_fusion.1.legendre_ref = bf16[8,256,128]{2,1,0:T(8,128)(2,1)S(1)} fusion(bf16[2,8,256,128]{3,2,1,0:T(8,128)(2,1)} %constant.91.clone, s32[]{:T(128)S(6)} %select_n.103), kind=kLoop, calls=%fused_computation.37 | loop fusion | bytes 1048580 | tf_op jit(solution)/shard_map/jit(dynamic_index_in_dim)/squeeze | solution.py:526
  18.6 0.1 constant_dynamic-slice_fusion
  18.7 1.0 dynamic-slice_bitcast_fusion.2.table_ref
  19.7 0.6 fusion.17
  20.3 1.2 %copy.18 = bf16[2,640,160]{2,1,0:T(8,128)(2,1)S(1)} copy(bf16[2,640,160]{1,2,0:T(8,128)(2,1)} %param.13) | data formatting | bytes 819200 | tf_op args[3]
  21.6 0.0 copy-done.13
  21.6 6.2 %collective-permute-done.5 = bf16[2,1,640]{2,0,1:T(2,128)(2,1)} collective-permute-done((bf16[2,1,640]{2,0,1:T(2,128)(2,1)S(1)}, bf16[2,1,640]{2,0,1:T(2,128)(2,1)}, u32[]{:S(2)}, u32[]{:S(2)}) %collective-permute-start.5) | collective-permute-done | bytes 2592 | tf_op jit(solution)/shard_map/ppermute | solution.py:29
  27.9 0.7 constant_dynamic-update-slice_fusion.2
  28.5 0.4 constant_dynamic-update-slice_fusion.1
  28.9 0.0 collective-permute-done.6
  28.9 0.7 constant_dynamic-update-slice_fusion
  29.6 1.6 %fusion.18 = (bf16[1,182,640]{2,0,1:T(2,128)(2,1)}, bf16[1,182,640]{2,0,1:T(2,128)(2,1)}) fusion(bf16[2,182,640]{2,0,1:T(2,128)(2,1)S(1)} %constant_dynamic-update-slice_fusion), kind=kLoop, calls=%fused_computation.63 | loop fusion | bytes 931840 | tf_op jit(solution)/shard_map/slice | solution.py:27
  31.2 4.2 %collective-permute-start.7 = (bf16[1,182,640]{2,0,1:T(2,128)(2,1)}, bf16[1,182,640]{2,0,1:T(2,128)(2,1)}, u32[]{:S(2)}, u32[]{:S(2)}) collective-permute-start(bf16[1,182,640]{2,0,1:T(2,128)(2,1)} %get-tuple-element.18), channel_id=1, source_target_pairs={{0,4},{4,8},{8,12},{12,16},{16,20},{20,24},{24,28},{1,5},{5,9},{9,... | collective-permute-start | bytes 698888 | tf_op jit(solution)/shard_map/ppermute | solution.py:29
  35.4 1.3 %collective-permute-start.8 = (bf16[1,182,640]{2,0,1:T(2,128)(2,1)}, bf16[1,182,640]{2,0,1:T(2,128)(2,1)}, u32[]{:S(2)}, u32[]{:S(2)}) collective-permute-start(bf16[1,182,640]{2,0,1:T(2,128)(2,1)} %get-tuple-element.19), channel_id=1, source_target_pairs={{4,0},{8,4},{12,8},{16,12},{20,16},{24,20},{28,24},{5,1},{9,5},{13... | collective-permute-start | bytes 698888 | tf_op jit(solution)/shard_map/ppermute | solution.py:30
  36.7 0.0 collective-permute-done.1
  36.7 0.9 broadcast_select_fusion
  37.6 0.0 all-to-all-done.own_ref
  37.6 0.1 collective-permute-start
  37.7 0.7 select_convert_fusion.3
  38.4 16.3 %collective-permute-done.7 = bf16[1,182,640]{2,0,1:T(2,128)(2,1)} collective-permute-done((bf16[1,182,640]{2,0,1:T(2,128)(2,1)}, bf16[1,182,640]{2,0,1:T(2,128)(2,1)}, u32[]{:S(2)}, u32[]{:S(2)}) %collective-permute-start.7) | collective-permute-done | bytes 232992 | tf_op jit(solution)/shard_map/ppermute | solution.py:29
  54.7 0.0 collective-permute-done.8
  54.7 3.9 %maximum_convert_fusion = f32[4,182,640]{2,0,1:T(4,128)} fusion(bf16[1,182,640]{2,0,1:T(2,128)(2,1)} %collective-permute-done.8, bf16[2,182,640]{2,0,1:T(2,128)(2,1)S(1)} %constant_dynamic-update-slice_fusion, bf16[1,182,640]{2,0,1:T(2,128)(2,1)} %collective-permute-done.7), kind=kLoop, calls=%fused_computation.4 | loop fusion | flops 2795520 | bytes 2795520 | tf_op jit(solution)/shard_map/convert_element_type | solution.py:479
  58.6 0.0 collective-permute-done.3
  58.6 2.5 %maximum_select_fusion.2 = bf16[2,2,640,160]{2,3,1,0:T(8,128)(2,1)} fusion(bf16[1,2,640,160]{2,3,1,0:T(8,128)(2,1)} %bitcast.12, bf16[1,2,640,160]{2,3,1,0:T(8,128)(2,1)} %bitcast.11, pred[]{:T(512)S(6)} %eq.30), kind=kLoop, calls=%fused_computation.31 | loop fusion | flops 1228800 | bytes 1638401 | tf_op jit(solution)/shard_map/jit(_where)/select_n | solution.py:493
  61.1 0.0 collective-permute-start.4
  61.1 0.0 collective-permute-done.other_ref
  61.1 0.1 broadcast_in_dim.50.tap_ref
  61.2 0.0 copy-start.4
  61.2 0.0 copy-start.5
  61.2 0.0 copy-start.6
  61.2 0.0 copy-start.7
  61.3 8.0 %spectral.1 = bf16[2,8,40,512]{3,2,1,0:T(8,128)(2,1)} custom-call(s32[1]{0:T(128)} %bitcast.parity_ref, bf16[16,120,128]{2,1,0:T(8,128)(2,1)S(1)} %all-to-all-done.own_ref, bf16[16,120,128]{2,1,0:T(8,128)(2,1)S(1)} %collective-permute-done.other_ref, bf16[160,256]{1,0:T(8,128)(2,1)S(1)} %pad_maximum_fusion.1.gain_ref, ...), custom_call_target="tpu_custom_call" | custom-call | tf_op jit(solution)/shard_map/spectral/pallas_call | solution.py:537
  69.3 6.6 %all-to-all-start.1 = ((bf16[16,40,512]{2,1,0:T(8,128)(2,1)}), bf16[16,40,512]{2,1,0:T(8,128)(2,1)S(1)}, u32[]{:S(2)}, u32[]{:S(2)}) async-start(bf16[16,40,512]{2,1,0:T(8,128)(2,1)} %bitcast.6), calls=%async_computation.1 | async-start | bytes 1310720 | tf_op jit(solution)/shard_map/all_to_all | solution.py:550
  75.9 12.0 %fusion.16 = bf16[2,180,640]{2,0,1:T(2,128)(2,1)S(1)} fusion(f32[4,182,640]{2,0,1:T(4,128)} %maximum_convert_fusion, bf16[2,180,640]{2,0,1:T(2,128)(2,1)S(1)} %copy-done.2, f32[640]{0:T(1024)S(1)} %copy-done.11, f32[640]{0:T(1024)S(1)} %copy-done.12, f32[640]{0:T(1024)S(1)} %copy-done.5, f32[640]{0:T(1024)S(1)} %copy-done.6, f32[640]{0:T(1024)S(1)} %copy-done.7, ...), kind=kLoop, calls=%fused_computation.30 | loop fusion | flops 6451200 | bytes 9239040 | tf_op jit(solution)/shard_map/convert_element_type | solution.py:488
  88.0 0.1 copy.23
  88.1 2.1 %copy.19 = bf16[2,640,160]{2,1,0:T(8,128)(2,1)} copy(bf16[2,640,160]{1,2,0:T(8,128)(2,1)} %collective-permute-done.3) | data formatting | bytes 819200 | tf_op jit(solution)/shard_map/ppermute | solution.py:492
  90.2 1.8 %maximum_select_fusion.1 = bf16[2,1,2,640,160]{4,3,2,1,0:T(8,128)(2,1)S(1)} fusion(bf16[1,1,2,640,160]{4,3,2,1,0:T(8,128)(2,1)} %bitcast.44, bf16[1,1,2,640,160]{4,3,2,1,0:T(8,128)(2,1)S(1)} %bitcast.43, pred[]{:T(512)S(6)} %eq.30), kind=kLoop, calls=%fused_computation.3 | loop fusion | flops 1228800 | bytes 1638401 | tf_op jit(solution)/shard_map/jit(_where)/select_n | solution.py:493
  92.0 0.0 collective-permute-done.4
  92.0 2.3 %copy.20 = bf16[2,2,640,160]{3,2,1,0:T(8,128)(2,1)} copy(bf16[2,2,640,160]{2,3,1,0:T(8,128)(2,1)} %collective-permute-done.4) | data formatting | bytes 1638400 | tf_op jit(solution)/shard_map/ppermute | solution.py:496
  94.3 0.0 all-to-all-done.1
  94.3 0.2 collective-permute-start.2
  94.5 2.5 %maximum_select_fusion = bf16[2,2,2,640,160]{4,3,2,1,0:T(8,128)(2,1)S(1)} fusion(bf16[2,1,2,640,160]{4,3,2,1,0:T(8,128)(2,1)} %bitcast.42, bf16[2,1,2,640,160]{4,3,2,1,0:T(8,128)(2,1)S(1)} %maximum_select_fusion.1, pred[]{:T(512)S(6)} %eq.29), kind=kLoop, calls=%fused_computation | loop fusion | flops 2457600 | bytes 3276801 | tf_op jit(solution)/shard_map/jit(_where)/select_n | solution.py:497
  97.0 0.2 slice_bitcast_fusion.3
  97.2 0.0 copy-start
  97.2 0.0 copy-start.1
  97.2 1.2 %pad_maximum_fusion.mix_ref = bf16[2,640,640]{2,1,0:T(8,128)(2,1)S(1)} fusion(bf16[2,640,160]{2,1,0:T(8,128)(2,1)S(1)} %get-tuple-element.15, bf16[2,640,160]{2,1,0:T(8,128)(2,1)S(1)} %get-tuple-element.16, bf16[2,640,160]{2,1,0:T(8,128)(2,1)S(1)} %get-tuple-element.17, bf16[2,640,160]{2,1,0:T(8,128)(2,1)S(1)} %get-tuple-element.14), kind=kLoop, calls=%fused_computation.1 | loop fusion | flops 6553600 | bytes 3276800 | tf_op jit(solution)/shard_map/concatenate | solution.py:502
  98.4 0.0 collective-permute-done.2.other_ref
  98.4 0.2 copy-done
  98.7 0.5 copy-done.1
  99.1 3.5 %finish.1 = bf16[2,180,640]{2,1,0:T(8,128)(2,1)S(1)} custom-call(bf16[640,512]{1,0:T(8,128)(2,1)S(1)} %bitcast.40, bf16[640,512]{1,0:T(8,128)(2,1)S(1)} %collective-permute-done.2.other_ref, bf16[2,368,256]{2,1,0:T(8,128)(2,1)S(1)} %dynamic-slice_bitcast_fusion.2.table_ref, bf16[2,640,640]{2,1,0:T(8,128)(2,1)S(1)} %pad_maximum_fusion.mix_ref, ...), custom_call_target="tpu_custom_call" | custom-call | tf_op jit(solution)/shard_map/finish/pallas_call | solution.py:555
  102.6 1.1 %copy.22 = bf16[2,180,640]{2,0,1:T(2,128)(2,1)} copy(bf16[2,180,640]{2,1,0:T(8,128)(2,1)S(1)} %finish.1) | data formatting | bytes 921600 | tf_op jit(solution)/shard_map/finish/pallas_call | solution.py:555
  (21 shorter events, 0.1 us)
Async XLA Ops:
  0.0 13.4 %copy-start.2 = (bf16[2,180,640]{2,0,1:T(2,128)(2,1)S(1)}, bf16[2,180,640]{2,0,1:T(2,128)(2,1)}, u32[]{:S(2)}) copy-start(bf16[2,180,640]{2,0,1:T(2,128)(2,1)} %param.10) | copy-start | bytes 1382404
  0.0 15.8 %copy-start.3 = (f32[3,3,640]{2,1,0:T(4,128)S(1)}, f32[3,3,640]{2,1,0:T(4,128)}, u32[]{:S(2)}) copy-start(f32[3,3,640]{2,1,0:T(4,128)} %param.11) | copy-start | bytes 69124
  1.0 35.8 %collective-permute-start.1 = (bf16[2,40,256]{2,1,0:T(8,128)(2,1)S(1)}, bf16[2,40,256]{2,1,0:T(8,128)(2,1)}, u32[]{:S(2)}, u32[]{:S(2)}) collective-permute-start(bf16[2,40,256]{2,1,0:T(8,128)(2,1)S(1)} %dynamic-slice_bitcast_fusion.3), channel_id=1, source_target_pairs={{0,1},{1,0},{2,3},{3,2},{4,5},{5,4},{6,7},{7,6},{8,9},{9,8},{10,11... | collective-permute-start | bytes 122888 | tf_op jit(solution)/shard_map/ppermute | solution.py:510
  3.6 34.0 %all-to-all-start = ((bf16[16,120,128]{2,1,0:T(8,128)(2,1)}), bf16[16,120,128]{2,1,0:T(8,128)(2,1)S(1)}, u32[]{:S(2)}, u32[]{:S(2)}) async-start(bf16[16,120,128]{2,1,0:T(8,128)(2,1)} %pack.1), calls=%async_computation | async-start | bytes 983040 | tf_op jit(solution)/shard_map/all_to_all | solution.py:474
  11.5 47.1 %collective-permute-start.3 = (bf16[2,640,160]{1,2,0:T(8,128)(2,1)}, bf16[2,640,160]{1,2,0:T(8,128)(2,1)}, u32[]{:S(2)}, u32[]{:S(2)}) collective-permute-start(bf16[2,640,160]{1,2,0:T(8,128)(2,1)} %param.13), channel_id=1, source_target_pairs={{0,2},{2,0},{1,3},{3,1},{4,6},{6,4},{5,7},{7,5},{8,10},{10,8},{9,1... | collective-permute-start | bytes 1228808 | tf_op jit(solution)/shard_map/ppermute | solution.py:492
  14.0 13.8 %collective-permute-start.5 = (bf16[2,1,640]{2,0,1:T(2,128)(2,1)S(1)}, bf16[2,1,640]{2,0,1:T(2,128)(2,1)}, u32[]{:S(2)}, u32[]{:S(2)}) collective-permute-start(bf16[2,1,640]{2,0,1:T(2,128)(2,1)S(1)} %get-tuple-element.21), channel_id=1, source_target_pairs={{0,1},{1,2},{2,3},{3,0},{4,5},{5,6},{6,7},{7,4},{8,9},{9,10},{10,1... | collective-permute-start | bytes 7688 | tf_op jit(solution)/shard_map/ppermute | solution.py:29
  14.0 14.9 %collective-permute-start.6 = (bf16[2,1,640]{2,0,1:T(2,128)(2,1)}, bf16[2,1,640]{2,0,1:T(2,128)(2,1)}, u32[]{:S(2)}, u32[]{:S(2)}) collective-permute-start(bf16[2,1,640]{2,0,1:T(2,128)(2,1)} %get-tuple-element.20), channel_id=1, source_target_pairs={{1,0},{2,1},{3,2},{0,3},{5,4},{6,5},{7,6},{4,7},{9,8},{10,9},{11,1... | collective-permute-start | bytes 7688 | tf_op jit(solution)/shard_map/ppermute | solution.py:30
  16.5 5.1 %copy-start.13 = (f32[640]{0:T(1024)S(1)}, f32[640]{0:T(1024)}, u32[]{:S(2)}) copy-start(f32[640]{0:T(1024)} %param.14) | copy-start | bytes 7684
  31.2 23.5 %collective-permute-start.7 = (bf16[1,182,640]{2,0,1:T(2,128)(2,1)}, bf16[1,182,640]{2,0,1:T(2,128)(2,1)}, u32[]{:S(2)}, u32[]{:S(2)}) collective-permute-start(bf16[1,182,640]{2,0,1:T(2,128)(2,1)} %get-tuple-element.18), channel_id=1, source_target_pairs={{0,4},{4,8},{8,12},{12,16},{16,20},{20,24},{24,28},{1,5},{5,9},{9,... | collective-permute-start | bytes 698888 | tf_op jit(solution)/shard_map/ppermute | solution.py:29
  35.4 19.3 %collective-permute-start.8 = (bf16[1,182,640]{2,0,1:T(2,128)(2,1)}, bf16[1,182,640]{2,0,1:T(2,128)(2,1)}, u32[]{:S(2)}, u32[]{:S(2)}) collective-permute-start(bf16[1,182,640]{2,0,1:T(2,128)(2,1)} %get-tuple-element.19), channel_id=1, source_target_pairs={{4,0},{8,4},{12,8},{16,12},{20,16},{24,20},{28,24},{5,1},{9,5},{13... | collective-permute-start | bytes 698888 | tf_op jit(solution)/shard_map/ppermute | solution.py:30
  37.6 23.4 %collective-permute-start = (bf16[16,120,128]{2,1,0:T(8,128)(2,1)S(1)}, bf16[16,120,128]{2,1,0:T(8,128)(2,1)S(1)}, u32[]{:S(2)}, u32[]{:S(2)}) collective-permute-start(bf16[16,120,128]{2,1,0:T(8,128)(2,1)S(1)} %all-to-all-done.own_ref), channel_id=1, source_target_pairs={{0,1},{1,0},{2,3},{3,2},{4,5},{5,4},{6,7},{7,6},{8,9},{9,8},{10,11... | collective-permute-start | bytes 1474568 | tf_op jit(solution)/shard_map/ppermute | solution.py:475
  61.1 30.9 %collective-permute-start.4 = (bf16[2,2,640,160]{2,3,1,0:T(8,128)(2,1)}, bf16[2,2,640,160]{2,3,1,0:T(8,128)(2,1)}, u32[]{:S(2)}, u32[]{:S(2)}) collective-permute-start(bf16[2,2,640,160]{2,3,1,0:T(8,128)(2,1)} %maximum_select_fusion.2), channel_id=1, source_target_pairs={{0,1},{1,0},{2,3},{3,2},{4,5},{5,4},{6,7},{7,6},{8,9},{9,8},{10,11... | collective-permute-start | bytes 2457608 | tf_op jit(solution)/shard_map/ppermute | solution.py:496
  61.2 14.7 %copy-start.4 = (f32[640]{0:T(1024)S(1)}, f32[640]{0:T(1024)}, u32[]{:S(2)}) copy-start(f32[640]{0:T(1024)} %get-tuple-element.5) | copy-start | bytes 7684
  61.2 14.7 %copy-start.5 = (f32[640]{0:T(1024)S(1)}, f32[640]{0:T(1024)}, u32[]{:S(2)}) copy-start(f32[640]{0:T(1024)} %get-tuple-element.6) | copy-start | bytes 7684
  61.2 14.7 %copy-start.6 = (f32[640]{0:T(1024)S(1)}, f32[640]{0:T(1024)}, u32[]{:S(2)}) copy-start(f32[640]{0:T(1024)} %get-tuple-element.7) | copy-start | bytes 7684
  61.2 14.7 %copy-start.7 = (f32[640]{0:T(1024)S(1)}, f32[640]{0:T(1024)}, u32[]{:S(2)}) copy-start(f32[640]{0:T(1024)} %get-tuple-element.8) | copy-start | bytes 7684
  61.2 14.7 %copy-start.8 = (f32[640]{0:T(1024)S(1)}, f32[640]{0:T(1024)}, u32[]{:S(2)}) copy-start(f32[640]{0:T(1024)} %get-tuple-element.9) | copy-start | bytes 7684
  61.2 14.7 %copy-start.9 = (f32[640]{0:T(1024)S(1)}, f32[640]{0:T(1024)}, u32[]{:S(2)}) copy-start(f32[640]{0:T(1024)} %get-tuple-element.10) | copy-start | bytes 7684
  61.2 14.7 %copy-start.10 = (f32[640]{0:T(1024)S(1)}, f32[640]{0:T(1024)}, u32[]{:S(2)}) copy-start(f32[640]{0:T(1024)} %get-tuple-element.11) | copy-start | bytes 7684
  61.3 14.7 %copy-start.11 = (f32[640]{0:T(1024)S(1)}, f32[640]{0:T(1024)}, u32[]{:S(2)}) copy-start(f32[640]{0:T(1024)} %get-tuple-element.12) | copy-start | bytes 7684
  61.3 14.7 %copy-start.12 = (f32[640]{0:T(1024)S(1)}, f32[640]{0:T(1024)}, u32[]{:S(2)}) copy-start(f32[640]{0:T(1024)} %get-tuple-element.13) | copy-start | bytes 7684
  69.3 25.1 %all-to-all-start.1 = ((bf16[16,40,512]{2,1,0:T(8,128)(2,1)}), bf16[16,40,512]{2,1,0:T(8,128)(2,1)S(1)}, u32[]{:S(2)}, u32[]{:S(2)}) async-start(bf16[16,40,512]{2,1,0:T(8,128)(2,1)} %bitcast.6), calls=%async_computation.1 | async-start | bytes 1310720 | tf_op jit(solution)/shard_map/all_to_all | solution.py:550
  94.3 4.1 %collective-permute-start.2 = (bf16[640,512]{1,0:T(8,128)(2,1)S(1)}, bf16[640,512]{1,0:T(8,128)(2,1)S(1)}, u32[]{:S(2)}, u32[]{:S(2)}) collective-permute-start(bf16[640,512]{1,0:T(8,128)(2,1)S(1)} %bitcast.39), channel_id=1, source_target_pairs={{0,1},{1,0},{2,3},{3,2},{4,5},{5,4},{6,7},{7,6},{8,9},{9,8},{10,11... | collective-permute-start | bytes 1966088 | tf_op jit(solution)/shard_map/ppermute | solution.py:553
  97.2 1.4 %copy-start = (bf16[640,1280]{1,0:T(8,128)(2,1)S(1)}, bf16[640,1280]{1,0:T(8,128)(2,1)}, u32[]{:S(2)}) copy-start(bf16[640,1280]{1,0:T(8,128)(2,1)} %expand_ref.1) | copy-start | bytes 4915204
  97.2 1.9 %copy-start.1 = (bf16[1280,640]{1,0:T(8,128)(2,1)S(1)}, bf16[1280,640]{1,0:T(8,128)(2,1)}, u32[]{:S(2)}) copy-start(bf16[1280,640]{1,0:T(8,128)(2,1)} %reduce_ref.1) | copy-start | bytes 4915204

commit v2 on v1

--- a/solution.py
+++ b/solution.py
@@ -203,6 +203,9 @@
     return block_output.reshape(lat_rows, sector_width, channel_total)
 
 
+contract_last = (((1,), (1,)), ((), ()))
+
+
 def legendre_constant(lat_total, mode_count):
     colatitude = (np.arange(lat_total // 2) + 0.5) * (math.pi / lat_total)
     cosines, sines = np.cos(colatitude)[:, None], np.sin(colatitude)[:, None]
@@ -293,8 +296,8 @@
 
 def spectral_body(
     lat_count, columns, share, width,
-    parity_ref, own_ref, other_ref, gain_ref, tap_ref, legendre_ref, table_ref, out_ref,
-    field_ref, first_ref, modes_ref,
+    parity_ref, own_ref, other_any, gain_ref, tap_ref, legendre_ref, table_ref, out_ref,
+    field_ref, first_ref, modes_ref, other_ref, sem,
 ):
     lat_total = 2 * lat_count
     north = lat_total // 2
@@ -302,7 +305,11 @@
     edge = width - LANES
     orders = legendre_ref.shape[2]
     parity = parity_ref[0]
+    arrival = pltpu.make_async_copy(other_any, other_ref, sem)
+    arrival.start()
     for source, core in ((own_ref, parity), (other_ref, 1 - parity)):
+        if source is other_ref:
+            arrival.wait()
         for column in range(columns):
             sector = 2 * column + core
             for band in range(lat_count):
@@ -409,27 +416,51 @@
                     out_ref[column, place // 2, :, at : at + orders] = value
 
 
+def stage_body(
+    place_ref, own_ref, table_ref,
+    mix_a_ref, mix_b_ref, mix_c_ref, mix_d_ref,
+    field_ref, mix_ref, sems,
+):
+    place = place_ref[0]
+    held = mix_a_ref.shape[1]
+    loads = []
+    for k, source in enumerate((mix_a_ref, mix_b_ref, mix_c_ref, mix_d_ref)):
+        sector = 2 * (place // 2 if k < 2 else 1 - place // 2) + (
+            place % 2 if k % 2 == 0 else 1 - place % 2
+        )
+        rows = pl.ds(pl.multiple_of(sector * held, held), held)
+        loads.append(pltpu.make_async_copy(source, mix_ref.at[:, rows, :], sems.at[k]))
+    for load in loads:
+        load.start()
+    modes = table_ref.shape[2]
+    for row in range(2):
+        field_ref[row] = lax.dot_general(
+            table_ref[0], own_ref[:, row * modes : (row + 1) * modes], contract_last,
+            preferred_element_type=jnp.float32,
+        )
+    for load in loads:
+        load.wait()
+
+
 def finish_body(
     width, padded,
-    own_ref, other_ref, table_ref, mix_ref, first_ref, gain_ref, expand_ref, reduce_ref, out_ref,
+    field_ref, other_ref, first_ref, gain_ref, table_ref, mix_ref, expand_ref, reduce_ref,
+    marker_ref, out_ref,
 ):
-    contract_last = (((1,), (1,)), ((), ()))
     modes = table_ref.shape[2]
     real, imag = [], []
     for row in range(2):
-        at = slice(row * modes, (row + 1) * modes)
-        field = lax.dot_general(
-            table_ref[0], own_ref[:, at], contract_last, preferred_element_type=jnp.float32
-        ) + lax.dot_general(
-            table_ref[1], other_ref[:, at], contract_last, preferred_element_type=jnp.float32
+        field = field_ref[row] + lax.dot_general(
+            table_ref[1], other_ref[:, row * modes : (row + 1) * modes], contract_last,
+            preferred_element_type=jnp.float32,
         )
         real.append(field[:padded])
         imag.append(field[padded:])
     real = jnp.concatenate(real, axis=0).astype(jnp.bfloat16)
     imag = jnp.concatenate(imag, axis=0).astype(jnp.bfloat16)
-    spectral_out = jnp.dot(real, mix_ref[0], preferred_element_type=jnp.float32) - jnp.dot(
-        imag, mix_ref[1], preferred_element_type=jnp.float32
-    )
+    spectral_out = lax.dot_general(
+        real, mix_ref[0], contract_last, preferred_element_type=jnp.float32
+    ) - lax.dot_general(imag, mix_ref[1], contract_last, preferred_element_type=jnp.float32)
     second = (first_ref[...].astype(jnp.float32) + spectral_out).astype(jnp.bfloat16)
     wide = second.astype(jnp.float32)
     scale = lax.rsqrt(jnp.mean(wide * wide, axis=-1, keepdims=True) + norm_eps)
@@ -441,6 +472,46 @@
     result = wide + update
     for row in range(2):
         out_ref[row] = result[row * padded : row * padded + width].astype(jnp.bfloat16)
+
+
+def local_body(
+    width, padded, above_ref, grid_ref, below_ref, west_ref, east_ref, tap_ref,
+    out_ref, marker_ref, tall_ref,
+):
+    marker_ref[...] = jnp.zeros_like(marker_ref)
+    west, east = west_ref[...].astype(jnp.float32), east_ref[...].astype(jnp.float32)
+    for k, row in enumerate((above_ref[...], grid_ref[0], grid_ref[1], below_ref[...])):
+        tall_ref[k, 8 + width // 8 * 8 :, :] = jnp.zeros(
+            (padded + 8 - width // 8 * 8, row.shape[1]), jnp.float32
+        )
+        tall_ref[k, 8 : 8 + width, :] = row.astype(jnp.float32)
+        tall_ref[k, 7:8, :] = west[k : k + 1]
+        tall_ref[k, 8 + width : 9 + width, :] = east[k : k + 1]
+    inside = lax.broadcasted_iota(jnp.int32, (padded, LANES), 0) < width
+    for piece in range(tall_ref.shape[2] // LANES):
+        lanes = slice(piece * LANES, (piece + 1) * LANES)
+        total = [None, None]
+        for k in range(4):
+            for col in range(3):
+                value = tall_ref[k, 7 + col : 7 + col + padded, lanes]
+                for row in range(2):
+                    if 0 <= k - row < 3:
+                        tap = tap_ref[3 * (k - row) + col : 3 * (k - row) + col + 1, lanes]
+                        part = tap * value
+                        total[row] = part if total[row] is None else total[row] + part
+        for row in range(2):
+            value = tall_ref[1 + row, 8 : 8 + padded, lanes] + gelu(total[row])
+            value = jnp.where(inside, value, 0.0)
+            total[row] = value
+        out_ref[:, lanes] = jnp.concatenate(total, axis=0).astype(jnp.bfloat16)
+
+
+def own_part(constant, at):
+    return lax.dynamic_index_in_dim(jnp.asarray(constant), at, 0, keepdims=False)
+
+
+def in_hbm(count):
+    return [pl.BlockSpec(memory_space=pl.ANY)] * count
 
 
 def in_vmem(count):
@@ -468,40 +539,18 @@
         in_specs=in_vmem(1),
         out_specs=in_vmem(1)[0],
         scratch_shapes=[pltpu.VMEM((2, span, channels), jnp.float32)],
-        compiler_params=pltpu.CompilerParams(vmem_limit_bytes=24 << 20),
+        compiler_params=pltpu.CompilerParams(vmem_limit_bytes=16 << 20),
         name="pack",
     )(grid_state)
+    packed, later = lax.optimization_barrier(
+        (packed, (grid_state, conv_weight, spectral_gain, spectral_weight))
+    )
+    grid_state, conv_weight, spectral_gain, spectral_weight = later
     own = lax.all_to_all(packed, over_chips, split_axis=0, concat_axis=0, tiled=True)
-    other = lax.ppermute(own, "core", swap)
-
-    lons = ("x", "core")
-    wrapped = padded_2(grid_state, ((lons, 1),), 1, True)
-    halo = padded_2(wrapped, (("lat", 0),), 1, False).astype(jnp.float32)
-    filtered = jnp.zeros(grid_state.shape, jnp.float32)
-    for row_shift in range(3):
-        for col_shift in range(3):
-            filtered = (
-                filtered
-                + conv_weight[row_shift, col_shift]
-                * halo[row_shift : row_shift + lat_rows, col_shift : col_shift + width]
-            )
-    first_section = (grid_state.astype(jnp.float32) + jax.nn.gelu(filtered)).astype(jnp.bfloat16)
-    first_rows = jnp.pad(first_section, ((0, 0), (0, padded - width), (0, 0))).reshape(-1, channels)
-
-    held = spectral_weight.shape[2]
-    across = lax.ppermute(spectral_weight, "x", [(i, (i + 1) % columns) for i in range(columns)])
-    pair = jnp.where(
-        column == 0, jnp.stack([spectral_weight, across]), jnp.stack([across, spectral_weight])
-    )
-    pair_other = lax.ppermute(pair, "core", swap)
-    quad = jnp.where(
-        core == 0,
-        jnp.stack([pair, pair_other], axis=1),
-        jnp.stack([pair_other, pair], axis=1),
-    )
-    mixing = jnp.concatenate(
-        [quad[i, j] for i in range(columns) for j in range(2)], axis=2
-    )
+
+    own_mix = spectral_weight.transpose(0, 2, 1)
+    across_mix = lax.ppermute(own_mix, "x", [(i, 1 - i) for i in range(columns)])
+    held = own_mix.shape[1]
 
     blocks = held // share
     piece = lax.dynamic_slice_in_dim(
@@ -523,45 +572,90 @@
     taps = lax.dynamic_slice_in_dim(conv_weight.reshape(9, channels), chip * share, share, axis=1)
     taps = jnp.broadcast_to(taps[:, :, None], (9, share, LANES))
 
-    legendre = lax.dynamic_index_in_dim(
-        jnp.asarray(parity_tables(lat_total, M)), core, 0, keepdims=False
-    )
-    analysis = lax.dynamic_index_in_dim(
-        jnp.asarray(analysis_constant(sectors, width, span, M)), core, 0, keepdims=False
-    )
-    synthesis = lax.dynamic_index_in_dim(
-        jnp.asarray(synthesis_constant(sectors, width, padded, M)),
-        2 * column + core, 0, keepdims=False,
-    )
+    legendre = own_part(parity_tables(lat_total, M), core)
+    analysis = own_part(analysis_constant(sectors, width, span, M), core)
+    table = own_part(synthesis_constant(sectors, width, padded, M), 2 * column + core)
+
+    own, grid_late, across_mix = lax.optimization_barrier((own, grid_state, across_mix))
+    other = lax.ppermute(own, "core", swap)
+    above = lax.ppermute(grid_late[1], "lat", [(i, i + 1) for i in range(lat_count - 1)])
+    below = lax.ppermute(grid_late[0], "lat", [(i + 1, i) for i in range(lat_count - 1)])
 
     bands = pl.pallas_call(
         functools.partial(spectral_body, lat_count, columns, share, width),
         out_shape=jax.ShapeDtypeStruct((columns, lat_count, share, 2 * M), jnp.bfloat16),
-        in_specs=[pl.BlockSpec(memory_space=pltpu.SMEM)] + in_vmem(6),
+        in_specs=[pl.BlockSpec(memory_space=pltpu.SMEM)]
+        + in_vmem(1) + in_hbm(1) + in_vmem(4),
         out_specs=in_vmem(1)[0],
         scratch_shapes=[
             pltpu.VMEM((sectors, lat_total, share, span), jnp.float32),
             pltpu.VMEM((sectors, lat_total * share, span), jnp.float32),
             pltpu.VMEM((lat_total * share, M), jnp.float32),
+            pltpu.VMEM(own.shape, jnp.bfloat16),
+            pltpu.SemaphoreType.DMA,
         ],
-        compiler_params=pltpu.CompilerParams(vmem_limit_bytes=40 << 20),
+        cost_estimate=pl.CostEstimate(flops=9 * 10**9, bytes_accessed=0, transcendentals=0),
+        compiler_params=pltpu.CompilerParams(vmem_limit_bytes=20 << 20),
         name="spectral",
     )(core[None], own, other, gain_rows, taps, legendre, analysis)
+    bands, above, below, across_mix = lax.optimization_barrier((bands, above, below, across_mix))
+    beside_mix = lax.ppermute(own_mix, "core", swap)
+    far_mix = lax.ppermute(across_mix, "core", swap)
+    ring = [(i, (i + 1) % sectors) for i in range(sectors)]
+    tall = (above, grid_state[0], grid_state[1], below)
+    west = lax.ppermute(
+        jnp.stack([row[width - 1] for row in tall]), ("x", "core"), ring
+    )
+    east = lax.ppermute(
+        jnp.stack([row[0] for row in tall]), ("x", "core"), [(j, i) for i, j in ring]
+    )
+    first_rows, marker = pl.pallas_call(
+        functools.partial(local_body, width, padded),
+        out_shape=[
+            jax.ShapeDtypeStruct((2 * padded, channels), jnp.bfloat16),
+            jax.ShapeDtypeStruct((8, LANES), jnp.float32),
+        ],
+        in_specs=in_vmem(6),
+        out_specs=in_vmem(2),
+        scratch_shapes=[pltpu.VMEM((4, padded + 16, channels), jnp.float32)],
+        cost_estimate=pl.CostEstimate(flops=8 * 10**9, bytes_accessed=0, transcendentals=0),
+        compiler_params=pltpu.CompilerParams(vmem_limit_bytes=16 << 20),
+        name="local",
+    )(above, grid_state, below, west, east, conv_weight.reshape(9, channels))
     back = lax.all_to_all(
         bands.reshape(chips, share, 2 * M), over_chips, split_axis=0, concat_axis=0, tiled=True
     ).reshape(channels, 2 * M)
+    back, marker, table = lax.optimization_barrier((back, marker, table))
     back_other = lax.ppermute(back, "core", swap)
+
+    field, mixing = pl.pallas_call(
+        stage_body,
+        out_shape=[
+            jax.ShapeDtypeStruct((2, 2 * padded, channels), jnp.float32),
+            jax.ShapeDtypeStruct((2, channels, channels), jnp.bfloat16),
+        ],
+        in_specs=[pl.BlockSpec(memory_space=pltpu.SMEM)] + in_vmem(2) + in_hbm(4),
+        out_specs=in_vmem(2),
+        scratch_shapes=[pltpu.SemaphoreType.DMA((4,))],
+        cost_estimate=pl.CostEstimate(flops=12 * 10**9, bytes_accessed=0, transcendentals=0),
+        compiler_params=pltpu.CompilerParams(vmem_limit_bytes=16 << 20),
+        name="stage",
+    )(
+        (2 * column + core)[None], back, table,
+        own_mix, beside_mix, across_mix, far_mix,
+    )
 
     return pl.pallas_call(
         functools.partial(finish_body, width, padded),
         out_shape=jax.ShapeDtypeStruct(grid_state.shape, jnp.bfloat16),
-        in_specs=in_vmem(8),
+        in_specs=in_vmem(9),
         out_specs=in_vmem(1)[0],
-        compiler_params=pltpu.CompilerParams(vmem_limit_bytes=40 << 20),
+        cost_estimate=pl.CostEstimate(flops=3 * 10**9, bytes_accessed=0, transcendentals=0),
+        compiler_params=pltpu.CompilerParams(vmem_limit_bytes=16 << 20),
         name="finish",
     )(
-        back, back_other, synthesis, mixing, first_rows, norm_gain[None, :],
-        expand_weight, reduce_weight,
+        field, back_other, first_rows, norm_gain[None, :], table, mixing, expand_weight,
+        reduce_weight, marker,
     )
 
 

time: 105 us -> 71.8 us (0.68)
  other arithmetic: 26 us -> 0.98 us
  local copies, waits for them, and re-layouts: 17.9 us -> 7.58 us
  waiting for transfers between devices: 22.6 us -> 25.6 us
  starting transfers between devices: 24.4 us -> 21.6 us
  Pallas kernels: 12.5 us -> 15.2 us
    ppermute x6 -> x7, waiting for transfers between devices: 22.6 us -> 1.68 us  [the longest x1 0.85 us: chip_shards(): lax.ppermute(grid_late[1], 'lat', [(i, i + 1) for i in range(lat_count -...]
    convert_element_type x2 -> x0, other arithmetic: 15.9 us -> none  [the longest x1 12 us: chip_shards(): (grid_state.astype(jnp.float32) + jax.nn.gelu(filtered)).astype(jnp.bfloa...]
    all_to_all x1, waiting for transfers between devices: 0.01 us -> 11.5 us  [chip_shards(): lax.all_to_all(packed, over_chips, split_axis=0, concat_axis=0, tiled=True)]
    all_to_all x1, waiting for transfers between devices: 0.01 us -> 11.4 us  [chip_shards(): lax.all_to_all(bands.reshape(chips, share, 2 * M), over_chips, split_axis...]
    select_n x3 -> x0, other arithmetic: 6.77 us -> none  [the longest x2 4.27 us: chip_shards(): jnp.where(column == 0, jnp.stack([spectral_weight, across]), jnp.stack([a...]
    ppermute x2 -> x0, local copies, waits for them, and re-layouts: 4.41 us -> none  [the longest x1 2.33 us: chip_shards(): pair_other = lax.ppermute(pair, 'core', swap)]
    slice x3 -> x2, local copies, waits for them, and re-layouts: 2.86 us -> 0.03 us  [chip_shards(): row[0]]
    pallas_call x0 -> x2, Pallas kernels: none -> 2.53 us  [the longest x1 1.53 us: chip_shards(): pl.pallas_call(functools.partial(local_body, width, padded), out_shape=[j...]
  transfers between devices with their start and end apart: 11 -> 12, of which waited for: 2 -> 6; matrix products, arithmetic and copies ran while one was open for 40% -> 8% of each run, Pallas kernels for 9% -> 15%
where the time goes in v2:
time: 71.8 us; the launch traced here: 71.3 us
  waiting for transfers between devices  25.6 us (36%)
  starting transfers between devices  21.6 us (30%)
  Pallas kernels  15.2 us (21%)
  local copies, waits for them, and re-layouts  7.58 us (11%)
  other arithmetic  0.98 us (1%)
    all_to_all x1, waiting for transfers between devices, chip_shards(): lax.all_to_all(packed, over_chips, split_axis=0, concat_axis=0, tiled=True)  11.5 us
    all_to_all x1, waiting for transfers between devices, chip_shards(): lax.all_to_all(bands.reshape(chips, share, 2 * M), over_chips, split_axis...  11.4 us
    pallas_call x1, Pallas kernels, chip_shards(): pl.pallas_call(functools.partial(spectral_body, lat_count, columns, share...  8.41 us
    all_to_all x1, starting transfers between devices, chip_shards(): lax.all_to_all(bands.reshape(chips, share, 2 * M), over_chips, split_axis...  6.21 us
    all_to_all x1, starting transfers between devices, chip_shards(): lax.all_to_all(packed, over_chips, split_axis=0, concat_axis=0, tiled=True)  5.94 us
    squeeze x3, local copies, waits for them, and re-layouts, own_part(): lax.dynamic_index_in_dim(jnp.asarray(constant), at, 0, keepdims=False)  3.19 us
    pallas_call x1, Pallas kernels, chip_shards(): pl.pallas_call(functools.partial(finish_body, width, padded), out_shape=j...  3.16 us
    ppermute x1, starting transfers between devices, chip_shards(): lax.ppermute(own_mix, 'x', [(i, 1 - i) for i in range(columns)])  2.94 us
  transfers between devices with their start and end apart: 12, of which 6 were waited for; matrix products, arithmetic and copies ran while one was open for 8% of the time, Pallas kernels for 15%

profile of v2, /device:TPU:0, one launch (start us, length us, event | category | flops | bytes accessed | tf_op | source)
XLA Modules:
  0.0 71.3 jit_solution(11189260315523671171)
XLA Ops:
  0.0 0.0 copy-start.7
  0.0 0.0 copy-start.2
  0.0 1.1 %copy.11.grid_ref = bf16[2,180,640]{2,1,0:T(8,128)(2,1)S(1)} copy(bf16[2,180,640]{2,0,1:T(2,128)(2,1)} %param.10) | data formatting | bytes 921600 | tf_op args[0]
  1.1 1.1 %pack.1 = bf16[16,120,128]{2,1,0:T(8,128)(2,1)} custom-call(bf16[2,180,640]{2,1,0:T(8,128)(2,1)S(1)} %copy.11.grid_ref), custom_call_target="tpu_custom_call" | custom-call | tf_op jit(solution)/shard_map/pack/pallas_call | solution.py:536
  2.3 0.0 copy-done.2
  2.3 2.9 %collective-permute-start = (bf16[2,160,640]{2,1,0:T(8,128)(2,1)S(1)}, bf16[2,160,640]{2,1,0:T(8,128)(2,1)S(1)}, u32[]{:S(2)}, u32[]{:S(2)}) collective-permute-start(bf16[2,160,640]{2,1,0:T(8,128)(2,1)S(1)} %bitcast.41), channel_id=1, source_target_pairs={{0,2},{2,0},{1,3},{3,1},{4,6},{6,4},{5,7},{7,5},{8,10},{10,8},{9,1... | collective-permute-start | bytes 1228808 | tf_op jit(solution)/shard_map/ppermute | solution.py:552
  5.2 0.0 collective-permute-start.7
  5.2 0.0 copy-start.5
  5.2 0.9 %dynamic-slice_bitcast_fusion.3 = bf16[2,40,256]{2,1,0:T(8,128)(2,1)S(1)} fusion(f32[2,256,160]{1,2,0:T(8,128)} %param.12, s32[]{:T(128)S(6)} %select_n.69), kind=kLoop, calls=%fused_computation.6 | loop fusion | bytes 81924 | tf_op jit(solution)/shard_map/transpose | solution.py:558
  6.2 0.5 collective-permute-start.2
  6.7 5.9 %all-to-all-start = ((bf16[16,120,128]{2,1,0:T(8,128)(2,1)}), bf16[16,120,128]{2,1,0:T(8,128)(2,1)S(1)}, u32[]{:S(2)}, u32[]{:S(2)}) async-start(bf16[16,120,128]{2,1,0:T(8,128)(2,1)} %pack.1), calls=%async_computation | async-start | bytes 983040 | tf_op jit(solution)/shard_map/all_to_all | solution.py:549
  12.6 0.0 copy-done.7
  12.7 1.1 %dynamic-slice_bitcast_fusion.table_ref = bf16[4,256,256]{2,1,0:T(8,128)(2,1)S(1)} fusion(bf16[2,4,256,256]{3,2,1,0:T(8,128)(2,1)} %constant.82.clone, s32[]{:T(128)S(6)} %select_n.76), kind=kLoop, calls=%fused_computation | loop fusion | bytes 1048580 | tf_op jit(solution)/shard_map/jit(dynamic_index_in_dim)/squeeze | solution.py:510
  13.7 1.1 %dynamic-slice_bitcast_fusion.1.legendre_ref = bf16[8,256,128]{2,1,0:T(8,128)(2,1)S(1)} fusion(bf16[2,8,256,128]{3,2,1,0:T(8,128)(2,1)} %constant.81.clone, s32[]{:T(128)S(6)} %select_n.76), kind=kLoop, calls=%fused_computation.1 | loop fusion | bytes 1048580 | tf_op jit(solution)/shard_map/jit(dynamic_index_in_dim)/squeeze | solution.py:510
  14.8 0.0 copy-done.5
  14.9 0.1 constant_dynamic-slice_fusion
  14.9 0.0 collective-permute-done.2
  14.9 0.9 %broadcast_select_fusion = bf16[2,40,256]{2,1,0:T(8,128)(2,1)S(1)} fusion(bf16[2,40,256]{2,1,0:T(8,128)(2,1)S(1)} %collective-permute-done.2, pred[]{:T(512)S(6)} %eq.22, f32[2,256,160]{1,2,0:T(8,128)} %param.12, s32[]{:T(128)S(6)} %select_n.69), kind=kLoop, calls=%fused_computation.13 | loop fusion | flops 20480 | bytes 122885 | tf_op jit(solution)/shard_map/jit(_where)/select_n | solution.py:560
  15.9 0.0 collective-permute-done.mix_c_ref
  15.9 11.5 %all-to-all-done.own_ref = bf16[16,120,128]{2,1,0:T(8,128)(2,1)S(1)} async-done(((bf16[16,120,128]{2,1,0:T(8,128)(2,1)}), bf16[16,120,128]{2,1,0:T(8,128)(2,1)S(1)}, u32[]{:S(2)}, u32[]{:S(2)}) %all-to-all-start) | async-done | bytes 491552 | tf_op jit(solution)/shard_map/all_to_all | solution.py:549
  27.4 0.0 collective-permute-start.1
  27.4 0.1 copy.12
  27.5 2.5 %collective-permute-start.3 = (bf16[180,640]{1,0:T(8,128)(2,1)S(1)}, bf16[180,640]{1,0:T(8,128)(2,1)S(1)}, u32[]{:S(2)}, u32[]{:S(2)}) collective-permute-start(bf16[180,640]{1,0:T(8,128)(2,1)S(1)} %get-tuple-element.44), channel_id=1, source_target_pairs={{0,4},{4,8},{8,12},{12,16},{16,20},{20,24},{24,28},{1,5},{5,9},{9,... | collective-permute-start | bytes 691208 | tf_op jit(solution)/shard_map/ppermute | solution.py:581
  30.0 1.3 %collective-permute-start.4 = (bf16[180,640]{1,0:T(8,128)(2,1)S(1)}, bf16[180,640]{1,0:T(8,128)(2,1)S(1)}, u32[]{:S(2)}, u32[]{:S(2)}) collective-permute-start(bf16[180,640]{1,0:T(8,128)(2,1)S(1)} %get-tuple-element.43), channel_id=1, source_target_pairs={{4,0},{8,4},{12,8},{16,12},{20,16},{24,20},{28,24},{5,1},{9,5},{13... | collective-permute-start | bytes 691208 | tf_op jit(solution)/shard_map/ppermute | solution.py:582
  31.3 0.0 collective-permute-done.1.other_any
  31.3 0.1 broadcast_in_dim.54.tap_ref
  31.4 8.4 %spectral.1 = bf16[2,8,40,512]{3,2,1,0:T(8,128)(2,1)} custom-call(s32[1]{0:T(128)} %bitcast.1.parity_ref, bf16[16,120,128]{2,1,0:T(8,128)(2,1)S(1)} %all-to-all-done.own_ref, bf16[16,120,128]{2,1,0:T(8,128)(2,1)S(1)} %collective-permute-done.1.other_any, bf16[160,256]{1,0:T(8,128)(2,1)S(1)} %pad_maximum_fusion.gain_ref, ...), custom_call_target="tpu_custom_call" | custom-call | flops 8999999488 | tf_op jit(solution)/shard_map/spectral/pallas_call | solution.py:584
  39.8 0.0 copy-start.6
  39.8 0.0 copy-start.8
  39.9 0.9 %collective-permute-done.3.above_ref = bf16[180,640]{1,0:T(8,128)(2,1)S(1)} collective-permute-done((bf16[180,640]{1,0:T(8,128)(2,1)S(1)}, bf16[180,640]{1,0:T(8,128)(2,1)S(1)}, u32[]{:S(2)}, u32[]{:S(2)}) %collective-permute-start.3) | collective-permute-done | bytes 230432 | tf_op jit(solution)/shard_map/ppermute | solution.py:581
  40.7 0.0 collective-permute-done.4.below_ref
  40.7 6.2 %all-to-all-start.1 = ((bf16[16,40,512]{2,1,0:T(8,128)(2,1)}), bf16[16,40,512]{2,1,0:T(8,128)(2,1)S(1)}, u32[]{:S(2)}, u32[]{:S(2)}) async-start(bf16[16,40,512]{2,1,0:T(8,128)(2,1)} %bitcast.10), calls=%async_computation.1 | async-start | bytes 1310720 | tf_op jit(solution)/shard_map/all_to_all | solution.py:625
  47.0 1.1 %collective-permute-start.6 = (bf16[4,640]{1,0:T(4,128)(2,1)S(1)}, bf16[4,640]{1,0:T(4,128)(2,1)S(1)}, u32[]{:S(2)}, u32[]{:S(2)}) collective-permute-start(bf16[4,640]{1,0:T(4,128)(2,1)S(1)} %pad_maximum_fusion.2), channel_id=1, source_target_pairs={{1,0},{2,1},{3,2},{0,3},{5,4},{6,5},{7,6},{4,7},{9,8},{10,9},{11,1... | collective-permute-start | bytes 15368 | tf_op jit(solution)/shard_map/ppermute | solution.py:609
  48.1 0.1 collective-permute-start.5
  48.1 1.0 %dynamic-slice_bitcast_fusion.2.table_ref = bf16[2,368,256]{2,1,0:T(8,128)(2,1)S(1)} fusion(bf16[4,2,368,256]{3,2,1,0:T(8,128)(2,1)} %constant.83.clone, s32[]{:T(128)S(6)} %select_n.77), kind=kLoop, calls=%fused_computation.2 | loop fusion | bytes 753668 | tf_op jit(solution)/shard_map/jit(dynamic_index_in_dim)/squeeze | solution.py:510
  49.2 0.0 copy-done.6
  49.2 0.1 copy.14.grid_ref
  49.2 0.0 copy-done.8
  49.2 1.1 %collective-permute-start.8 = (bf16[2,160,640]{2,1,0:T(8,128)(2,1)S(1)}, bf16[2,160,640]{2,1,0:T(8,128)(2,1)S(1)}, u32[]{:S(2)}, u32[]{:S(2)}) collective-permute-start(bf16[2,160,640]{2,1,0:T(8,128)(2,1)S(1)} %collective-permute-done.mix_c_ref), channel_id=1, source_target_pairs={{0,1},{1,0},{2,3},{3,2},{4,5},{5,4},{6,7},{7,6},{8,9},{9,8},{10,11... | collective-permute-start | bytes 1228808 | tf_op jit(solution)/shard_map/ppermute | solution.py:603
  50.3 0.1 collective-permute-done.6.east_ref
  50.5 0.7 collective-permute-done.5.west_ref
  51.2 1.5 %local.1 = (bf16[368,640]{1,0:T(8,128)(2,1)S(1)}, f32[8,128]{1,0:T(8,128)S(1)}) custom-call(bf16[180,640]{1,0:T(8,128)(2,1)S(1)} %collective-permute-done.3.above_ref, bf16[2,180,640]{2,1,0:T(8,128)(2,1)S(1)} %copy.14.grid_ref, bf16[180,640]{1,0:T(8,128)(2,1)S(1)} %collective-permute-done.4.below_ref, bf16[4,640]{1,0:T(4,128)(2,1)S(1)} %collective-permute-done.5.west_ref, ...), custom_call_target="tpu_custom_call" | custom-call | flops 8000000000 | tf_op jit(solution)/shard_map/local/pallas_call | solution.py:612
  52.7 0.0 copy-start.3
  52.7 0.8 %copy-done.3 = bf16[368,640]{1,0:T(8,128)(2,1)} copy-done((bf16[368,640]{1,0:T(8,128)(2,1)}, bf16[368,640]{1,0:T(8,128)(2,1)S(1)}, u32[]{:S(2)}) %copy-start.3) | copy-done | bytes 471064
  53.5 11.4 %all-to-all-done.1 = bf16[16,40,512]{2,1,0:T(8,128)(2,1)S(1)} async-done(((bf16[16,40,512]{2,1,0:T(8,128)(2,1)}), bf16[16,40,512]{2,1,0:T(8,128)(2,1)S(1)}, u32[]{:S(2)}, u32[]{:S(2)}) %all-to-all-start.1) | async-done | bytes 655392 | tf_op jit(solution)/shard_map/all_to_all | solution.py:625
  64.9 0.0 collective-permute-start.9
  64.9 0.0 collective-permute-done.7.mix_b_ref
  64.9 0.0 collective-permute-done.8.mix_d_ref
  64.9 0.0 copy-start
  64.9 0.0 copy-start.1
  64.9 0.0 copy-start.4
  64.9 1.0 %stage.1 = (f32[2,368,640]{2,1,0:T(8,128)S(1)}, bf16[2,640,640]{2,1,0:T(8,128)(2,1)S(1)}) custom-call(s32[1]{0:T(128)} %bitcast.place_ref, bf16[640,512]{1,0:T(8,128)(2,1)S(1)} %bitcast.40, bf16[2,368,256]{2,1,0:T(8,128)(2,1)S(1)} %dynamic-slice_bitcast_fusion.2.table_ref, bf16[2,160,640]{2,1,0:T(8,128)(2,1)S(1)} %bitcast.43, ...), custom_call_target="tpu_custom_call" | custom-call | flops 12000000000 | tf_op jit(solution)/shard_map/stage/pallas_call | solution.py:631
  65.9 1.0 %collective-permute-done.9.other_ref = bf16[640,512]{1,0:T(8,128)(2,1)S(1)} collective-permute-done((bf16[640,512]{1,0:T(8,128)(2,1)S(1)}, bf16[640,512]{1,0:T(8,128)(2,1)S(1)}, u32[]{:S(2)}, u32[]{:S(2)}) %collective-permute-start.9) | collective-permute-done | bytes 655392 | tf_op jit(solution)/shard_map/ppermute | solution.py:629
  67.0 0.0 copy-done
  67.0 0.0 copy-done.1
  67.0 0.0 copy-done.4
  67.0 3.2 %finish.1 = bf16[2,180,640]{2,1,0:T(8,128)(2,1)S(1)} custom-call(f32[2,368,640]{2,1,0:T(8,128)S(1)} %get-tuple-element.39.field_ref, bf16[640,512]{1,0:T(8,128)(2,1)S(1)} %collective-permute-done.9.other_ref, bf16[368,640]{1,0:T(8,128)(2,1)S(1)} %copy-done.4, f32[1,640]{1,0:T(1,128)S(1)} %broadcast_in_dim.55.gain_ref, ...), custom_call_target="tpu_custom_call" | custom-call | flops 3000000000 | tf_op jit(solution)/shard_map/finish/pallas_call | solution.py:648
  70.2 1.1 %copy.15 = bf16[2,180,640]{2,0,1:T(2,128)(2,1)} copy(bf16[2,180,640]{2,1,0:T(8,128)(2,1)S(1)} %finish.1) | data formatting | bytes 921600 | tf_op jit(solution)/shard_map/finish/pallas_call | solution.py:648
  (10 shorter events, 0.2 us)
Async XLA Ops:
  0.0 12.6 %copy-start.7 = (f32[3,3,640]{2,1,0:T(4,128)S(1)}, f32[3,3,640]{2,1,0:T(4,128)}, u32[]{:S(2)}) copy-start(f32[3,3,640]{2,1,0:T(4,128)} %param.11) | copy-start | bytes 69124
  0.0 2.3 %copy-start.2 = (bf16[2,640,160]{1,2,0:T(8,128)(2,1)S(1)}, bf16[2,640,160]{1,2,0:T(8,128)(2,1)}, u32[]{:S(2)}) copy-start(bf16[2,640,160]{1,2,0:T(8,128)(2,1)} %param.13) | copy-start | bytes 1228804
  2.3 13.6 %collective-permute-start = (bf16[2,160,640]{2,1,0:T(8,128)(2,1)S(1)}, bf16[2,160,640]{2,1,0:T(8,128)(2,1)S(1)}, u32[]{:S(2)}, u32[]{:S(2)}) collective-permute-start(bf16[2,160,640]{2,1,0:T(8,128)(2,1)S(1)} %bitcast.41), channel_id=1, source_target_pairs={{0,2},{2,0},{1,3},{3,1},{4,6},{6,4},{5,7},{7,5},{8,10},{10,8},{9,1... | collective-permute-start | bytes 1228808 | tf_op jit(solution)/shard_map/ppermute | solution.py:552
  5.2 59.7 %collective-permute-start.7 = (bf16[2,160,640]{2,1,0:T(8,128)(2,1)S(1)}, bf16[2,160,640]{2,1,0:T(8,128)(2,1)S(1)}, u32[]{:S(2)}, u32[]{:S(2)}) collective-permute-start(bf16[2,160,640]{2,1,0:T(8,128)(2,1)S(1)} %bitcast.42), channel_id=1, source_target_pairs={{0,1},{1,0},{2,3},{3,2},{4,5},{5,4},{6,7},{7,6},{8,9},{9,8},{10,11... | collective-permute-start | bytes 1228808 | tf_op jit(solution)/shard_map/ppermute | solution.py:602
  5.2 9.6 %copy-start.5 = (bf16[2,180,640]{2,0,1:T(2,128)(2,1)S(1)}, bf16[2,180,640]{2,0,1:T(2,128)(2,1)}, u32[]{:S(2)}) copy-start(bf16[2,180,640]{2,0,1:T(2,128)(2,1)} %param.10) | copy-start | bytes 1382404
  6.2 8.8 %collective-permute-start.2 = (bf16[2,40,256]{2,1,0:T(8,128)(2,1)S(1)}, bf16[2,40,256]{2,1,0:T(8,128)(2,1)S(1)}, u32[]{:S(2)}, u32[]{:S(2)}) collective-permute-start(bf16[2,40,256]{2,1,0:T(8,128)(2,1)S(1)} %dynamic-slice_bitcast_fusion.3), channel_id=1, source_target_pairs={{0,1},{1,0},{2,3},{3,2},{4,5},{5,4},{6,7},{7,6},{8,9},{9,8},{10,11... | collective-permute-start | bytes 122888 | tf_op jit(solution)/shard_map/ppermute | solution.py:559
  6.7 20.7 %all-to-all-start = ((bf16[16,120,128]{2,1,0:T(8,128)(2,1)}), bf16[16,120,128]{2,1,0:T(8,128)(2,1)S(1)}, u32[]{:S(2)}, u32[]{:S(2)}) async-start(bf16[16,120,128]{2,1,0:T(8,128)(2,1)} %pack.1), calls=%async_computation | async-start | bytes 983040 | tf_op jit(solution)/shard_map/all_to_all | solution.py:549
  27.4 3.9 %collective-permute-start.1 = (bf16[16,120,128]{2,1,0:T(8,128)(2,1)S(1)}, bf16[16,120,128]{2,1,0:T(8,128)(2,1)S(1)}, u32[]{:S(2)}, u32[]{:S(2)}) collective-permute-start(bf16[16,120,128]{2,1,0:T(8,128)(2,1)S(1)} %all-to-all-done.own_ref), channel_id=1, source_target_pairs={{0,1},{1,0},{2,3},{3,2},{4,5},{5,4},{6,7},{7,6},{8,9},{9,8},{10,11... | collective-permute-start | bytes 1474568 | tf_op jit(solution)/shard_map/ppermute | solution.py:580
  27.5 13.2 %collective-permute-start.3 = (bf16[180,640]{1,0:T(8,128)(2,1)S(1)}, bf16[180,640]{1,0:T(8,128)(2,1)S(1)}, u32[]{:S(2)}, u32[]{:S(2)}) collective-permute-start(bf16[180,640]{1,0:T(8,128)(2,1)S(1)} %get-tuple-element.44), channel_id=1, source_target_pairs={{0,4},{4,8},{8,12},{12,16},{16,20},{20,24},{24,28},{1,5},{5,9},{9,... | collective-permute-start | bytes 691208 | tf_op jit(solution)/shard_map/ppermute | solution.py:581
  30.0 10.7 %collective-permute-start.4 = (bf16[180,640]{1,0:T(8,128)(2,1)S(1)}, bf16[180,640]{1,0:T(8,128)(2,1)S(1)}, u32[]{:S(2)}, u32[]{:S(2)}) collective-permute-start(bf16[180,640]{1,0:T(8,128)(2,1)S(1)} %get-tuple-element.43), channel_id=1, source_target_pairs={{4,0},{8,4},{12,8},{16,12},{20,16},{24,20},{28,24},{5,1},{9,5},{13... | collective-permute-start | bytes 691208 | tf_op jit(solution)/shard_map/ppermute | solution.py:582
  39.8 9.3 %copy-start.6 = (bf16[2,180,640]{2,0,1:T(2,128)(2,1)S(1)}, bf16[2,180,640]{2,0,1:T(2,128)(2,1)}, u32[]{:S(2)}) copy-start(bf16[2,180,640]{2,0,1:T(2,128)(2,1)} %param.10) | copy-start | bytes 1382404
  39.8 9.4 %copy-start.8 = (f32[640]{0:T(1024)S(1)}, f32[640]{0:T(1024)}, u32[]{:S(2)}) copy-start(f32[640]{0:T(1024)} %param.14) | copy-start | bytes 7684
  40.7 24.2 %all-to-all-start.1 = ((bf16[16,40,512]{2,1,0:T(8,128)(2,1)}), bf16[16,40,512]{2,1,0:T(8,128)(2,1)S(1)}, u32[]{:S(2)}, u32[]{:S(2)}) async-start(bf16[16,40,512]{2,1,0:T(8,128)(2,1)} %bitcast.10), calls=%async_computation.1 | async-start | bytes 1310720 | tf_op jit(solution)/shard_map/all_to_all | solution.py:625
  47.0 3.5 %collective-permute-start.6 = (bf16[4,640]{1,0:T(4,128)(2,1)S(1)}, bf16[4,640]{1,0:T(4,128)(2,1)S(1)}, u32[]{:S(2)}, u32[]{:S(2)}) collective-permute-start(bf16[4,640]{1,0:T(4,128)(2,1)S(1)} %pad_maximum_fusion.2), channel_id=1, source_target_pairs={{1,0},{2,1},{3,2},{0,3},{5,4},{6,5},{7,6},{4,7},{9,8},{10,9},{11,1... | collective-permute-start | bytes 15368 | tf_op jit(solution)/shard_map/ppermute | solution.py:609
  48.1 3.1 %collective-permute-start.5 = (bf16[4,640]{1,0:T(4,128)(2,1)S(1)}, bf16[4,640]{1,0:T(4,128)(2,1)S(1)}, u32[]{:S(2)}, u32[]{:S(2)}) collective-permute-start(bf16[4,640]{1,0:T(4,128)(2,1)S(1)} %pad_maximum_fusion.1), channel_id=1, source_target_pairs={{0,1},{1,2},{2,3},{3,0},{4,5},{5,6},{6,7},{7,4},{8,9},{9,10},{10,1... | collective-permute-start | bytes 15368 | tf_op jit(solution)/shard_map/ppermute | solution.py:606
  49.2 15.6 %collective-permute-start.8 = (bf16[2,160,640]{2,1,0:T(8,128)(2,1)S(1)}, bf16[2,160,640]{2,1,0:T(8,128)(2,1)S(1)}, u32[]{:S(2)}, u32[]{:S(2)}) collective-permute-start(bf16[2,160,640]{2,1,0:T(8,128)(2,1)S(1)} %collective-permute-done.mix_c_ref), channel_id=1, source_target_pairs={{0,1},{1,0},{2,3},{3,2},{4,5},{5,4},{6,7},{7,6},{8,9},{9,8},{10,11... | collective-permute-start | bytes 1228808 | tf_op jit(solution)/shard_map/ppermute | solution.py:603
  52.7 0.8 %copy-start.3 = (bf16[368,640]{1,0:T(8,128)(2,1)}, bf16[368,640]{1,0:T(8,128)(2,1)S(1)}, u32[]{:S(2)}) copy-start(bf16[368,640]{1,0:T(8,128)(2,1)S(1)} %get-tuple-element.40.first_ref) | copy-start | bytes 1413124
  64.9 2.1 %collective-permute-start.9 = (bf16[640,512]{1,0:T(8,128)(2,1)S(1)}, bf16[640,512]{1,0:T(8,128)(2,1)S(1)}, u32[]{:S(2)}, u32[]{:S(2)}) collective-permute-start(bf16[640,512]{1,0:T(8,128)(2,1)S(1)} %bitcast.39), channel_id=1, source_target_pairs={{0,1},{1,0},{2,3},{3,2},{4,5},{5,4},{6,7},{7,6},{8,9},{9,8},{10,11... | collective-permute-start | bytes 1966088 | tf_op jit(solution)/shard_map/ppermute | solution.py:629
  64.9 2.1 %copy-start = (bf16[640,1280]{1,0:T(8,128)(2,1)S(1)}, bf16[640,1280]{1,0:T(8,128)(2,1)}, u32[]{:S(2)}) copy-start(bf16[640,1280]{1,0:T(8,128)(2,1)} %expand_ref.1) | copy-start | bytes 4915204
  64.9 2.1 %copy-start.1 = (bf16[1280,640]{1,0:T(8,128)(2,1)S(1)}, bf16[1280,640]{1,0:T(8,128)(2,1)}, u32[]{:S(2)}) copy-start(bf16[1280,640]{1,0:T(8,128)(2,1)} %reduce_ref.1) | copy-start | bytes 4915204
  64.9 2.1 %copy-start.4 = (bf16[368,640]{1,0:T(8,128)(2,1)S(1)}, bf16[368,640]{1,0:T(8,128)(2,1)}, u32[]{:S(2)}) copy-start(bf16[368,640]{1,0:T(8,128)(2,1)} %copy-done.3) | copy-start | bytes 1413124

commit v3 on v2

--- a/solution.py
+++ b/solution.py
@@ -542,6 +542,7 @@
         compiler_params=pltpu.CompilerParams(vmem_limit_bytes=16 << 20),
         name="pack",
     )(grid_state)
+    grid_first = grid_state
     packed, later = lax.optimization_barrier(
         (packed, (grid_state, conv_weight, spectral_gain, spectral_weight))
     )
@@ -549,7 +550,6 @@
     own = lax.all_to_all(packed, over_chips, split_axis=0, concat_axis=0, tiled=True)
 
     own_mix = spectral_weight.transpose(0, 2, 1)
-    across_mix = lax.ppermute(own_mix, "x", [(i, 1 - i) for i in range(columns)])
     held = own_mix.shape[1]
 
     blocks = held // share
@@ -576,10 +576,11 @@
     analysis = own_part(analysis_constant(sectors, width, span, M), core)
     table = own_part(synthesis_constant(sectors, width, padded, M), 2 * column + core)
 
-    own, grid_late, across_mix = lax.optimization_barrier((own, grid_state, across_mix))
+    across_mix = lax.ppermute(own_mix, "x", [(i, 1 - i) for i in range(columns)])
+    own, across_mix = lax.optimization_barrier((own, across_mix))
     other = lax.ppermute(own, "core", swap)
-    above = lax.ppermute(grid_late[1], "lat", [(i, i + 1) for i in range(lat_count - 1)])
-    below = lax.ppermute(grid_late[0], "lat", [(i + 1, i) for i in range(lat_count - 1)])
+    above = lax.ppermute(grid_first[1], "lat", [(i, i + 1) for i in range(lat_count - 1)])
+    below = lax.ppermute(grid_first[0], "lat", [(i + 1, i) for i in range(lat_count - 1)])
 
     bands = pl.pallas_call(
         functools.partial(spectral_body, lat_count, columns, share, width),

time: 71.8 us -> 67.4 us (0.939)
  waiting for transfers between devices: 25.6 us -> 20.1 us
  local copies, waits for them, and re-layouts: 7.58 us -> 9.54 us
  starting transfers between devices: 21.6 us -> 20.7 us
    all_to_all x1, waiting for transfers between devices: 11.5 us -> 5.84 us  [chip_shards(): lax.all_to_all(packed, over_chips, split_axis=0, concat_axis=0, tiled=True)]
    all_to_all x1, starting transfers between devices: 6.21 us -> 3.99 us  [chip_shards(): lax.all_to_all(bands.reshape(chips, share, 2 * M), over_chips, split_axis...]
    ppermute x2, starting transfers between devices: 3.77 us -> 5.12 us  [the longest x1 3.83 us: chip_shards(): lax.ppermute(grid_first[1], 'lat', [(i, i + 1) for i in range(lat_count -...]
    ppermute x1, waiting for transfers between devices: 0.01 us -> 0.91 us  [chip_shards(): other = lax.ppermute(own, 'core', swap)]
    ppermute x2, waiting for transfers between devices: 0.86 us -> 0.01 us  [the longest x1 0.01 us: chip_shards(): lax.ppermute(grid_first[1], 'lat', [(i, i + 1) for i in range(lat_count -...]
    slice x2, local copies, waits for them, and re-layouts: 0.03 us -> 0.79 us  [chip_shards(): row[0]]
    unnamed x19 -> x17, local copies, waits for them, and re-layouts: 1.94 us -> 1.95 us
  transfers between devices with their start and end apart: 12 -> 12, of which waited for: 6 -> 6; matrix products, arithmetic and copies ran while one was open for 8% -> 11% of each run, Pallas kernels for 15% -> 16%
where the time goes in v3:
time: 67.4 us; the launch traced here: 66.8 us
  starting transfers between devices  20.7 us (31%)
  waiting for transfers between devices  20.1 us (30%)
  Pallas kernels  15.1 us (22%)
  local copies, waits for them, and re-layouts  9.54 us (14%)
  other arithmetic  0.98 us (1%)
    all_to_all x1, waiting for transfers between devices, chip_shards(): lax.all_to_all(bands.reshape(chips, share, 2 * M), over_chips, split_axis...  11.4 us
    pallas_call x1, Pallas kernels, chip_shards(): pl.pallas_call(functools.partial(spectral_body, lat_count, columns, share...  8.32 us
    all_to_all x1, starting transfers between devices, chip_shards(): lax.all_to_all(packed, over_chips, split_axis=0, concat_axis=0, tiled=True)  5.94 us
    all_to_all x1, waiting for transfers between devices, chip_shards(): lax.all_to_all(packed, over_chips, split_axis=0, concat_axis=0, tiled=True)  5.84 us
    all_to_all x1, starting transfers between devices, chip_shards(): lax.all_to_all(bands.reshape(chips, share, 2 * M), over_chips, split_axis...  3.99 us
    ppermute x1, starting transfers between devices, chip_shards(): lax.ppermute(grid_first[1], 'lat', [(i, i + 1) for i in range(lat_count -...  3.83 us
    squeeze x3, local copies, waits for them, and re-layouts, own_part(): lax.dynamic_index_in_dim(jnp.asarray(constant), at, 0, keepdims=False)  3.19 us
    pallas_call x1, Pallas kernels, chip_shards(): pl.pallas_call(functools.partial(finish_body, width, padded), out_shape=j...  3.15 us
  transfers between devices with their start and end apart: 12, of which 6 were waited for; matrix products, arithmetic and copies ran while one was open for 11% of the time, Pallas kernels for 16%

profile of v3, /device:TPU:0, one launch (start us, length us, event | category | flops | bytes accessed | tf_op | source)
XLA Modules:
  0.0 66.8 jit_solution(14799539987644761002)
XLA Ops:
  0.0 0.0 copy-start.2
  0.0 1.1 %copy.11.grid_ref = bf16[2,180,640]{2,1,0:T(8,128)(2,1)S(1)} copy(bf16[2,180,640]{2,0,1:T(2,128)(2,1)} %param.10) | data formatting | bytes 921600 | tf_op args[0]
  1.1 0.0 copy-start.6
  1.1 1.1 %pack.1 = bf16[16,120,128]{2,1,0:T(8,128)(2,1)} custom-call(bf16[2,180,640]{2,1,0:T(8,128)(2,1)S(1)} %copy.11.grid_ref), custom_call_target="tpu_custom_call" | custom-call | tf_op jit(solution)/shard_map/pack/pallas_call | solution.py:536
  2.3 0.0 copy-done.2
  2.3 2.9 %collective-permute-start = (bf16[2,160,640]{2,1,0:T(8,128)(2,1)S(1)}, bf16[2,160,640]{2,1,0:T(8,128)(2,1)S(1)}, u32[]{:S(2)}, u32[]{:S(2)}) collective-permute-start(bf16[2,160,640]{2,1,0:T(8,128)(2,1)S(1)} %bitcast.41), channel_id=1, source_target_pairs={{0,2},{2,0},{1,3},{3,1},{4,6},{6,4},{5,7},{7,5},{8,10},{10,8},{9,1... | collective-permute-start | bytes 1228808 | tf_op jit(solution)/shard_map/ppermute | solution.py:579
  5.2 0.0 collective-permute-start.7
  5.2 1.5 %dynamic-slice_bitcast_fusion.3 = bf16[2,40,256]{2,1,0:T(8,128)(2,1)} fusion(f32[2,256,160]{1,2,0:T(8,128)} %param.12, s32[]{:T(128)S(6)} %select_n.69), kind=kLoop, calls=%fused_computation.6 | loop fusion | bytes 81924 | tf_op jit(solution)/shard_map/transpose | solution.py:558
  6.7 0.5 collective-permute-start.2
  7.2 5.9 %all-to-all-start = ((bf16[16,120,128]{2,1,0:T(8,128)(2,1)}), bf16[16,120,128]{2,1,0:T(8,128)(2,1)S(1)}, u32[]{:S(2)}, u32[]{:S(2)}) async-start(bf16[16,120,128]{2,1,0:T(8,128)(2,1)} %pack.1), calls=%async_computation | async-start | bytes 983040 | tf_op jit(solution)/shard_map/all_to_all | solution.py:550
  13.2 0.7 %slice_bitcast_fusion = (bf16[180,640]{1,0:T(8,128)(2,1)S(1)}, bf16[180,640]{1,0:T(8,128)(2,1)}) fusion(bf16[2,180,640]{2,1,0:T(8,128)(2,1)S(1)} %copy.11.grid_ref), kind=kLoop, calls=%fused_computation.3 | loop fusion | bytes 921600 | tf_op jit(solution)/shard_map/squeeze | solution.py:583
  13.9 3.8 %collective-permute-start.3 = (bf16[180,640]{1,0:T(8,128)(2,1)}, bf16[180,640]{1,0:T(8,128)(2,1)S(1)}, u32[]{:S(2)}, u32[]{:S(2)}) collective-permute-start(bf16[180,640]{1,0:T(8,128)(2,1)} %get-tuple-element.42), channel_id=1, source_target_pairs={{0,4},{4,8},{8,12},{12,16},{16,20},{20,24},{24,28},{1,5},{5,9},{9,... | collective-permute-start | bytes 691208 | tf_op jit(solution)/shard_map/ppermute | solution.py:582
  17.7 1.3 %collective-permute-start.4 = (bf16[180,640]{1,0:T(8,128)(2,1)S(1)}, bf16[180,640]{1,0:T(8,128)(2,1)S(1)}, u32[]{:S(2)}, u32[]{:S(2)}) collective-permute-start(bf16[180,640]{1,0:T(8,128)(2,1)S(1)} %get-tuple-element.41), channel_id=1, source_target_pairs={{4,0},{8,4},{12,8},{16,12},{20,16},{24,20},{28,24},{5,1},{9,5},{13... | collective-permute-start | bytes 691208 | tf_op jit(solution)/shard_map/ppermute | solution.py:583
  19.1 0.0 copy-done.6
  19.1 1.1 %dynamic-slice_bitcast_fusion.table_ref = bf16[4,256,256]{2,1,0:T(8,128)(2,1)S(1)} fusion(bf16[2,4,256,256]{3,2,1,0:T(8,128)(2,1)} %constant.82.clone, s32[]{:T(128)S(6)} %select_n.76), kind=kLoop, calls=%fused_computation | loop fusion | bytes 1048580 | tf_op jit(solution)/shard_map/jit(dynamic_index_in_dim)/squeeze | solution.py:510
  20.2 1.1 %dynamic-slice_bitcast_fusion.1.legendre_ref = bf16[8,256,128]{2,1,0:T(8,128)(2,1)S(1)} fusion(bf16[2,8,256,128]{3,2,1,0:T(8,128)(2,1)} %constant.81.clone, s32[]{:T(128)S(6)} %select_n.76), kind=kLoop, calls=%fused_computation.1 | loop fusion | bytes 1048580 | tf_op jit(solution)/shard_map/jit(dynamic_index_in_dim)/squeeze | solution.py:510
  21.3 0.1 constant_dynamic-slice_fusion
  21.3 0.8 %slice_bitcast_fusion.5 = (bf16[1,640]{1,0:T(2,128)(2,1)S(1)}, bf16[1,640]{1,0:T(2,128)(2,1)S(1)}, bf16[1,640]{1,0:T(2,128)(2,1)S(1)}, bf16[1,640]{1,0:T(2,128)(2,1)S(1)}) fusion(bf16[2,180,640]{2,0,1:T(2,128)(2,1)} %param.10), kind=kLoop, calls=%fused_computation.17 | loop fusion | bytes 10240 | tf_op jit(solution)/shard_map/slice | solution.py:611
  22.2 0.0 collective-permute-done.mix_c_ref
  22.2 5.8 %all-to-all-done.own_ref = bf16[16,120,128]{2,1,0:T(8,128)(2,1)S(1)} async-done(((bf16[16,120,128]{2,1,0:T(8,128)(2,1)}), bf16[16,120,128]{2,1,0:T(8,128)(2,1)S(1)}, u32[]{:S(2)}, u32[]{:S(2)}) %all-to-all-start) | async-done | bytes 491552 | tf_op jit(solution)/shard_map/all_to_all | solution.py:550
  28.0 0.0 collective-permute-start.1
  28.0 0.0 collective-permute-done.2
  28.0 0.9 %broadcast_select_fusion = bf16[2,40,256]{2,1,0:T(8,128)(2,1)S(1)} fusion(bf16[2,40,256]{2,1,0:T(8,128)(2,1)} %collective-permute-done.2, pred[]{:T(512)S(6)} %eq.22, f32[2,256,160]{1,2,0:T(8,128)} %param.12, s32[]{:T(128)S(6)} %select_n.69), kind=kLoop, calls=%fused_computation.13 | loop fusion | flops 20480 | bytes 122885 | tf_op jit(solution)/shard_map/jit(_where)/select_n | solution.py:560
  29.0 0.9 %collective-permute-done.1.other_any = bf16[16,120,128]{2,1,0:T(8,128)(2,1)S(1)} collective-permute-done((bf16[16,120,128]{2,1,0:T(8,128)(2,1)S(1)}, bf16[16,120,128]{2,1,0:T(8,128)(2,1)S(1)}, u32[]{:S(2)}, u32[]{:S(2)}) %collective-permute-start.1) | collective-permute-done | bytes 491552 | tf_op jit(solution)/shard_map/ppermute | solution.py:581
  29.9 0.1 broadcast_in_dim.54.tap_ref
  30.0 8.3 %spectral.1 = bf16[2,8,40,512]{3,2,1,0:T(8,128)(2,1)} custom-call(s32[1]{0:T(128)} %bitcast.1.parity_ref, bf16[16,120,128]{2,1,0:T(8,128)(2,1)S(1)} %all-to-all-done.own_ref, bf16[16,120,128]{2,1,0:T(8,128)(2,1)S(1)} %collective-permute-done.1.other_any, bf16[160,256]{1,0:T(8,128)(2,1)S(1)} %pad_maximum_fusion.gain_ref, ...), custom_call_target="tpu_custom_call" | custom-call | flops 8999999488 | tf_op jit(solution)/shard_map/spectral/pallas_call | solution.py:585
  38.3 0.0 copy-start.5
  38.3 0.0 copy-start.7
  38.3 0.0 collective-permute-done.3.above_ref
  38.3 0.0 collective-permute-done.4.below_ref
  38.4 4.0 %all-to-all-start.1 = ((bf16[16,40,512]{2,1,0:T(8,128)(2,1)}), bf16[16,40,512]{2,1,0:T(8,128)(2,1)S(1)}, u32[]{:S(2)}, u32[]{:S(2)}) async-start(bf16[16,40,512]{2,1,0:T(8,128)(2,1)} %bitcast.10), calls=%async_computation.1 | async-start | bytes 1310720 | tf_op jit(solution)/shard_map/all_to_all | solution.py:626
  42.4 1.1 %collective-permute-start.6 = (bf16[4,640]{1,0:T(4,128)(2,1)S(1)}, bf16[4,640]{1,0:T(4,128)(2,1)S(1)}, u32[]{:S(2)}, u32[]{:S(2)}) collective-permute-start(bf16[4,640]{1,0:T(4,128)(2,1)S(1)} %pad_maximum_fusion.2), channel_id=1, source_target_pairs={{1,0},{2,1},{3,2},{0,3},{5,4},{6,5},{7,6},{4,7},{9,8},{10,9},{11,1... | collective-permute-start | bytes 15368 | tf_op jit(solution)/shard_map/ppermute | solution.py:610
  43.6 0.1 collective-permute-start.5
  43.6 1.0 %dynamic-slice_bitcast_fusion.2.table_ref = bf16[2,368,256]{2,1,0:T(8,128)(2,1)S(1)} fusion(bf16[4,2,368,256]{3,2,1,0:T(8,128)(2,1)} %constant.83.clone, s32[]{:T(128)S(6)} %select_n.77), kind=kLoop, calls=%fused_computation.2 | loop fusion | bytes 753668 | tf_op jit(solution)/shard_map/jit(dynamic_index_in_dim)/squeeze | solution.py:510
  44.7 0.0 copy-done.5
  44.7 0.1 copy.14.grid_ref
  44.7 0.0 copy-done.7
  44.8 1.0 %collective-permute-start.8 = (bf16[2,160,640]{2,1,0:T(8,128)(2,1)S(1)}, bf16[2,160,640]{2,1,0:T(8,128)(2,1)S(1)}, u32[]{:S(2)}, u32[]{:S(2)}) collective-permute-start(bf16[2,160,640]{2,1,0:T(8,128)(2,1)S(1)} %collective-permute-done.mix_c_ref), channel_id=1, source_target_pairs={{0,1},{1,0},{2,3},{3,2},{4,5},{5,4},{6,7},{7,6},{8,9},{9,8},{10,11... | collective-permute-start | bytes 1228808 | tf_op jit(solution)/shard_map/ppermute | solution.py:604
  45.8 0.2 collective-permute-done.6.east_ref
  45.9 0.7 %collective-permute-done.5.west_ref = bf16[4,640]{1,0:T(4,128)(2,1)S(1)} collective-permute-done((bf16[4,640]{1,0:T(4,128)(2,1)S(1)}, bf16[4,640]{1,0:T(4,128)(2,1)S(1)}, u32[]{:S(2)}, u32[]{:S(2)}) %collective-permute-start.5) | collective-permute-done | bytes 5152 | tf_op jit(solution)/shard_map/ppermute | solution.py:607
  46.7 1.5 %local.1 = (bf16[368,640]{1,0:T(8,128)(2,1)S(1)}, f32[8,128]{1,0:T(8,128)S(1)}) custom-call(bf16[180,640]{1,0:T(8,128)(2,1)S(1)} %collective-permute-done.3.above_ref, bf16[2,180,640]{2,1,0:T(8,128)(2,1)S(1)} %copy.14.grid_ref, bf16[180,640]{1,0:T(8,128)(2,1)S(1)} %collective-permute-done.4.below_ref, bf16[4,640]{1,0:T(4,128)(2,1)S(1)} %collective-permute-done.5.west_ref, ...), custom_call_target="tpu_custom_call" | custom-call | flops 8000000000 | tf_op jit(solution)/shard_map/local/pallas_call | solution.py:613
  48.2 0.0 copy-start.3
  48.2 0.8 %copy-done.3 = bf16[368,640]{1,0:T(8,128)(2,1)} copy-done((bf16[368,640]{1,0:T(8,128)(2,1)}, bf16[368,640]{1,0:T(8,128)(2,1)S(1)}, u32[]{:S(2)}) %copy-start.3) | copy-done | bytes 471064
  49.0 11.4 %all-to-all-done.1 = bf16[16,40,512]{2,1,0:T(8,128)(2,1)S(1)} async-done(((bf16[16,40,512]{2,1,0:T(8,128)(2,1)}), bf16[16,40,512]{2,1,0:T(8,128)(2,1)S(1)}, u32[]{:S(2)}, u32[]{:S(2)}) %all-to-all-start.1) | async-done | bytes 655392 | tf_op jit(solution)/shard_map/all_to_all | solution.py:626
  60.4 0.0 collective-permute-start.9
  60.4 0.0 collective-permute-done.7.mix_b_ref
  60.4 0.0 collective-permute-done.8.mix_d_ref
  60.4 0.0 copy-start
  60.4 0.0 copy-start.1
  60.4 0.0 copy-start.4
  60.4 1.0 %stage.1 = (f32[2,368,640]{2,1,0:T(8,128)S(1)}, bf16[2,640,640]{2,1,0:T(8,128)(2,1)S(1)}) custom-call(s32[1]{0:T(128)} %bitcast.place_ref, bf16[640,512]{1,0:T(8,128)(2,1)S(1)} %bitcast.40, bf16[2,368,256]{2,1,0:T(8,128)(2,1)S(1)} %dynamic-slice_bitcast_fusion.2.table_ref, bf16[2,160,640]{2,1,0:T(8,128)(2,1)S(1)} %bitcast.43, ...), custom_call_target="tpu_custom_call" | custom-call | flops 12000000000 | tf_op jit(solution)/shard_map/stage/pallas_call | solution.py:632
  61.4 1.0 %collective-permute-done.9.other_ref = bf16[640,512]{1,0:T(8,128)(2,1)S(1)} collective-permute-done((bf16[640,512]{1,0:T(8,128)(2,1)S(1)}, bf16[640,512]{1,0:T(8,128)(2,1)S(1)}, u32[]{:S(2)}, u32[]{:S(2)}) %collective-permute-start.9) | collective-permute-done | bytes 655392 | tf_op jit(solution)/shard_map/ppermute | solution.py:630
  62.5 0.0 copy-done
  62.5 0.0 copy-done.1
  62.5 0.0 copy-done.4
  62.5 3.2 %finish.1 = bf16[2,180,640]{2,1,0:T(8,128)(2,1)S(1)} custom-call(f32[2,368,640]{2,1,0:T(8,128)S(1)} %get-tuple-element.37.field_ref, bf16[640,512]{1,0:T(8,128)(2,1)S(1)} %collective-permute-done.9.other_ref, bf16[368,640]{1,0:T(8,128)(2,1)S(1)} %copy-done.4, f32[1,640]{1,0:T(1,128)S(1)} %broadcast_in_dim.55.gain_ref, ...), custom_call_target="tpu_custom_call" | custom-call | flops 3000000000 | tf_op jit(solution)/shard_map/finish/pallas_call | solution.py:649
  65.6 1.1 %copy.15 = bf16[2,180,640]{2,0,1:T(2,128)(2,1)} copy(bf16[2,180,640]{2,1,0:T(8,128)(2,1)S(1)} %finish.1) | data formatting | bytes 921600 | tf_op jit(solution)/shard_map/finish/pallas_call | solution.py:649
  (8 shorter events, 0.1 us)
Async XLA Ops:
  0.0 2.3 %copy-start.2 = (bf16[2,640,160]{1,2,0:T(8,128)(2,1)S(1)}, bf16[2,640,160]{1,2,0:T(8,128)(2,1)}, u32[]{:S(2)}) copy-start(bf16[2,640,160]{1,2,0:T(8,128)(2,1)} %param.13) | copy-start | bytes 1228804
  1.1 17.9 %copy-start.6 = (f32[3,3,640]{2,1,0:T(4,128)S(1)}, f32[3,3,640]{2,1,0:T(4,128)}, u32[]{:S(2)}) copy-start(f32[3,3,640]{2,1,0:T(4,128)} %param.11) | copy-start | bytes 69124
  2.3 19.9 %collective-permute-start = (bf16[2,160,640]{2,1,0:T(8,128)(2,1)S(1)}, bf16[2,160,640]{2,1,0:T(8,128)(2,1)S(1)}, u32[]{:S(2)}, u32[]{:S(2)}) collective-permute-start(bf16[2,160,640]{2,1,0:T(8,128)(2,1)S(1)} %bitcast.41), channel_id=1, source_target_pairs={{0,2},{2,0},{1,3},{3,1},{4,6},{6,4},{5,7},{7,5},{8,10},{10,8},{9,1... | collective-permute-start | bytes 1228808 | tf_op jit(solution)/shard_map/ppermute | solution.py:579
  5.2 55.2 %collective-permute-start.7 = (bf16[2,160,640]{2,1,0:T(8,128)(2,1)S(1)}, bf16[2,160,640]{2,1,0:T(8,128)(2,1)S(1)}, u32[]{:S(2)}, u32[]{:S(2)}) collective-permute-start(bf16[2,160,640]{2,1,0:T(8,128)(2,1)S(1)} %bitcast.42), channel_id=1, source_target_pairs={{0,1},{1,0},{2,3},{3,2},{4,5},{5,4},{6,7},{7,6},{8,9},{9,8},{10,11... | collective-permute-start | bytes 1228808 | tf_op jit(solution)/shard_map/ppermute | solution.py:603
  6.7 21.3 %collective-permute-start.2 = (bf16[2,40,256]{2,1,0:T(8,128)(2,1)}, bf16[2,40,256]{2,1,0:T(8,128)(2,1)}, u32[]{:S(2)}, u32[]{:S(2)}) collective-permute-start(bf16[2,40,256]{2,1,0:T(8,128)(2,1)} %dynamic-slice_bitcast_fusion.3), channel_id=1, source_target_pairs={{0,1},{1,0},{2,3},{3,2},{4,5},{5,4},{6,7},{7,6},{8,9},{9,8},{10,11... | collective-permute-start | bytes 122888 | tf_op jit(solution)/shard_map/ppermute | solution.py:559
  7.2 20.8 %all-to-all-start = ((bf16[16,120,128]{2,1,0:T(8,128)(2,1)}), bf16[16,120,128]{2,1,0:T(8,128)(2,1)S(1)}, u32[]{:S(2)}, u32[]{:S(2)}) async-start(bf16[16,120,128]{2,1,0:T(8,128)(2,1)} %pack.1), calls=%async_computation | async-start | bytes 983040 | tf_op jit(solution)/shard_map/all_to_all | solution.py:550
  13.9 24.4 %collective-permute-start.3 = (bf16[180,640]{1,0:T(8,128)(2,1)}, bf16[180,640]{1,0:T(8,128)(2,1)S(1)}, u32[]{:S(2)}, u32[]{:S(2)}) collective-permute-start(bf16[180,640]{1,0:T(8,128)(2,1)} %get-tuple-element.42), channel_id=1, source_target_pairs={{0,4},{4,8},{8,12},{12,16},{16,20},{20,24},{24,28},{1,5},{5,9},{9,... | collective-permute-start | bytes 691208 | tf_op jit(solution)/shard_map/ppermute | solution.py:582
  17.7 20.6 %collective-permute-start.4 = (bf16[180,640]{1,0:T(8,128)(2,1)S(1)}, bf16[180,640]{1,0:T(8,128)(2,1)S(1)}, u32[]{:S(2)}, u32[]{:S(2)}) collective-permute-start(bf16[180,640]{1,0:T(8,128)(2,1)S(1)} %get-tuple-element.41), channel_id=1, source_target_pairs={{4,0},{8,4},{12,8},{16,12},{20,16},{24,20},{28,24},{5,1},{9,5},{13... | collective-permute-start | bytes 691208 | tf_op jit(solution)/shard_map/ppermute | solution.py:583
  28.0 1.9 %collective-permute-start.1 = (bf16[16,120,128]{2,1,0:T(8,128)(2,1)S(1)}, bf16[16,120,128]{2,1,0:T(8,128)(2,1)S(1)}, u32[]{:S(2)}, u32[]{:S(2)}) collective-permute-start(bf16[16,120,128]{2,1,0:T(8,128)(2,1)S(1)} %all-to-all-done.own_ref), channel_id=1, source_target_pairs={{0,1},{1,0},{2,3},{3,2},{4,5},{5,4},{6,7},{7,6},{8,9},{9,8},{10,11... | collective-permute-start | bytes 1474568 | tf_op jit(solution)/shard_map/ppermute | solution.py:581
  38.3 6.4 %copy-start.5 = (bf16[2,180,640]{2,0,1:T(2,128)(2,1)S(1)}, bf16[2,180,640]{2,0,1:T(2,128)(2,1)}, u32[]{:S(2)}) copy-start(bf16[2,180,640]{2,0,1:T(2,128)(2,1)} %param.10) | copy-start | bytes 1382404
  38.3 6.4 %copy-start.7 = (f32[640]{0:T(1024)S(1)}, f32[640]{0:T(1024)}, u32[]{:S(2)}) copy-start(f32[640]{0:T(1024)} %param.14) | copy-start | bytes 7684
  38.4 22.0 %all-to-all-start.1 = ((bf16[16,40,512]{2,1,0:T(8,128)(2,1)}), bf16[16,40,512]{2,1,0:T(8,128)(2,1)S(1)}, u32[]{:S(2)}, u32[]{:S(2)}) async-start(bf16[16,40,512]{2,1,0:T(8,128)(2,1)} %bitcast.10), calls=%async_computation.1 | async-start | bytes 1310720 | tf_op jit(solution)/shard_map/all_to_all | solution.py:626
  42.4 3.5 %collective-permute-start.6 = (bf16[4,640]{1,0:T(4,128)(2,1)S(1)}, bf16[4,640]{1,0:T(4,128)(2,1)S(1)}, u32[]{:S(2)}, u32[]{:S(2)}) collective-permute-start(bf16[4,640]{1,0:T(4,128)(2,1)S(1)} %pad_maximum_fusion.2), channel_id=1, source_target_pairs={{1,0},{2,1},{3,2},{0,3},{5,4},{6,5},{7,6},{4,7},{9,8},{10,9},{11,1... | collective-permute-start | bytes 15368 | tf_op jit(solution)/shard_map/ppermute | solution.py:610
  43.6 3.1 %collective-permute-start.5 = (bf16[4,640]{1,0:T(4,128)(2,1)S(1)}, bf16[4,640]{1,0:T(4,128)(2,1)S(1)}, u32[]{:S(2)}, u32[]{:S(2)}) collective-permute-start(bf16[4,640]{1,0:T(4,128)(2,1)S(1)} %pad_maximum_fusion.1), channel_id=1, source_target_pairs={{0,1},{1,2},{2,3},{3,0},{4,5},{5,6},{6,7},{7,4},{8,9},{9,10},{10,1... | collective-permute-start | bytes 15368 | tf_op jit(solution)/shard_map/ppermute | solution.py:607
  44.8 15.6 %collective-permute-start.8 = (bf16[2,160,640]{2,1,0:T(8,128)(2,1)S(1)}, bf16[2,160,640]{2,1,0:T(8,128)(2,1)S(1)}, u32[]{:S(2)}, u32[]{:S(2)}) collective-permute-start(bf16[2,160,640]{2,1,0:T(8,128)(2,1)S(1)} %collective-permute-done.mix_c_ref), channel_id=1, source_target_pairs={{0,1},{1,0},{2,3},{3,2},{4,5},{5,4},{6,7},{7,6},{8,9},{9,8},{10,11... | collective-permute-start | bytes 1228808 | tf_op jit(solution)/shard_map/ppermute | solution.py:604
  48.2 0.8 %copy-start.3 = (bf16[368,640]{1,0:T(8,128)(2,1)}, bf16[368,640]{1,0:T(8,128)(2,1)S(1)}, u32[]{:S(2)}) copy-start(bf16[368,640]{1,0:T(8,128)(2,1)S(1)} %get-tuple-element.38.first_ref) | copy-start | bytes 1413124
  60.4 2.1 %collective-permute-start.9 = (bf16[640,512]{1,0:T(8,128)(2,1)S(1)}, bf16[640,512]{1,0:T(8,128)(2,1)S(1)}, u32[]{:S(2)}, u32[]{:S(2)}) collective-permute-start(bf16[640,512]{1,0:T(8,128)(2,1)S(1)} %bitcast.39), channel_id=1, source_target_pairs={{0,1},{1,0},{2,3},{3,2},{4,5},{5,4},{6,7},{7,6},{8,9},{9,8},{10,11... | collective-permute-start | bytes 1966088 | tf_op jit(solution)/shard_map/ppermute | solution.py:630
  60.4 2.1 %copy-start = (bf16[640,1280]{1,0:T(8,128)(2,1)S(1)}, bf16[640,1280]{1,0:T(8,128)(2,1)}, u32[]{:S(2)}) copy-start(bf16[640,1280]{1,0:T(8,128)(2,1)} %expand_ref.1) | copy-start | bytes 4915204
  60.4 2.1 %copy-start.1 = (bf16[1280,640]{1,0:T(8,128)(2,1)S(1)}, bf16[1280,640]{1,0:T(8,128)(2,1)}, u32[]{:S(2)}) copy-start(bf16[1280,640]{1,0:T(8,128)(2,1)} %reduce_ref.1) | copy-start | bytes 4915204
  60.4 2.1 %copy-start.4 = (bf16[368,640]{1,0:T(8,128)(2,1)S(1)}, bf16[368,640]{1,0:T(8,128)(2,1)}, u32[]{:S(2)}) copy-start(bf16[368,640]{1,0:T(8,128)(2,1)} %copy-done.3) | copy-start | bytes 1413124

commit v4 on v3

--- a/solution.py
+++ b/solution.py
@@ -297,12 +297,13 @@
 def spectral_body(
     lat_count, columns, share, width,
     parity_ref, own_ref, other_any, gain_ref, tap_ref, legendre_ref, table_ref, out_ref,
-    field_ref, first_ref, modes_ref, other_ref, sem,
+    field_ref, exact_ref, west_ref, east_ref, first_ref, modes_ref, other_ref, sem,
 ):
     lat_total = 2 * lat_count
     north = lat_total // 2
     sectors = 2 * columns
     edge = width - LANES
+    span = 2 * LANES
     orders = legendre_ref.shape[2]
     parity = parity_ref[0]
     arrival = pltpu.make_async_copy(other_any, other_ref, sem)
@@ -315,17 +316,40 @@
             for band in range(lat_count):
                 block = source[column * lat_count + band].astype(jnp.float32)
                 rest = block[2 * share :]
-                field_ref[sector, 2 * band, :, 0:LANES] = block[:share]
-                field_ref[sector, 2 * band, :, LANES:] = rest
-                field_ref[sector, 2 * band + 1, :, 0:LANES] = block[share : 2 * share]
-                field_ref[sector, 2 * band + 1, :, LANES:] = pltpu.roll(rest, LANES - edge, axis=1)
-
-    lane = lax.broadcasted_iota(jnp.int32, (8, LANES), 1)
-
-    def filter_sector(sector, unused):
+                high = jnp.concatenate([rest, pltpu.roll(rest, LANES - edge, axis=1)], axis=0)
+                whole = jnp.concatenate([block[: 2 * share], high], axis=1)
+                rows = slice(2 * band * share, 2 * (band + 1) * share)
+                exact_ref[sector, rows, :] = whole.astype(jnp.bfloat16)
+                field_ref[sector, 2 * band] = whole[:share]
+                field_ref[sector, 2 * band + 1] = whole[share:]
+
+    took = lax.broadcasted_iota(jnp.int32, (2 * span, 2 * span), 0)
+    gave = lax.broadcasted_iota(jnp.int32, (2 * span, 2 * span), 1)
+    one, zero = jnp.float32(1.0), jnp.float32(0.0)
+    picks = jnp.where((took + 1 == gave) & (took < span - 1), one, zero)
+    picks = jnp.where((took == span + edge - 1) & (gave == 0), one, picks)
+    picks = jnp.where((took + span - 1 == gave) & (took > 0) & (took < width), one, picks)
+    picks = jnp.where((took == span + LANES) & (gave == span + width - 1), one, picks)
+    picks = picks.astype(jnp.bfloat16)
+
+    def shift_sector(sector, unused):
         after = lax.rem(sector + 1, sectors)
         before = lax.rem(sector + sectors - 1, sectors)
-
+        beside = jnp.dot(
+            jnp.concatenate(
+                [exact_ref[sector], exact_ref[before, :, LANES:], exact_ref[after, :, :LANES]],
+                axis=1,
+            ),
+            picks,
+            preferred_element_type=jnp.float32,
+        )
+        west_ref[sector] = beside[:, :span].reshape(lat_total, share, span)
+        east_ref[sector] = beside[:, span:].reshape(lat_total, share, span)
+        return unused
+
+    lax.fori_loop(0, sectors, shift_sector, 0)
+
+    def filter_sector(sector, unused):
         def filter_rows(tile, unused):
             rows = pl.ds(pl.multiple_of(tile * 8, 8), 8)
             taps = []
@@ -338,14 +362,9 @@
                 first_ref[sector, pl.ds(pl.multiple_of(t * share + tile * 8, 8), 8), :] = value + gelu(sum_)
 
             for t in range(lat_total):
-                low = field_ref[sector, t, rows, 0:LANES]
-                high = field_ref[sector, t, rows, LANES:]
-                right = pltpu.roll(field_ref[after, t, rows, 0:LANES], edge, axis=1)
-                left = pltpu.roll(field_ref[before, t, rows, LANES:], LANES - edge, axis=1)
-                high = jnp.where(lane == edge, right, jnp.where(lane == LANES - 1, left, high))
-                value = jnp.concatenate([low, high], axis=1)
-                west = pltpu.roll(value, 1, axis=1)
-                east = pltpu.roll(value, 2 * LANES - 1, axis=1)
+                value = field_ref[sector, t, rows, :]
+                west = west_ref[sector, t, rows, :]
+                east = east_ref[sector, t, rows, :]
 
                 def weigh(row):
                     return (
@@ -552,6 +571,8 @@
     own_mix = spectral_weight.transpose(0, 2, 1)
     held = own_mix.shape[1]
 
+    across_mix = lax.ppermute(own_mix, "x", [(i, 1 - i) for i in range(columns)])
+    across_mix, spectral_gain = lax.optimization_barrier((across_mix, spectral_gain))
     blocks = held // share
     piece = lax.dynamic_slice_in_dim(
         spectral_gain, (lat_at % blocks) * share, share, axis=2
@@ -576,7 +597,6 @@
     analysis = own_part(analysis_constant(sectors, width, span, M), core)
     table = own_part(synthesis_constant(sectors, width, padded, M), 2 * column + core)
 
-    across_mix = lax.ppermute(own_mix, "x", [(i, 1 - i) for i in range(columns)])
     own, across_mix = lax.optimization_barrier((own, across_mix))
     other = lax.ppermute(own, "core", swap)
     above = lax.ppermute(grid_first[1], "lat", [(i, i + 1) for i in range(lat_count - 1)])
@@ -590,13 +610,16 @@
         out_specs=in_vmem(1)[0],
         scratch_shapes=[
             pltpu.VMEM((sectors, lat_total, share, span), jnp.float32),
+            pltpu.VMEM((sectors, lat_total * share, span), jnp.bfloat16),
+            pltpu.VMEM((sectors, lat_total, share, span), jnp.float32),
+            pltpu.VMEM((sectors, lat_total, share, span), jnp.float32),
             pltpu.VMEM((sectors, lat_total * share, span), jnp.float32),
             pltpu.VMEM((lat_total * share, M), jnp.float32),
             pltpu.VMEM(own.shape, jnp.bfloat16),
             pltpu.SemaphoreType.DMA,
         ],
         cost_estimate=pl.CostEstimate(flops=9 * 10**9, bytes_accessed=0, transcendentals=0),
-        compiler_params=pltpu.CompilerParams(vmem_limit_bytes=20 << 20),
+        compiler_params=pltpu.CompilerParams(vmem_limit_bytes=28 << 20),
         name="spectral",
     )(core[None], own, other, gain_rows, taps, legendre, analysis)
     bands, above, below, across_mix = lax.optimization_barrier((bands, above, below, across_mix))

time: 67.4 us -> 65.3 us (0.969)
  waiting for transfers between devices: 20.1 us -> 18.9 us
    all_to_all x1, waiting for transfers between devices: 5.84 us -> 4.66 us  [chip_shards(): lax.all_to_all(packed, over_chips, split_axis=0, concat_axis=0, tiled=True)]
  transfers between devices with their start and end apart: 12 -> 12, of which waited for: 6 -> 6; matrix products, arithmetic and copies ran while one was open for 11% -> 12% of each run, Pallas kernels for 16% -> 16%
where the time goes in v4:
time: 65.3 us; the launch traced here: 64.7 us
  starting transfers between devices  20.3 us (31%)
  waiting for transfers between devices  18.9 us (29%)
  Pallas kernels  14.6 us (22%)
  local copies, waits for them, and re-layouts  9.54 us (15%)
  other arithmetic  0.98 us (2%)
    all_to_all x1, waiting for transfers between devices, chip_shards(): lax.all_to_all(bands.reshape(chips, share, 2 * M), over_chips, split_axis...  11.4 us
    pallas_call x1, Pallas kernels, chip_shards(): pl.pallas_call(functools.partial(spectral_body, lat_count, columns, share...  7.72 us
    all_to_all x1, starting transfers between devices, chip_shards(): lax.all_to_all(packed, over_chips, split_axis=0, concat_axis=0, tiled=True)  5.94 us
    all_to_all x1, waiting for transfers between devices, chip_shards(): lax.all_to_all(packed, over_chips, split_axis=0, concat_axis=0, tiled=True)  4.66 us
    all_to_all x1, starting transfers between devices, chip_shards(): lax.all_to_all(bands.reshape(chips, share, 2 * M), over_chips, split_axis...  4.06 us
    ppermute x1, starting transfers between devices, chip_shards(): lax.ppermute(grid_first[1], 'lat', [(i, i + 1) for i in range(lat_count -...  3.83 us
    pallas_call x1, Pallas kernels, chip_shards(): pl.pallas_call(functools.partial(finish_body, width, padded), out_shape=j...  3.22 us
    squeeze x3, local copies, waits for them, and re-layouts, own_part(): lax.dynamic_index_in_dim(jnp.asarray(constant), at, 0, keepdims=False)  3.18 us
  transfers between devices with their start and end apart: 12, of which 6 were waited for; matrix products, arithmetic and copies ran while one was open for 12% of the time, Pallas kernels for 16%

profile of v4, /device:TPU:0, one launch (start us, length us, event | category | flops | bytes accessed | tf_op | source)
XLA Modules:
  0.0 64.7 jit_solution(2130075797891505042)
XLA Ops:
  0.0 0.0 copy-start.2
  0.0 1.1 %copy.11.grid_ref = bf16[2,180,640]{2,1,0:T(8,128)(2,1)S(1)} copy(bf16[2,180,640]{2,0,1:T(2,128)(2,1)} %param.10) | data formatting | bytes 921600 | tf_op args[0]
  1.1 0.0 copy-start.6
  1.1 1.1 %pack.1 = bf16[16,120,128]{2,1,0:T(8,128)(2,1)} custom-call(bf16[2,180,640]{2,1,0:T(8,128)(2,1)S(1)} %copy.11.grid_ref), custom_call_target="tpu_custom_call" | custom-call | tf_op jit(solution)/shard_map/pack/pallas_call | solution.py:555
  2.3 0.0 copy-done.2
  2.3 2.9 %collective-permute-start = (bf16[2,160,640]{2,1,0:T(8,128)(2,1)S(1)}, bf16[2,160,640]{2,1,0:T(8,128)(2,1)S(1)}, u32[]{:S(2)}, u32[]{:S(2)}) collective-permute-start(bf16[2,160,640]{2,1,0:T(8,128)(2,1)S(1)} %bitcast.41), channel_id=1, source_target_pairs={{0,2},{2,0},{1,3},{3,1},{4,6},{6,4},{5,7},{7,5},{8,10},{10,8},{9,1... | collective-permute-start | bytes 1228808 | tf_op jit(solution)/shard_map/ppermute | solution.py:574
  5.2 0.0 collective-permute-start.7
  5.2 5.9 %all-to-all-start = ((bf16[16,120,128]{2,1,0:T(8,128)(2,1)}), bf16[16,120,128]{2,1,0:T(8,128)(2,1)S(1)}, u32[]{:S(2)}, u32[]{:S(2)}) async-start(bf16[16,120,128]{2,1,0:T(8,128)(2,1)} %pack.1), calls=%async_computation | async-start | bytes 983040 | tf_op jit(solution)/shard_map/all_to_all | solution.py:569
  11.2 0.7 %slice_bitcast_fusion = (bf16[180,640]{1,0:T(8,128)(2,1)S(1)}, bf16[180,640]{1,0:T(8,128)(2,1)}) fusion(bf16[2,180,640]{2,1,0:T(8,128)(2,1)S(1)} %copy.11.grid_ref), kind=kLoop, calls=%fused_computation.3 | loop fusion | bytes 921600 | tf_op jit(solution)/shard_map/squeeze | solution.py:603
  11.9 3.8 %collective-permute-start.3 = (bf16[180,640]{1,0:T(8,128)(2,1)}, bf16[180,640]{1,0:T(8,128)(2,1)S(1)}, u32[]{:S(2)}, u32[]{:S(2)}) collective-permute-start(bf16[180,640]{1,0:T(8,128)(2,1)} %get-tuple-element.46), channel_id=1, source_target_pairs={{0,4},{4,8},{8,12},{12,16},{16,20},{20,24},{24,28},{1,5},{5,9},{9,... | collective-permute-start | bytes 691208 | tf_op jit(solution)/shard_map/ppermute | solution.py:602
  15.7 1.3 %collective-permute-start.4 = (bf16[180,640]{1,0:T(8,128)(2,1)S(1)}, bf16[180,640]{1,0:T(8,128)(2,1)S(1)}, u32[]{:S(2)}, u32[]{:S(2)}) collective-permute-start(bf16[180,640]{1,0:T(8,128)(2,1)S(1)} %get-tuple-element.45), channel_id=1, source_target_pairs={{4,0},{8,4},{12,8},{16,12},{20,16},{24,20},{28,24},{5,1},{9,5},{13... | collective-permute-start | bytes 691208 | tf_op jit(solution)/shard_map/ppermute | solution.py:603
  17.1 0.0 copy-done.6
  17.1 1.1 %dynamic-slice_bitcast_fusion.table_ref = bf16[4,256,256]{2,1,0:T(8,128)(2,1)S(1)} fusion(bf16[2,4,256,256]{3,2,1,0:T(8,128)(2,1)} %constant.82.clone, s32[]{:T(128)S(6)} %select_n.76), kind=kLoop, calls=%fused_computation | loop fusion | bytes 1048580 | tf_op jit(solution)/shard_map/jit(dynamic_index_in_dim)/squeeze | solution.py:529
  18.2 0.1 constant_dynamic-slice_fusion
  18.3 1.1 %dynamic-slice_bitcast_fusion.1.legendre_ref = bf16[8,256,128]{2,1,0:T(8,128)(2,1)S(1)} fusion(bf16[2,8,256,128]{3,2,1,0:T(8,128)(2,1)} %constant.81.clone, s32[]{:T(128)S(6)} %select_n.76), kind=kLoop, calls=%fused_computation.1 | loop fusion | bytes 1048580 | tf_op jit(solution)/shard_map/jit(dynamic_index_in_dim)/squeeze | solution.py:529
  19.3 0.8 %slice_bitcast_fusion.5 = (bf16[1,640]{1,0:T(2,128)(2,1)S(1)}, bf16[1,640]{1,0:T(2,128)(2,1)S(1)}, bf16[1,640]{1,0:T(2,128)(2,1)S(1)}, bf16[1,640]{1,0:T(2,128)(2,1)S(1)}) fusion(bf16[2,180,640]{2,0,1:T(2,128)(2,1)} %param.10), kind=kLoop, calls=%fused_computation.17 | loop fusion | bytes 10240 | tf_op jit(solution)/shard_map/slice | solution.py:634
  20.1 0.0 collective-permute-done.mix_c_ref
  20.1 1.5 %dynamic-slice_bitcast_fusion.3 = bf16[2,40,256]{2,1,0:T(8,128)(2,1)} fusion(f32[2,256,160]{1,2,0:T(8,128)} %param.12, s32[]{:T(128)S(6)} %select_n.69), kind=kLoop, calls=%fused_computation.6 | loop fusion | bytes 81924 | tf_op jit(solution)/shard_map/transpose | solution.py:579
  21.6 0.0 collective-permute-start.2
  21.7 4.7 %all-to-all-done.own_ref = bf16[16,120,128]{2,1,0:T(8,128)(2,1)S(1)} async-done(((bf16[16,120,128]{2,1,0:T(8,128)(2,1)}), bf16[16,120,128]{2,1,0:T(8,128)(2,1)S(1)}, u32[]{:S(2)}, u32[]{:S(2)}) %all-to-all-start) | async-done | bytes 491552 | tf_op jit(solution)/shard_map/all_to_all | solution.py:569
  26.3 0.0 collective-permute-start.1
  26.3 0.0 collective-permute-done.2
  26.3 0.9 %broadcast_select_fusion = bf16[2,40,256]{2,1,0:T(8,128)(2,1)S(1)} fusion(bf16[2,40,256]{2,1,0:T(8,128)(2,1)} %collective-permute-done.2, pred[]{:T(512)S(6)} %eq.22, f32[2,256,160]{1,2,0:T(8,128)} %param.12, s32[]{:T(128)S(6)} %select_n.69), kind=kLoop, calls=%fused_computation.13 | loop fusion | flops 20480 | bytes 122885 | tf_op jit(solution)/shard_map/jit(_where)/select_n | solution.py:581
  27.3 0.9 %collective-permute-done.1.other_any = bf16[16,120,128]{2,1,0:T(8,128)(2,1)S(1)} collective-permute-done((bf16[16,120,128]{2,1,0:T(8,128)(2,1)S(1)}, bf16[16,120,128]{2,1,0:T(8,128)(2,1)S(1)}, u32[]{:S(2)}, u32[]{:S(2)}) %collective-permute-start.1) | collective-permute-done | bytes 491552 | tf_op jit(solution)/shard_map/ppermute | solution.py:601
  28.2 0.1 broadcast_in_dim.54.tap_ref
  28.3 7.7 %spectral.1 = bf16[2,8,40,512]{3,2,1,0:T(8,128)(2,1)} custom-call(s32[1]{0:T(128)} %bitcast.1.parity_ref, bf16[16,120,128]{2,1,0:T(8,128)(2,1)S(1)} %all-to-all-done.own_ref, bf16[16,120,128]{2,1,0:T(8,128)(2,1)S(1)} %collective-permute-done.1.other_any, bf16[160,256]{1,0:T(8,128)(2,1)S(1)} %pad_maximum_fusion.gain_ref, ...), custom_call_target="tpu_custom_call" | custom-call | flops 8999999488 | tf_op jit(solution)/shard_map/spectral/pallas_call | solution.py:605
  36.0 0.0 copy-start.5
  36.1 0.0 copy-start.7
  36.1 0.0 collective-permute-done.3.above_ref
  36.1 0.0 collective-permute-done.4.below_ref
  36.1 4.1 %all-to-all-start.1 = ((bf16[16,40,512]{2,1,0:T(8,128)(2,1)}), bf16[16,40,512]{2,1,0:T(8,128)(2,1)S(1)}, u32[]{:S(2)}, u32[]{:S(2)}) async-start(bf16[16,40,512]{2,1,0:T(8,128)(2,1)} %bitcast.10), calls=%async_computation.1 | async-start | bytes 1310720 | tf_op jit(solution)/shard_map/all_to_all | solution.py:649
  40.2 1.2 %collective-permute-start.6 = (bf16[4,640]{1,0:T(4,128)(2,1)S(1)}, bf16[4,640]{1,0:T(4,128)(2,1)S(1)}, u32[]{:S(2)}, u32[]{:S(2)}) collective-permute-start(bf16[4,640]{1,0:T(4,128)(2,1)S(1)} %pad_maximum_fusion.2), channel_id=1, source_target_pairs={{1,0},{2,1},{3,2},{0,3},{5,4},{6,5},{7,6},{4,7},{9,8},{10,9},{11,1... | collective-permute-start | bytes 15368 | tf_op jit(solution)/shard_map/ppermute | solution.py:633
  41.4 0.1 collective-permute-start.5
  41.4 1.0 %dynamic-slice_bitcast_fusion.2.table_ref = bf16[2,368,256]{2,1,0:T(8,128)(2,1)S(1)} fusion(bf16[4,2,368,256]{3,2,1,0:T(8,128)(2,1)} %constant.83.clone, s32[]{:T(128)S(6)} %select_n.77), kind=kLoop, calls=%fused_computation.2 | loop fusion | bytes 753668 | tf_op jit(solution)/shard_map/jit(dynamic_index_in_dim)/squeeze | solution.py:529
  42.5 0.0 copy-done.5
  42.5 0.1 copy.14.grid_ref
  42.5 0.0 copy-done.7
  42.6 1.0 %collective-permute-start.8 = (bf16[2,160,640]{2,1,0:T(8,128)(2,1)S(1)}, bf16[2,160,640]{2,1,0:T(8,128)(2,1)S(1)}, u32[]{:S(2)}, u32[]{:S(2)}) collective-permute-start(bf16[2,160,640]{2,1,0:T(8,128)(2,1)S(1)} %collective-permute-done.mix_c_ref), channel_id=1, source_target_pairs={{0,1},{1,0},{2,3},{3,2},{4,5},{5,4},{6,7},{7,6},{8,9},{9,8},{10,11... | collective-permute-start | bytes 1228808 | tf_op jit(solution)/shard_map/ppermute | solution.py:627
  43.6 0.1 collective-permute-done.6.east_ref
  43.7 0.8 %collective-permute-done.5.west_ref = bf16[4,640]{1,0:T(4,128)(2,1)S(1)} collective-permute-done((bf16[4,640]{1,0:T(4,128)(2,1)S(1)}, bf16[4,640]{1,0:T(4,128)(2,1)S(1)}, u32[]{:S(2)}, u32[]{:S(2)}) %collective-permute-start.5) | collective-permute-done | bytes 5152 | tf_op jit(solution)/shard_map/ppermute | solution.py:630
  44.5 1.5 %local.1 = (bf16[368,640]{1,0:T(8,128)(2,1)S(1)}, f32[8,128]{1,0:T(8,128)S(1)}) custom-call(bf16[180,640]{1,0:T(8,128)(2,1)S(1)} %collective-permute-done.3.above_ref, bf16[2,180,640]{2,1,0:T(8,128)(2,1)S(1)} %copy.14.grid_ref, bf16[180,640]{1,0:T(8,128)(2,1)S(1)} %collective-permute-done.4.below_ref, bf16[4,640]{1,0:T(4,128)(2,1)S(1)} %collective-permute-done.5.west_ref, ...), custom_call_target="tpu_custom_call" | custom-call | flops 8000000000 | tf_op jit(solution)/shard_map/local/pallas_call | solution.py:636
  46.0 0.0 copy-start.3
  46.0 0.8 %copy-done.3 = bf16[368,640]{1,0:T(8,128)(2,1)} copy-done((bf16[368,640]{1,0:T(8,128)(2,1)}, bf16[368,640]{1,0:T(8,128)(2,1)S(1)}, u32[]{:S(2)}) %copy-start.3) | copy-done | bytes 471064
  46.8 11.4 %all-to-all-done.1 = bf16[16,40,512]{2,1,0:T(8,128)(2,1)S(1)} async-done(((bf16[16,40,512]{2,1,0:T(8,128)(2,1)}), bf16[16,40,512]{2,1,0:T(8,128)(2,1)S(1)}, u32[]{:S(2)}, u32[]{:S(2)}) %all-to-all-start.1) | async-done | bytes 655392 | tf_op jit(solution)/shard_map/all_to_all | solution.py:649
  58.2 0.0 collective-permute-start.9
  58.2 0.0 collective-permute-done.7.mix_b_ref
  58.2 0.0 collective-permute-done.8.mix_d_ref
  58.2 0.0 copy-start
  58.2 0.0 copy-start.1
  58.2 0.0 copy-start.4
  58.2 1.0 %stage.1 = (f32[2,368,640]{2,1,0:T(8,128)S(1)}, bf16[2,640,640]{2,1,0:T(8,128)(2,1)S(1)}) custom-call(s32[1]{0:T(128)} %bitcast.place_ref, bf16[640,512]{1,0:T(8,128)(2,1)S(1)} %bitcast.40, bf16[2,368,256]{2,1,0:T(8,128)(2,1)S(1)} %dynamic-slice_bitcast_fusion.2.table_ref, bf16[2,160,640]{2,1,0:T(8,128)(2,1)S(1)} %bitcast.43, ...), custom_call_target="tpu_custom_call" | custom-call | flops 12000000000 | tf_op jit(solution)/shard_map/stage/pallas_call | solution.py:655
  59.3 1.0 %collective-permute-done.9.other_ref = bf16[640,512]{1,0:T(8,128)(2,1)S(1)} collective-permute-done((bf16[640,512]{1,0:T(8,128)(2,1)S(1)}, bf16[640,512]{1,0:T(8,128)(2,1)S(1)}, u32[]{:S(2)}, u32[]{:S(2)}) %collective-permute-start.9) | collective-permute-done | bytes 655392 | tf_op jit(solution)/shard_map/ppermute | solution.py:653
  60.3 0.0 copy-done
  60.3 0.0 copy-done.1
  60.3 0.0 copy-done.4
  60.3 3.2 %finish.1 = bf16[2,180,640]{2,1,0:T(8,128)(2,1)S(1)} custom-call(f32[2,368,640]{2,1,0:T(8,128)S(1)} %get-tuple-element.41.field_ref, bf16[640,512]{1,0:T(8,128)(2,1)S(1)} %collective-permute-done.9.other_ref, bf16[368,640]{1,0:T(8,128)(2,1)S(1)} %copy-done.4, f32[1,640]{1,0:T(1,128)S(1)} %broadcast_in_dim.55.gain_ref, ...), custom_call_target="tpu_custom_call" | custom-call | flops 3000000000 | tf_op jit(solution)/shard_map/finish/pallas_call | solution.py:672
  63.5 1.1 %copy.15 = bf16[2,180,640]{2,0,1:T(2,128)(2,1)} copy(bf16[2,180,640]{2,1,0:T(8,128)(2,1)S(1)} %finish.1) | data formatting | bytes 921600 | tf_op jit(solution)/shard_map/finish/pallas_call | solution.py:672
  (8 shorter events, 0.1 us)
Async XLA Ops:
  0.0 2.3 %copy-start.2 = (bf16[2,640,160]{1,2,0:T(8,128)(2,1)S(1)}, bf16[2,640,160]{1,2,0:T(8,128)(2,1)}, u32[]{:S(2)}) copy-start(bf16[2,640,160]{1,2,0:T(8,128)(2,1)} %param.13) | copy-start | bytes 1228804
  1.1 15.9 %copy-start.6 = (f32[3,3,640]{2,1,0:T(4,128)S(1)}, f32[3,3,640]{2,1,0:T(4,128)}, u32[]{:S(2)}) copy-start(f32[3,3,640]{2,1,0:T(4,128)} %param.11) | copy-start | bytes 69124
  2.3 17.9 %collective-permute-start = (bf16[2,160,640]{2,1,0:T(8,128)(2,1)S(1)}, bf16[2,160,640]{2,1,0:T(8,128)(2,1)S(1)}, u32[]{:S(2)}, u32[]{:S(2)}) collective-permute-start(bf16[2,160,640]{2,1,0:T(8,128)(2,1)S(1)} %bitcast.41), channel_id=1, source_target_pairs={{0,2},{2,0},{1,3},{3,1},{4,6},{6,4},{5,7},{7,5},{8,10},{10,8},{9,1... | collective-permute-start | bytes 1228808 | tf_op jit(solution)/shard_map/ppermute | solution.py:574
  5.2 53.0 %collective-permute-start.7 = (bf16[2,160,640]{2,1,0:T(8,128)(2,1)S(1)}, bf16[2,160,640]{2,1,0:T(8,128)(2,1)S(1)}, u32[]{:S(2)}, u32[]{:S(2)}) collective-permute-start(bf16[2,160,640]{2,1,0:T(8,128)(2,1)S(1)} %bitcast.42), channel_id=1, source_target_pairs={{0,1},{1,0},{2,3},{3,2},{4,5},{5,4},{6,7},{7,6},{8,9},{9,8},{10,11... | collective-permute-start | bytes 1228808 | tf_op jit(solution)/shard_map/ppermute | solution.py:626
  5.2 21.1 %all-to-all-start = ((bf16[16,120,128]{2,1,0:T(8,128)(2,1)}), bf16[16,120,128]{2,1,0:T(8,128)(2,1)S(1)}, u32[]{:S(2)}, u32[]{:S(2)}) async-start(bf16[16,120,128]{2,1,0:T(8,128)(2,1)} %pack.1), calls=%async_computation | async-start | bytes 983040 | tf_op jit(solution)/shard_map/all_to_all | solution.py:569
  11.9 24.2 %collective-permute-start.3 = (bf16[180,640]{1,0:T(8,128)(2,1)}, bf16[180,640]{1,0:T(8,128)(2,1)S(1)}, u32[]{:S(2)}, u32[]{:S(2)}) collective-permute-start(bf16[180,640]{1,0:T(8,128)(2,1)} %get-tuple-element.46), channel_id=1, source_target_pairs={{0,4},{4,8},{8,12},{12,16},{16,20},{20,24},{24,28},{1,5},{5,9},{9,... | collective-permute-start | bytes 691208 | tf_op jit(solution)/shard_map/ppermute | solution.py:602
  15.7 20.3 %collective-permute-start.4 = (bf16[180,640]{1,0:T(8,128)(2,1)S(1)}, bf16[180,640]{1,0:T(8,128)(2,1)S(1)}, u32[]{:S(2)}, u32[]{:S(2)}) collective-permute-start(bf16[180,640]{1,0:T(8,128)(2,1)S(1)} %get-tuple-element.45), channel_id=1, source_target_pairs={{4,0},{8,4},{12,8},{16,12},{20,16},{24,20},{28,24},{5,1},{9,5},{13... | collective-permute-start | bytes 691208 | tf_op jit(solution)/shard_map/ppermute | solution.py:603
  21.6 4.7 %collective-permute-start.2 = (bf16[2,40,256]{2,1,0:T(8,128)(2,1)}, bf16[2,40,256]{2,1,0:T(8,128)(2,1)}, u32[]{:S(2)}, u32[]{:S(2)}) collective-permute-start(bf16[2,40,256]{2,1,0:T(8,128)(2,1)} %dynamic-slice_bitcast_fusion.3), channel_id=1, source_target_pairs={{0,1},{1,0},{2,3},{3,2},{4,5},{5,4},{6,7},{7,6},{8,9},{9,8},{10,11... | collective-permute-start | bytes 122888 | tf_op jit(solution)/shard_map/ppermute | solution.py:580
  26.3 1.9 %collective-permute-start.1 = (bf16[16,120,128]{2,1,0:T(8,128)(2,1)S(1)}, bf16[16,120,128]{2,1,0:T(8,128)(2,1)S(1)}, u32[]{:S(2)}, u32[]{:S(2)}) collective-permute-start(bf16[16,120,128]{2,1,0:T(8,128)(2,1)S(1)} %all-to-all-done.own_ref), channel_id=1, source_target_pairs={{0,1},{1,0},{2,3},{3,2},{4,5},{5,4},{6,7},{7,6},{8,9},{9,8},{10,11... | collective-permute-start | bytes 1474568 | tf_op jit(solution)/shard_map/ppermute | solution.py:601
  36.0 6.4 %copy-start.5 = (bf16[2,180,640]{2,0,1:T(2,128)(2,1)S(1)}, bf16[2,180,640]{2,0,1:T(2,128)(2,1)}, u32[]{:S(2)}) copy-start(bf16[2,180,640]{2,0,1:T(2,128)(2,1)} %param.10) | copy-start | bytes 1382404
  36.1 6.5 %copy-start.7 = (f32[640]{0:T(1024)S(1)}, f32[640]{0:T(1024)}, u32[]{:S(2)}) copy-start(f32[640]{0:T(1024)} %param.14) | copy-start | bytes 7684
  36.1 22.1 %all-to-all-start.1 = ((bf16[16,40,512]{2,1,0:T(8,128)(2,1)}), bf16[16,40,512]{2,1,0:T(8,128)(2,1)S(1)}, u32[]{:S(2)}, u32[]{:S(2)}) async-start(bf16[16,40,512]{2,1,0:T(8,128)(2,1)} %bitcast.10), calls=%async_computation.1 | async-start | bytes 1310720 | tf_op jit(solution)/shard_map/all_to_all | solution.py:649
  40.2 3.5 %collective-permute-start.6 = (bf16[4,640]{1,0:T(4,128)(2,1)S(1)}, bf16[4,640]{1,0:T(4,128)(2,1)S(1)}, u32[]{:S(2)}, u32[]{:S(2)}) collective-permute-start(bf16[4,640]{1,0:T(4,128)(2,1)S(1)} %pad_maximum_fusion.2), channel_id=1, source_target_pairs={{1,0},{2,1},{3,2},{0,3},{5,4},{6,5},{7,6},{4,7},{9,8},{10,9},{11,1... | collective-permute-start | bytes 15368 | tf_op jit(solution)/shard_map/ppermute | solution.py:633
  41.4 3.1 %collective-permute-start.5 = (bf16[4,640]{1,0:T(4,128)(2,1)S(1)}, bf16[4,640]{1,0:T(4,128)(2,1)S(1)}, u32[]{:S(2)}, u32[]{:S(2)}) collective-permute-start(bf16[4,640]{1,0:T(4,128)(2,1)S(1)} %pad_maximum_fusion.1), channel_id=1, source_target_pairs={{0,1},{1,2},{2,3},{3,0},{4,5},{5,6},{6,7},{7,4},{8,9},{9,10},{10,1... | collective-permute-start | bytes 15368 | tf_op jit(solution)/shard_map/ppermute | solution.py:630
  42.6 15.6 %collective-permute-start.8 = (bf16[2,160,640]{2,1,0:T(8,128)(2,1)S(1)}, bf16[2,160,640]{2,1,0:T(8,128)(2,1)S(1)}, u32[]{:S(2)}, u32[]{:S(2)}) collective-permute-start(bf16[2,160,640]{2,1,0:T(8,128)(2,1)S(1)} %collective-permute-done.mix_c_ref), channel_id=1, source_target_pairs={{0,1},{1,0},{2,3},{3,2},{4,5},{5,4},{6,7},{7,6},{8,9},{9,8},{10,11... | collective-permute-start | bytes 1228808 | tf_op jit(solution)/shard_map/ppermute | solution.py:627
  46.0 0.8 %copy-start.3 = (bf16[368,640]{1,0:T(8,128)(2,1)}, bf16[368,640]{1,0:T(8,128)(2,1)S(1)}, u32[]{:S(2)}) copy-start(bf16[368,640]{1,0:T(8,128)(2,1)S(1)} %get-tuple-element.42.first_ref) | copy-start | bytes 1413124
  58.2 2.1 %collective-permute-start.9 = (bf16[640,512]{1,0:T(8,128)(2,1)S(1)}, bf16[640,512]{1,0:T(8,128)(2,1)S(1)}, u32[]{:S(2)}, u32[]{:S(2)}) collective-permute-start(bf16[640,512]{1,0:T(8,128)(2,1)S(1)} %bitcast.39), channel_id=1, source_target_pairs={{0,1},{1,0},{2,3},{3,2},{4,5},{5,4},{6,7},{7,6},{8,9},{9,8},{10,11... | collective-permute-start | bytes 1966088 | tf_op jit(solution)/shard_map/ppermute | solution.py:653
  58.2 2.1 %copy-start = (bf16[640,1280]{1,0:T(8,128)(2,1)S(1)}, bf16[640,1280]{1,0:T(8,128)(2,1)}, u32[]{:S(2)}) copy-start(bf16[640,1280]{1,0:T(8,128)(2,1)} %expand_ref.1) | copy-start | bytes 4915204
  58.2 2.1 %copy-start.1 = (bf16[1280,640]{1,0:T(8,128)(2,1)S(1)}, bf16[1280,640]{1,0:T(8,128)(2,1)}, u32[]{:S(2)}) copy-start(bf16[1280,640]{1,0:T(8,128)(2,1)} %reduce_ref.1) | copy-start | bytes 4915204
  58.2 2.1 %copy-start.4 = (bf16[368,640]{1,0:T(8,128)(2,1)S(1)}, bf16[368,640]{1,0:T(8,128)(2,1)}, u32[]{:S(2)}) copy-start(bf16[368,640]{1,0:T(8,128)(2,1)} %copy-done.3) | copy-start | bytes 1413124

commit v5 on v4

--- a/solution.py
+++ b/solution.py
@@ -296,8 +296,8 @@
 
 def spectral_body(
     lat_count, columns, share, width,
-    parity_ref, own_ref, other_any, gain_ref, tap_ref, legendre_ref, table_ref, out_ref,
-    field_ref, exact_ref, west_ref, east_ref, first_ref, modes_ref, other_ref, sem,
+    parity_ref, own_ref, other_ref, gain_ref, tap_ref, legendre_ref, table_ref, out_ref,
+    field_ref, exact_ref, west_ref, east_ref, first_ref, modes_ref,
 ):
     lat_total = 2 * lat_count
     north = lat_total // 2
@@ -306,11 +306,7 @@
     span = 2 * LANES
     orders = legendre_ref.shape[2]
     parity = parity_ref[0]
-    arrival = pltpu.make_async_copy(other_any, other_ref, sem)
-    arrival.start()
     for source, core in ((own_ref, parity), (other_ref, 1 - parity)):
-        if source is other_ref:
-            arrival.wait()
         for column in range(columns):
             sector = 2 * column + core
             for band in range(lat_count):
@@ -323,31 +319,39 @@
                 field_ref[sector, 2 * band] = whole[:share]
                 field_ref[sector, 2 * band + 1] = whole[share:]
 
-    took = lax.broadcasted_iota(jnp.int32, (2 * span, 2 * span), 0)
-    gave = lax.broadcasted_iota(jnp.int32, (2 * span, 2 * span), 1)
+    took = lax.broadcasted_iota(jnp.int32, (span, span), 0)
+    gave = lax.broadcasted_iota(jnp.int32, (span, span), 1)
     one, zero = jnp.float32(1.0), jnp.float32(0.0)
-    picks = jnp.where((took + 1 == gave) & (took < span - 1), one, zero)
-    picks = jnp.where((took == span + edge - 1) & (gave == 0), one, picks)
-    picks = jnp.where((took + span - 1 == gave) & (took > 0) & (took < width), one, picks)
-    picks = jnp.where((took == span + LANES) & (gave == span + width - 1), one, picks)
-    picks = picks.astype(jnp.bfloat16)
-
-    def shift_sector(sector, unused):
-        after = lax.rem(sector + 1, sectors)
-        before = lax.rem(sector + sectors - 1, sectors)
-        beside = jnp.dot(
-            jnp.concatenate(
-                [exact_ref[sector], exact_ref[before, :, LANES:], exact_ref[after, :, :LANES]],
-                axis=1,
-            ),
-            picks,
-            preferred_element_type=jnp.float32,
-        )
-        west_ref[sector] = beside[:, :span].reshape(lat_total, share, span)
-        east_ref[sector] = beside[:, span:].reshape(lat_total, share, span)
-        return unused
-
-    lax.fori_loop(0, sectors, shift_sector, 0)
+
+    inner = jnp.where((took + 1 == gave + LANES) & (gave < LANES), one, zero)
+    inner = jnp.where((took == gave - LANES + 1) & (gave >= LANES), one, inner)
+    inner = inner.astype(jnp.bfloat16)
+    to_west = jnp.where((took == gave + LANES - 1) & (gave > 0), one, zero)
+    to_west = jnp.where((took == edge - 1) & (gave == 0), one, to_west)
+    to_west = to_west[:, :LANES].astype(jnp.bfloat16)
+    to_east = jnp.where((took == gave + 1) & (gave < edge - 1), one, zero)
+    to_east = jnp.where((took == LANES) & (gave == edge - 1), one, to_east)
+    to_east = to_east[:, :LANES].astype(jnp.bfloat16)
+
+    def spread(value):
+        return value.reshape(lat_total, share, LANES)
+
+    for sector in range(sectors):
+        middle = jnp.dot(exact_ref[sector], inner, preferred_element_type=jnp.float32)
+        west_ref[sector, :, :, LANES:] = spread(middle[:, :LANES])
+        east_ref[sector, :, :, :LANES] = spread(middle[:, LANES:])
+        before = jnp.concatenate(
+            [exact_ref[(sector - 1) % sectors, :, LANES:], exact_ref[sector, :, :LANES]], axis=1
+        )
+        west_ref[sector, :, :, :LANES] = spread(
+            jnp.dot(before, to_west, preferred_element_type=jnp.float32)
+        )
+        after = jnp.concatenate(
+            [exact_ref[sector, :, LANES:], exact_ref[(sector + 1) % sectors, :, :LANES]], axis=1
+        )
+        east_ref[sector, :, :, LANES:] = spread(
+            jnp.dot(after, to_east, preferred_element_type=jnp.float32)
+        )
 
     def filter_sector(sector, unused):
         def filter_rows(tile, unused):
@@ -605,8 +609,7 @@
     bands = pl.pallas_call(
         functools.partial(spectral_body, lat_count, columns, share, width),
         out_shape=jax.ShapeDtypeStruct((columns, lat_count, share, 2 * M), jnp.bfloat16),
-        in_specs=[pl.BlockSpec(memory_space=pltpu.SMEM)]
-        + in_vmem(1) + in_hbm(1) + in_vmem(4),
+        in_specs=[pl.BlockSpec(memory_space=pltpu.SMEM)] + in_vmem(6),
         out_specs=in_vmem(1)[0],
         scratch_shapes=[
             pltpu.VMEM((sectors, lat_total, share, span), jnp.float32),
@@ -615,8 +618,6 @@
             pltpu.VMEM((sectors, lat_total, share, span), jnp.float32),
             pltpu.VMEM((sectors, lat_total * share, span), jnp.float32),
             pltpu.VMEM((lat_total * share, M), jnp.float32),
-            pltpu.VMEM(own.shape, jnp.bfloat16),
-            pltpu.SemaphoreType.DMA,
         ],
         cost_estimate=pl.CostEstimate(flops=9 * 10**9, bytes_accessed=0, transcendentals=0),
         compiler_params=pltpu.CompilerParams(vmem_limit_bytes=28 << 20),

time: 65.3 us -> 64 us (0.980)
  Pallas kernels: 14.6 us -> 13.4 us
    pallas_call x1, Pallas kernels: 7.72 us -> 6.46 us  [chip_shards(): pl.pallas_call(functools.partial(spectral_body, lat_count, columns, share...]
  transfers between devices with their start and end apart: 12 -> 12, of which waited for: 6 -> 6; matrix products, arithmetic and copies ran while one was open for 12% -> 12% of each run, Pallas kernels for 16% -> 14%
where the time goes in v5:
time: 64 us; the launch traced here: 63.4 us
  starting transfers between devices  20.3 us (32%)
  waiting for transfers between devices  18.9 us (30%)
  Pallas kernels  13.4 us (21%)
  local copies, waits for them, and re-layouts  9.54 us (15%)
  other arithmetic  0.98 us (2%)
    all_to_all x1, waiting for transfers between devices, chip_shards(): lax.all_to_all(bands.reshape(chips, share, 2 * M), over_chips, split_axis...  11.4 us
    pallas_call x1, Pallas kernels, chip_shards(): pl.pallas_call(functools.partial(spectral_body, lat_count, columns, share...  6.46 us
    all_to_all x1, starting transfers between devices, chip_shards(): lax.all_to_all(packed, over_chips, split_axis=0, concat_axis=0, tiled=True)  5.94 us
    all_to_all x1, waiting for transfers between devices, chip_shards(): lax.all_to_all(packed, over_chips, split_axis=0, concat_axis=0, tiled=True)  4.66 us
    all_to_all x1, starting transfers between devices, chip_shards(): lax.all_to_all(bands.reshape(chips, share, 2 * M), over_chips, split_axis...  4.06 us
    ppermute x1, starting transfers between devices, chip_shards(): lax.ppermute(grid_first[1], 'lat', [(i, i + 1) for i in range(lat_count -...  3.83 us
    pallas_call x1, Pallas kernels, chip_shards(): pl.pallas_call(functools.partial(finish_body, width, padded), out_shape=j...  3.22 us
    squeeze x3, local copies, waits for them, and re-layouts, own_part(): lax.dynamic_index_in_dim(jnp.asarray(constant), at, 0, keepdims=False)  3.18 us
  transfers between devices with their start and end apart: 12, of which 6 were waited for; matrix products, arithmetic and copies ran while one was open for 12% of the time, Pallas kernels for 14%

profile of v5, /device:TPU:0, one launch (start us, length us, event | category | flops | bytes accessed | tf_op | source)
XLA Modules:
  0.0 63.4 jit_solution(9932221759071340766)
XLA Ops:
  0.0 0.0 copy-start.2
  0.0 1.1 %copy.11.grid_ref = bf16[2,180,640]{2,1,0:T(8,128)(2,1)S(1)} copy(bf16[2,180,640]{2,0,1:T(2,128)(2,1)} %param.10) | data formatting | bytes 921600 | tf_op args[0]
  1.1 0.0 copy-start.6
  1.1 1.1 %pack.1 = bf16[16,120,128]{2,1,0:T(8,128)(2,1)} custom-call(bf16[2,180,640]{2,1,0:T(8,128)(2,1)S(1)} %copy.11.grid_ref), custom_call_target="tpu_custom_call" | custom-call | tf_op jit(solution)/shard_map/pack/pallas_call | solution.py:559
  2.3 0.0 copy-done.2
  2.3 2.9 %collective-permute-start = (bf16[2,160,640]{2,1,0:T(8,128)(2,1)S(1)}, bf16[2,160,640]{2,1,0:T(8,128)(2,1)S(1)}, u32[]{:S(2)}, u32[]{:S(2)}) collective-permute-start(bf16[2,160,640]{2,1,0:T(8,128)(2,1)S(1)} %bitcast.41), channel_id=1, source_target_pairs={{0,2},{2,0},{1,3},{3,1},{4,6},{6,4},{5,7},{7,5},{8,10},{10,8},{9,1... | collective-permute-start | bytes 1228808 | tf_op jit(solution)/shard_map/ppermute | solution.py:578
  5.2 0.0 collective-permute-start.7
  5.2 5.9 %all-to-all-start = ((bf16[16,120,128]{2,1,0:T(8,128)(2,1)}), bf16[16,120,128]{2,1,0:T(8,128)(2,1)S(1)}, u32[]{:S(2)}, u32[]{:S(2)}) async-start(bf16[16,120,128]{2,1,0:T(8,128)(2,1)} %pack.1), calls=%async_computation | async-start | bytes 983040 | tf_op jit(solution)/shard_map/all_to_all | solution.py:573
  11.2 0.7 %slice_bitcast_fusion = (bf16[180,640]{1,0:T(8,128)(2,1)S(1)}, bf16[180,640]{1,0:T(8,128)(2,1)}) fusion(bf16[2,180,640]{2,1,0:T(8,128)(2,1)S(1)} %copy.11.grid_ref), kind=kLoop, calls=%fused_computation.3 | loop fusion | bytes 921600 | tf_op jit(solution)/shard_map/squeeze | solution.py:607
  11.9 3.8 %collective-permute-start.3 = (bf16[180,640]{1,0:T(8,128)(2,1)}, bf16[180,640]{1,0:T(8,128)(2,1)S(1)}, u32[]{:S(2)}, u32[]{:S(2)}) collective-permute-start(bf16[180,640]{1,0:T(8,128)(2,1)} %get-tuple-element.46), channel_id=1, source_target_pairs={{0,4},{4,8},{8,12},{12,16},{16,20},{20,24},{24,28},{1,5},{5,9},{9,... | collective-permute-start | bytes 691208 | tf_op jit(solution)/shard_map/ppermute | solution.py:606
  15.7 1.3 %collective-permute-start.4 = (bf16[180,640]{1,0:T(8,128)(2,1)S(1)}, bf16[180,640]{1,0:T(8,128)(2,1)S(1)}, u32[]{:S(2)}, u32[]{:S(2)}) collective-permute-start(bf16[180,640]{1,0:T(8,128)(2,1)S(1)} %get-tuple-element.45), channel_id=1, source_target_pairs={{4,0},{8,4},{12,8},{16,12},{20,16},{24,20},{28,24},{5,1},{9,5},{13... | collective-permute-start | bytes 691208 | tf_op jit(solution)/shard_map/ppermute | solution.py:607
  17.1 0.0 copy-done.6
  17.1 1.1 %dynamic-slice_bitcast_fusion.table_ref = bf16[4,256,256]{2,1,0:T(8,128)(2,1)S(1)} fusion(bf16[2,4,256,256]{3,2,1,0:T(8,128)(2,1)} %constant.82.clone, s32[]{:T(128)S(6)} %select_n.76), kind=kLoop, calls=%fused_computation | loop fusion | bytes 1048580 | tf_op jit(solution)/shard_map/jit(dynamic_index_in_dim)/squeeze | solution.py:533
  18.2 0.1 constant_dynamic-slice_fusion
  18.3 1.1 %dynamic-slice_bitcast_fusion.1.legendre_ref = bf16[8,256,128]{2,1,0:T(8,128)(2,1)S(1)} fusion(bf16[2,8,256,128]{3,2,1,0:T(8,128)(2,1)} %constant.81.clone, s32[]{:T(128)S(6)} %select_n.76), kind=kLoop, calls=%fused_computation.1 | loop fusion | bytes 1048580 | tf_op jit(solution)/shard_map/jit(dynamic_index_in_dim)/squeeze | solution.py:533
  19.3 0.8 %slice_bitcast_fusion.5 = (bf16[1,640]{1,0:T(2,128)(2,1)S(1)}, bf16[1,640]{1,0:T(2,128)(2,1)S(1)}, bf16[1,640]{1,0:T(2,128)(2,1)S(1)}, bf16[1,640]{1,0:T(2,128)(2,1)S(1)}) fusion(bf16[2,180,640]{2,0,1:T(2,128)(2,1)} %param.10), kind=kLoop, calls=%fused_computation.17 | loop fusion | bytes 10240 | tf_op jit(solution)/shard_map/slice | solution.py:635
  20.1 0.0 collective-permute-done.mix_c_ref
  20.1 1.5 %dynamic-slice_bitcast_fusion.3 = bf16[2,40,256]{2,1,0:T(8,128)(2,1)} fusion(f32[2,256,160]{1,2,0:T(8,128)} %param.12, s32[]{:T(128)S(6)} %select_n.69), kind=kLoop, calls=%fused_computation.6 | loop fusion | bytes 81924 | tf_op jit(solution)/shard_map/transpose | solution.py:583
  21.6 0.0 collective-permute-start.2
  21.7 4.7 %all-to-all-done.own_ref = bf16[16,120,128]{2,1,0:T(8,128)(2,1)S(1)} async-done(((bf16[16,120,128]{2,1,0:T(8,128)(2,1)}), bf16[16,120,128]{2,1,0:T(8,128)(2,1)S(1)}, u32[]{:S(2)}, u32[]{:S(2)}) %all-to-all-start) | async-done | bytes 491552 | tf_op jit(solution)/shard_map/all_to_all | solution.py:573
  26.3 0.0 collective-permute-start.1
  26.3 0.0 collective-permute-done.2
  26.3 0.9 %broadcast_select_fusion = bf16[2,40,256]{2,1,0:T(8,128)(2,1)S(1)} fusion(bf16[2,40,256]{2,1,0:T(8,128)(2,1)} %collective-permute-done.2, pred[]{:T(512)S(6)} %eq.22, f32[2,256,160]{1,2,0:T(8,128)} %param.12, s32[]{:T(128)S(6)} %select_n.69), kind=kLoop, calls=%fused_computation.13 | loop fusion | flops 20480 | bytes 122885 | tf_op jit(solution)/shard_map/jit(_where)/select_n | solution.py:585
  27.3 0.9 %collective-permute-done.1.other_ref = bf16[16,120,128]{2,1,0:T(8,128)(2,1)S(1)} collective-permute-done((bf16[16,120,128]{2,1,0:T(8,128)(2,1)S(1)}, bf16[16,120,128]{2,1,0:T(8,128)(2,1)S(1)}, u32[]{:S(2)}, u32[]{:S(2)}) %collective-permute-start.1) | collective-permute-done | bytes 491552 | tf_op jit(solution)/shard_map/ppermute | solution.py:605
  28.2 0.1 broadcast_in_dim.54.tap_ref
  28.3 6.5 %spectral.1 = bf16[2,8,40,512]{3,2,1,0:T(8,128)(2,1)} custom-call(s32[1]{0:T(128)} %bitcast.1.parity_ref, bf16[16,120,128]{2,1,0:T(8,128)(2,1)S(1)} %all-to-all-done.own_ref, bf16[16,120,128]{2,1,0:T(8,128)(2,1)S(1)} %collective-permute-done.1.other_ref, bf16[160,256]{1,0:T(8,128)(2,1)S(1)} %pad_maximum_fusion.gain_ref, ...), custom_call_target="tpu_custom_call" | custom-call | flops 8999999488 | tf_op jit(solution)/shard_map/spectral/pallas_call | solution.py:609
  34.8 0.0 copy-start.5
  34.8 0.0 copy-start.7
  34.8 0.0 collective-permute-done.3.above_ref
  34.8 0.0 collective-permute-done.4.below_ref
  34.8 4.1 %all-to-all-start.1 = ((bf16[16,40,512]{2,1,0:T(8,128)(2,1)}), bf16[16,40,512]{2,1,0:T(8,128)(2,1)S(1)}, u32[]{:S(2)}, u32[]{:S(2)}) async-start(bf16[16,40,512]{2,1,0:T(8,128)(2,1)} %bitcast.10), calls=%async_computation.1 | async-start | bytes 1310720 | tf_op jit(solution)/shard_map/all_to_all | solution.py:650
  38.9 1.2 %collective-permute-start.6 = (bf16[4,640]{1,0:T(4,128)(2,1)S(1)}, bf16[4,640]{1,0:T(4,128)(2,1)S(1)}, u32[]{:S(2)}, u32[]{:S(2)}) collective-permute-start(bf16[4,640]{1,0:T(4,128)(2,1)S(1)} %pad_maximum_fusion.2), channel_id=1, source_target_pairs={{1,0},{2,1},{3,2},{0,3},{5,4},{6,5},{7,6},{4,7},{9,8},{10,9},{11,1... | collective-permute-start | bytes 15368 | tf_op jit(solution)/shard_map/ppermute | solution.py:634
  40.1 0.1 collective-permute-start.5
  40.2 1.0 %dynamic-slice_bitcast_fusion.2.table_ref = bf16[2,368,256]{2,1,0:T(8,128)(2,1)S(1)} fusion(bf16[4,2,368,256]{3,2,1,0:T(8,128)(2,1)} %constant.83.clone, s32[]{:T(128)S(6)} %select_n.77), kind=kLoop, calls=%fused_computation.2 | loop fusion | bytes 753668 | tf_op jit(solution)/shard_map/jit(dynamic_index_in_dim)/squeeze | solution.py:533
  41.2 0.0 copy-done.5
  41.2 0.1 copy.14.grid_ref
  41.2 0.0 copy-done.7
  41.3 1.0 %collective-permute-start.8 = (bf16[2,160,640]{2,1,0:T(8,128)(2,1)S(1)}, bf16[2,160,640]{2,1,0:T(8,128)(2,1)S(1)}, u32[]{:S(2)}, u32[]{:S(2)}) collective-permute-start(bf16[2,160,640]{2,1,0:T(8,128)(2,1)S(1)} %collective-permute-done.mix_c_ref), channel_id=1, source_target_pairs={{0,1},{1,0},{2,3},{3,2},{4,5},{5,4},{6,7},{7,6},{8,9},{9,8},{10,11... | collective-permute-start | bytes 1228808 | tf_op jit(solution)/shard_map/ppermute | solution.py:628
  42.3 0.1 collective-permute-done.6.east_ref
  42.4 0.8 %collective-permute-done.5.west_ref = bf16[4,640]{1,0:T(4,128)(2,1)S(1)} collective-permute-done((bf16[4,640]{1,0:T(4,128)(2,1)S(1)}, bf16[4,640]{1,0:T(4,128)(2,1)S(1)}, u32[]{:S(2)}, u32[]{:S(2)}) %collective-permute-start.5) | collective-permute-done | bytes 5152 | tf_op jit(solution)/shard_map/ppermute | solution.py:631
  43.2 1.5 %local.1 = (bf16[368,640]{1,0:T(8,128)(2,1)S(1)}, f32[8,128]{1,0:T(8,128)S(1)}) custom-call(bf16[180,640]{1,0:T(8,128)(2,1)S(1)} %collective-permute-done.3.above_ref, bf16[2,180,640]{2,1,0:T(8,128)(2,1)S(1)} %copy.14.grid_ref, bf16[180,640]{1,0:T(8,128)(2,1)S(1)} %collective-permute-done.4.below_ref, bf16[4,640]{1,0:T(4,128)(2,1)S(1)} %collective-permute-done.5.west_ref, ...), custom_call_target="tpu_custom_call" | custom-call | flops 8000000000 | tf_op jit(solution)/shard_map/local/pallas_call | solution.py:637
  44.7 0.0 copy-start.3
  44.7 0.8 %copy-done.3 = bf16[368,640]{1,0:T(8,128)(2,1)} copy-done((bf16[368,640]{1,0:T(8,128)(2,1)}, bf16[368,640]{1,0:T(8,128)(2,1)S(1)}, u32[]{:S(2)}) %copy-start.3) | copy-done | bytes 471064
  45.5 11.4 %all-to-all-done.1 = bf16[16,40,512]{2,1,0:T(8,128)(2,1)S(1)} async-done(((bf16[16,40,512]{2,1,0:T(8,128)(2,1)}), bf16[16,40,512]{2,1,0:T(8,128)(2,1)S(1)}, u32[]{:S(2)}, u32[]{:S(2)}) %all-to-all-start.1) | async-done | bytes 655392 | tf_op jit(solution)/shard_map/all_to_all | solution.py:650
  56.9 0.0 collective-permute-start.9
  56.9 0.0 collective-permute-done.7.mix_b_ref
  56.9 0.0 collective-permute-done.8.mix_d_ref
  56.9 0.0 copy-start
  56.9 0.0 copy-start.1
  56.9 0.0 copy-start.4
  56.9 1.0 %stage.1 = (f32[2,368,640]{2,1,0:T(8,128)S(1)}, bf16[2,640,640]{2,1,0:T(8,128)(2,1)S(1)}) custom-call(s32[1]{0:T(128)} %bitcast.place_ref, bf16[640,512]{1,0:T(8,128)(2,1)S(1)} %bitcast.40, bf16[2,368,256]{2,1,0:T(8,128)(2,1)S(1)} %dynamic-slice_bitcast_fusion.2.table_ref, bf16[2,160,640]{2,1,0:T(8,128)(2,1)S(1)} %bitcast.43, ...), custom_call_target="tpu_custom_call" | custom-call | flops 12000000000 | tf_op jit(solution)/shard_map/stage/pallas_call | solution.py:656
  58.0 1.0 %collective-permute-done.9.other_ref = bf16[640,512]{1,0:T(8,128)(2,1)S(1)} collective-permute-done((bf16[640,512]{1,0:T(8,128)(2,1)S(1)}, bf16[640,512]{1,0:T(8,128)(2,1)S(1)}, u32[]{:S(2)}, u32[]{:S(2)}) %collective-permute-start.9) | collective-permute-done | bytes 655392 | tf_op jit(solution)/shard_map/ppermute | solution.py:654
  59.0 0.0 copy-done
  59.0 0.0 copy-done.1
  59.0 0.0 copy-done.4
  59.0 3.2 %finish.1 = bf16[2,180,640]{2,1,0:T(8,128)(2,1)S(1)} custom-call(f32[2,368,640]{2,1,0:T(8,128)S(1)} %get-tuple-element.41.field_ref, bf16[640,512]{1,0:T(8,128)(2,1)S(1)} %collective-permute-done.9.other_ref, bf16[368,640]{1,0:T(8,128)(2,1)S(1)} %copy-done.4, f32[1,640]{1,0:T(1,128)S(1)} %broadcast_in_dim.55.gain_ref, ...), custom_call_target="tpu_custom_call" | custom-call | flops 3000000000 | tf_op jit(solution)/shard_map/finish/pallas_call | solution.py:673
  62.2 1.1 %copy.15 = bf16[2,180,640]{2,0,1:T(2,128)(2,1)} copy(bf16[2,180,640]{2,1,0:T(8,128)(2,1)S(1)} %finish.1) | data formatting | bytes 921600 | tf_op jit(solution)/shard_map/finish/pallas_call | solution.py:673
  (8 shorter events, 0.1 us)
Async XLA Ops:
  0.0 2.3 %copy-start.2 = (bf16[2,640,160]{1,2,0:T(8,128)(2,1)S(1)}, bf16[2,640,160]{1,2,0:T(8,128)(2,1)}, u32[]{:S(2)}) copy-start(bf16[2,640,160]{1,2,0:T(8,128)(2,1)} %param.13) | copy-start | bytes 1228804
  1.1 15.9 %copy-start.6 = (f32[3,3,640]{2,1,0:T(4,128)S(1)}, f32[3,3,640]{2,1,0:T(4,128)}, u32[]{:S(2)}) copy-start(f32[3,3,640]{2,1,0:T(4,128)} %param.11) | copy-start | bytes 69124
  2.3 17.9 %collective-permute-start = (bf16[2,160,640]{2,1,0:T(8,128)(2,1)S(1)}, bf16[2,160,640]{2,1,0:T(8,128)(2,1)S(1)}, u32[]{:S(2)}, u32[]{:S(2)}) collective-permute-start(bf16[2,160,640]{2,1,0:T(8,128)(2,1)S(1)} %bitcast.41), channel_id=1, source_target_pairs={{0,2},{2,0},{1,3},{3,1},{4,6},{6,4},{5,7},{7,5},{8,10},{10,8},{9,1... | collective-permute-start | bytes 1228808 | tf_op jit(solution)/shard_map/ppermute | solution.py:578
  5.2 51.7 %collective-permute-start.7 = (bf16[2,160,640]{2,1,0:T(8,128)(2,1)S(1)}, bf16[2,160,640]{2,1,0:T(8,128)(2,1)S(1)}, u32[]{:S(2)}, u32[]{:S(2)}) collective-permute-start(bf16[2,160,640]{2,1,0:T(8,128)(2,1)S(1)} %bitcast.42), channel_id=1, source_target_pairs={{0,1},{1,0},{2,3},{3,2},{4,5},{5,4},{6,7},{7,6},{8,9},{9,8},{10,11... | collective-permute-start | bytes 1228808 | tf_op jit(solution)/shard_map/ppermute | solution.py:627
  5.2 21.1 %all-to-all-start = ((bf16[16,120,128]{2,1,0:T(8,128)(2,1)}), bf16[16,120,128]{2,1,0:T(8,128)(2,1)S(1)}, u32[]{:S(2)}, u32[]{:S(2)}) async-start(bf16[16,120,128]{2,1,0:T(8,128)(2,1)} %pack.1), calls=%async_computation | async-start | bytes 983040 | tf_op jit(solution)/shard_map/all_to_all | solution.py:573
  11.9 22.9 %collective-permute-start.3 = (bf16[180,640]{1,0:T(8,128)(2,1)}, bf16[180,640]{1,0:T(8,128)(2,1)S(1)}, u32[]{:S(2)}, u32[]{:S(2)}) collective-permute-start(bf16[180,640]{1,0:T(8,128)(2,1)} %get-tuple-element.46), channel_id=1, source_target_pairs={{0,4},{4,8},{8,12},{12,16},{16,20},{20,24},{24,28},{1,5},{5,9},{9,... | collective-permute-start | bytes 691208 | tf_op jit(solution)/shard_map/ppermute | solution.py:606
  15.7 19.1 %collective-permute-start.4 = (bf16[180,640]{1,0:T(8,128)(2,1)S(1)}, bf16[180,640]{1,0:T(8,128)(2,1)S(1)}, u32[]{:S(2)}, u32[]{:S(2)}) collective-permute-start(bf16[180,640]{1,0:T(8,128)(2,1)S(1)} %get-tuple-element.45), channel_id=1, source_target_pairs={{4,0},{8,4},{12,8},{16,12},{20,16},{24,20},{28,24},{5,1},{9,5},{13... | collective-permute-start | bytes 691208 | tf_op jit(solution)/shard_map/ppermute | solution.py:607
  21.6 4.7 %collective-permute-start.2 = (bf16[2,40,256]{2,1,0:T(8,128)(2,1)}, bf16[2,40,256]{2,1,0:T(8,128)(2,1)}, u32[]{:S(2)}, u32[]{:S(2)}) collective-permute-start(bf16[2,40,256]{2,1,0:T(8,128)(2,1)} %dynamic-slice_bitcast_fusion.3), channel_id=1, source_target_pairs={{0,1},{1,0},{2,3},{3,2},{4,5},{5,4},{6,7},{7,6},{8,9},{9,8},{10,11... | collective-permute-start | bytes 122888 | tf_op jit(solution)/shard_map/ppermute | solution.py:584
  26.3 1.9 %collective-permute-start.1 = (bf16[16,120,128]{2,1,0:T(8,128)(2,1)S(1)}, bf16[16,120,128]{2,1,0:T(8,128)(2,1)S(1)}, u32[]{:S(2)}, u32[]{:S(2)}) collective-permute-start(bf16[16,120,128]{2,1,0:T(8,128)(2,1)S(1)} %all-to-all-done.own_ref), channel_id=1, source_target_pairs={{0,1},{1,0},{2,3},{3,2},{4,5},{5,4},{6,7},{7,6},{8,9},{9,8},{10,11... | collective-permute-start | bytes 1474568 | tf_op jit(solution)/shard_map/ppermute | solution.py:605
  34.8 6.4 %copy-start.5 = (bf16[2,180,640]{2,0,1:T(2,128)(2,1)S(1)}, bf16[2,180,640]{2,0,1:T(2,128)(2,1)}, u32[]{:S(2)}) copy-start(bf16[2,180,640]{2,0,1:T(2,128)(2,1)} %param.10) | copy-start | bytes 1382404
  34.8 6.5 %copy-start.7 = (f32[640]{0:T(1024)S(1)}, f32[640]{0:T(1024)}, u32[]{:S(2)}) copy-start(f32[640]{0:T(1024)} %param.14) | copy-start | bytes 7684
  34.8 22.1 %all-to-all-start.1 = ((bf16[16,40,512]{2,1,0:T(8,128)(2,1)}), bf16[16,40,512]{2,1,0:T(8,128)(2,1)S(1)}, u32[]{:S(2)}, u32[]{:S(2)}) async-start(bf16[16,40,512]{2,1,0:T(8,128)(2,1)} %bitcast.10), calls=%async_computation.1 | async-start | bytes 1310720 | tf_op jit(solution)/shard_map/all_to_all | solution.py:650
  38.9 3.5 %collective-permute-start.6 = (bf16[4,640]{1,0:T(4,128)(2,1)S(1)}, bf16[4,640]{1,0:T(4,128)(2,1)S(1)}, u32[]{:S(2)}, u32[]{:S(2)}) collective-permute-start(bf16[4,640]{1,0:T(4,128)(2,1)S(1)} %pad_maximum_fusion.2), channel_id=1, source_target_pairs={{1,0},{2,1},{3,2},{0,3},{5,4},{6,5},{7,6},{4,7},{9,8},{10,9},{11,1... | collective-permute-start | bytes 15368 | tf_op jit(solution)/shard_map/ppermute | solution.py:634
  40.1 3.1 %collective-permute-start.5 = (bf16[4,640]{1,0:T(4,128)(2,1)S(1)}, bf16[4,640]{1,0:T(4,128)(2,1)S(1)}, u32[]{:S(2)}, u32[]{:S(2)}) collective-permute-start(bf16[4,640]{1,0:T(4,128)(2,1)S(1)} %pad_maximum_fusion.1), channel_id=1, source_target_pairs={{0,1},{1,2},{2,3},{3,0},{4,5},{5,6},{6,7},{7,4},{8,9},{9,10},{10,1... | collective-permute-start | bytes 15368 | tf_op jit(solution)/shard_map/ppermute | solution.py:631
  41.3 15.6 %collective-permute-start.8 = (bf16[2,160,640]{2,1,0:T(8,128)(2,1)S(1)}, bf16[2,160,640]{2,1,0:T(8,128)(2,1)S(1)}, u32[]{:S(2)}, u32[]{:S(2)}) collective-permute-start(bf16[2,160,640]{2,1,0:T(8,128)(2,1)S(1)} %collective-permute-done.mix_c_ref), channel_id=1, source_target_pairs={{0,1},{1,0},{2,3},{3,2},{4,5},{5,4},{6,7},{7,6},{8,9},{9,8},{10,11... | collective-permute-start | bytes 1228808 | tf_op jit(solution)/shard_map/ppermute | solution.py:628
  44.7 0.8 %copy-start.3 = (bf16[368,640]{1,0:T(8,128)(2,1)}, bf16[368,640]{1,0:T(8,128)(2,1)S(1)}, u32[]{:S(2)}) copy-start(bf16[368,640]{1,0:T(8,128)(2,1)S(1)} %get-tuple-element.42.first_ref) | copy-start | bytes 1413124
  56.9 2.1 %collective-permute-start.9 = (bf16[640,512]{1,0:T(8,128)(2,1)S(1)}, bf16[640,512]{1,0:T(8,128)(2,1)S(1)}, u32[]{:S(2)}, u32[]{:S(2)}) collective-permute-start(bf16[640,512]{1,0:T(8,128)(2,1)S(1)} %bitcast.39), channel_id=1, source_target_pairs={{0,1},{1,0},{2,3},{3,2},{4,5},{5,4},{6,7},{7,6},{8,9},{9,8},{10,11... | collective-permute-start | bytes 1966088 | tf_op jit(solution)/shard_map/ppermute | solution.py:654
  56.9 2.1 %copy-start = (bf16[640,1280]{1,0:T(8,128)(2,1)S(1)}, bf16[640,1280]{1,0:T(8,128)(2,1)}, u32[]{:S(2)}) copy-start(bf16[640,1280]{1,0:T(8,128)(2,1)} %expand_ref.1) | copy-start | bytes 4915204
  56.9 2.1 %copy-start.1 = (bf16[1280,640]{1,0:T(8,128)(2,1)S(1)}, bf16[1280,640]{1,0:T(8,128)(2,1)}, u32[]{:S(2)}) copy-start(bf16[1280,640]{1,0:T(8,128)(2,1)} %reduce_ref.1) | copy-start | bytes 4915204
  56.9 2.1 %copy-start.4 = (bf16[368,640]{1,0:T(8,128)(2,1)S(1)}, bf16[368,640]{1,0:T(8,128)(2,1)}, u32[]{:S(2)}) copy-start(bf16[368,640]{1,0:T(8,128)(2,1)} %copy-done.3) | copy-start | bytes 1413124

commit v6 on v5

--- a/solution.py
+++ b/solution.py
@@ -567,9 +567,9 @@
     )(grid_state)
     grid_first = grid_state
     packed, later = lax.optimization_barrier(
-        (packed, (grid_state, conv_weight, spectral_gain, spectral_weight))
-    )
-    grid_state, conv_weight, spectral_gain, spectral_weight = later
+        (packed, (grid_state, conv_weight, spectral_gain))
+    )
+    grid_state, conv_weight, spectral_gain = later
     own = lax.all_to_all(packed, over_chips, split_axis=0, concat_axis=0, tiled=True)
 
     own_mix = spectral_weight.transpose(0, 2, 1)

time: 64 us -> 63.9 us (level)
  local copies, waits for them, and re-layouts: 9.54 us -> 8.2 us
  waiting for transfers between devices: 18.9 us -> 20.2 us
    all_to_all x1, waiting for transfers between devices: 4.66 us -> 5.92 us  [chip_shards(): lax.all_to_all(packed, over_chips, split_axis=0, concat_axis=0, tiled=True)]
    slice x2, local copies, waits for them, and re-layouts: 0.79 us -> 0.03 us  [chip_shards(): row[0]]
  transfers between devices with their start and end apart: 12 -> 12, of which waited for: 6 -> 6; matrix products, arithmetic and copies ran while one was open for 12% -> 11% of each run, Pallas kernels for 14% -> 16%
where the time goes in v6:
time: 63.9 us; the launch traced here: 63.2 us
  starting transfers between devices  20.2 us (32%)
  waiting for transfers between devices  20.2 us (32%)
  Pallas kernels  13.4 us (21%)
  local copies, waits for them, and re-layouts  8.2 us (13%)
  other arithmetic  0.97 us (2%)
    all_to_all x1, waiting for transfers between devices, chip_shards(): lax.all_to_all(bands.reshape(chips, share, 2 * M), over_chips, split_axis...  11.4 us
    pallas_call x1, Pallas kernels, chip_shards(): pl.pallas_call(functools.partial(spectral_body, lat_count, columns, share...  6.51 us
    all_to_all x1, starting transfers between devices, chip_shards(): lax.all_to_all(packed, over_chips, split_axis=0, concat_axis=0, tiled=True)  5.94 us
    all_to_all x1, waiting for transfers between devices, chip_shards(): lax.all_to_all(packed, over_chips, split_axis=0, concat_axis=0, tiled=True)  5.92 us
    all_to_all x1, starting transfers between devices, chip_shards(): lax.all_to_all(bands.reshape(chips, share, 2 * M), over_chips, split_axis...  3.94 us
    ppermute x1, starting transfers between devices, chip_shards(): lax.ppermute(grid_first[1], 'lat', [(i, i + 1) for i in range(lat_count -...  3.83 us
    pallas_call x1, Pallas kernels, chip_shards(): pl.pallas_call(functools.partial(finish_body, width, padded), out_shape=j...  3.25 us
    squeeze x3, local copies, waits for them, and re-layouts, own_part(): lax.dynamic_index_in_dim(jnp.asarray(constant), at, 0, keepdims=False)  3.18 us
  transfers between devices with their start and end apart: 12, of which 6 were waited for; matrix products, arithmetic and copies ran while one was open for 11% of the time, Pallas kernels for 16%

profile of v6, /device:TPU:0, one launch (start us, length us, event | category | flops | bytes accessed | tf_op | source)
XLA Modules:
  0.0 63.2 jit_solution(10730726865325054358)
XLA Ops:
  0.0 2.9 %collective-permute-start = (bf16[2,160,640]{2,1,0:T(8,128)(2,1)}, bf16[2,160,640]{2,1,0:T(8,128)(2,1)S(1)}, u32[]{:S(2)}, u32[]{:S(2)}) collective-permute-start(bf16[2,160,640]{2,1,0:T(8,128)(2,1)} %bitcast.41), channel_id=1, source_target_pairs={{0,2},{2,0},{1,3},{3,1},{4,6},{6,4},{5,7},{7,5},{8,10},{10,8},{9,1... | collective-permute-start | bytes 1228808 | tf_op jit(solution)/shard_map/ppermute | solution.py:578
  2.9 0.0 collective-permute-start.7
  2.9 1.1 %copy.11.grid_ref = bf16[2,180,640]{2,1,0:T(8,128)(2,1)S(1)} copy(bf16[2,180,640]{2,0,1:T(2,128)(2,1)} %param.10) | data formatting | bytes 921600 | tf_op args[0]
  4.0 0.0 copy-start.6
  4.0 1.1 %pack.1 = bf16[16,120,128]{2,1,0:T(8,128)(2,1)} custom-call(bf16[2,180,640]{2,1,0:T(8,128)(2,1)S(1)} %copy.11.grid_ref), custom_call_target="tpu_custom_call" | custom-call | tf_op jit(solution)/shard_map/pack/pallas_call | solution.py:559
  5.2 5.9 %all-to-all-start = ((bf16[16,120,128]{2,1,0:T(8,128)(2,1)}), bf16[16,120,128]{2,1,0:T(8,128)(2,1)S(1)}, u32[]{:S(2)}, u32[]{:S(2)}) async-start(bf16[16,120,128]{2,1,0:T(8,128)(2,1)} %pack.1), calls=%async_computation | async-start | bytes 983040 | tf_op jit(solution)/shard_map/all_to_all | solution.py:573
  11.1 0.0 copy-start.5
  11.1 0.8 %slice_bitcast_fusion = (bf16[180,640]{1,0:T(8,128)(2,1)}, bf16[180,640]{1,0:T(8,128)(2,1)}) fusion(bf16[2,180,640]{2,1,0:T(8,128)(2,1)S(1)} %copy.11.grid_ref), kind=kLoop, calls=%fused_computation.3 | loop fusion | bytes 921600 | tf_op jit(solution)/shard_map/squeeze | solution.py:607
  11.9 3.8 %collective-permute-start.3 = (bf16[180,640]{1,0:T(8,128)(2,1)}, bf16[180,640]{1,0:T(8,128)(2,1)S(1)}, u32[]{:S(2)}, u32[]{:S(2)}) collective-permute-start(bf16[180,640]{1,0:T(8,128)(2,1)} %get-tuple-element.44), channel_id=1, source_target_pairs={{0,4},{4,8},{8,12},{12,16},{16,20},{20,24},{24,28},{1,5},{5,9},{9,... | collective-permute-start | bytes 691208 | tf_op jit(solution)/shard_map/ppermute | solution.py:606
  15.8 1.3 %collective-permute-start.4 = (bf16[180,640]{1,0:T(8,128)(2,1)}, bf16[180,640]{1,0:T(8,128)(2,1)S(1)}, u32[]{:S(2)}, u32[]{:S(2)}) collective-permute-start(bf16[180,640]{1,0:T(8,128)(2,1)} %get-tuple-element.43), channel_id=1, source_target_pairs={{4,0},{8,4},{12,8},{16,12},{20,16},{24,20},{28,24},{5,1},{9,5},{13... | collective-permute-start | bytes 691208 | tf_op jit(solution)/shard_map/ppermute | solution.py:607
  17.1 0.0 copy-done.6
  17.1 1.1 %dynamic-slice_bitcast_fusion.table_ref = bf16[4,256,256]{2,1,0:T(8,128)(2,1)S(1)} fusion(bf16[2,4,256,256]{3,2,1,0:T(8,128)(2,1)} %constant.82.clone, s32[]{:T(128)S(6)} %select_n.76), kind=kLoop, calls=%fused_computation | loop fusion | bytes 1048580 | tf_op jit(solution)/shard_map/jit(dynamic_index_in_dim)/squeeze | solution.py:533
  18.2 0.1 constant_dynamic-slice_fusion
  18.3 1.1 %dynamic-slice_bitcast_fusion.1.legendre_ref = bf16[8,256,128]{2,1,0:T(8,128)(2,1)S(1)} fusion(bf16[2,8,256,128]{3,2,1,0:T(8,128)(2,1)} %constant.81.clone, s32[]{:T(128)S(6)} %select_n.76), kind=kLoop, calls=%fused_computation.1 | loop fusion | bytes 1048580 | tf_op jit(solution)/shard_map/jit(dynamic_index_in_dim)/squeeze | solution.py:533
  19.4 0.0 copy-done.5
  19.4 0.0 collective-permute-done.mix_c_ref
  19.4 0.9 %dynamic-slice_bitcast_fusion.3 = bf16[2,40,256]{2,1,0:T(8,128)(2,1)S(1)} fusion(f32[2,256,160]{1,2,0:T(8,128)} %param.12, s32[]{:T(128)S(6)} %select_n.69), kind=kLoop, calls=%fused_computation.6 | loop fusion | bytes 81924 | tf_op jit(solution)/shard_map/transpose | solution.py:583
  20.3 0.0 collective-permute-start.2
  20.4 5.9 %all-to-all-done.own_ref = bf16[16,120,128]{2,1,0:T(8,128)(2,1)S(1)} async-done(((bf16[16,120,128]{2,1,0:T(8,128)(2,1)}), bf16[16,120,128]{2,1,0:T(8,128)(2,1)S(1)}, u32[]{:S(2)}, u32[]{:S(2)}) %all-to-all-start) | async-done | bytes 491552 | tf_op jit(solution)/shard_map/all_to_all | solution.py:573
  26.3 0.0 collective-permute-start.1
  26.3 0.0 collective-permute-done.2
  26.3 0.9 %broadcast_select_fusion = bf16[2,40,256]{2,1,0:T(8,128)(2,1)S(1)} fusion(bf16[2,40,256]{2,1,0:T(8,128)(2,1)S(1)} %collective-permute-done.2, pred[]{:T(512)S(6)} %eq.22, f32[2,256,160]{1,2,0:T(8,128)} %param.12, s32[]{:T(128)S(6)} %select_n.69), kind=kLoop, calls=%fused_computation.13 | loop fusion | flops 20480 | bytes 122885 | tf_op jit(solution)/shard_map/jit(_where)/select_n | solution.py:585
  27.2 0.9 %collective-permute-done.1.other_ref = bf16[16,120,128]{2,1,0:T(8,128)(2,1)S(1)} collective-permute-done((bf16[16,120,128]{2,1,0:T(8,128)(2,1)S(1)}, bf16[16,120,128]{2,1,0:T(8,128)(2,1)S(1)}, u32[]{:S(2)}, u32[]{:S(2)}) %collective-permute-start.1) | collective-permute-done | bytes 491552 | tf_op jit(solution)/shard_map/ppermute | solution.py:605
  28.1 0.1 broadcast_in_dim.54.tap_ref
  28.3 6.5 %spectral.1 = bf16[2,8,40,512]{3,2,1,0:T(8,128)(2,1)} custom-call(s32[1]{0:T(128)} %bitcast.1.parity_ref, bf16[16,120,128]{2,1,0:T(8,128)(2,1)S(1)} %all-to-all-done.own_ref, bf16[16,120,128]{2,1,0:T(8,128)(2,1)S(1)} %collective-permute-done.1.other_ref, bf16[160,256]{1,0:T(8,128)(2,1)S(1)} %pad_maximum_fusion.gain_ref, ...), custom_call_target="tpu_custom_call" | custom-call | flops 8999999488 | tf_op jit(solution)/shard_map/spectral/pallas_call | solution.py:609
  34.8 0.0 copy-start.7
  34.8 0.0 collective-permute-done.3.above_ref
  34.8 0.0 collective-permute-done.4.below_ref
  34.8 3.9 %all-to-all-start.1 = ((bf16[16,40,512]{2,1,0:T(8,128)(2,1)}), bf16[16,40,512]{2,1,0:T(8,128)(2,1)S(1)}, u32[]{:S(2)}, u32[]{:S(2)}) async-start(bf16[16,40,512]{2,1,0:T(8,128)(2,1)} %bitcast.10), calls=%async_computation.1 | async-start | bytes 1310720 | tf_op jit(solution)/shard_map/all_to_all | solution.py:650
  38.8 1.1 %collective-permute-start.6 = (bf16[4,640]{1,0:T(4,128)(2,1)S(1)}, bf16[4,640]{1,0:T(4,128)(2,1)S(1)}, u32[]{:S(2)}, u32[]{:S(2)}) collective-permute-start(bf16[4,640]{1,0:T(4,128)(2,1)S(1)} %pad_maximum_fusion.2), channel_id=1, source_target_pairs={{1,0},{2,1},{3,2},{0,3},{5,4},{6,5},{7,6},{4,7},{9,8},{10,9},{11,1... | collective-permute-start | bytes 15368 | tf_op jit(solution)/shard_map/ppermute | solution.py:634
  39.9 0.1 collective-permute-start.5
  40.0 1.0 %dynamic-slice_bitcast_fusion.2.table_ref = bf16[2,368,256]{2,1,0:T(8,128)(2,1)S(1)} fusion(bf16[4,2,368,256]{3,2,1,0:T(8,128)(2,1)} %constant.83.clone, s32[]{:T(128)S(6)} %select_n.77), kind=kLoop, calls=%fused_computation.2 | loop fusion | bytes 753668 | tf_op jit(solution)/shard_map/jit(dynamic_index_in_dim)/squeeze | solution.py:533
  41.0 0.1 copy.14.grid_ref
  41.1 0.0 copy-done.7
  41.1 0.0 copy-start.2
  41.1 1.0 %collective-permute-start.8 = (bf16[2,160,640]{2,1,0:T(8,128)(2,1)S(1)}, bf16[2,160,640]{2,1,0:T(8,128)(2,1)S(1)}, u32[]{:S(2)}, u32[]{:S(2)}) collective-permute-start(bf16[2,160,640]{2,1,0:T(8,128)(2,1)S(1)} %collective-permute-done.mix_c_ref), channel_id=1, source_target_pairs={{0,1},{1,0},{2,3},{3,2},{4,5},{5,4},{6,7},{7,6},{8,9},{9,8},{10,11... | collective-permute-start | bytes 1228808 | tf_op jit(solution)/shard_map/ppermute | solution.py:628
  42.1 0.1 collective-permute-done.6.east_ref
  42.3 0.8 %collective-permute-done.5.west_ref = bf16[4,640]{1,0:T(4,128)(2,1)S(1)} collective-permute-done((bf16[4,640]{1,0:T(4,128)(2,1)S(1)}, bf16[4,640]{1,0:T(4,128)(2,1)S(1)}, u32[]{:S(2)}, u32[]{:S(2)}) %collective-permute-start.5) | collective-permute-done | bytes 5152 | tf_op jit(solution)/shard_map/ppermute | solution.py:631
  43.0 1.5 %local.1 = (bf16[368,640]{1,0:T(8,128)(2,1)S(1)}, f32[8,128]{1,0:T(8,128)S(1)}) custom-call(bf16[180,640]{1,0:T(8,128)(2,1)S(1)} %collective-permute-done.3.above_ref, bf16[2,180,640]{2,1,0:T(8,128)(2,1)S(1)} %copy.14.grid_ref, bf16[180,640]{1,0:T(8,128)(2,1)S(1)} %collective-permute-done.4.below_ref, bf16[4,640]{1,0:T(4,128)(2,1)S(1)} %collective-permute-done.5.west_ref, ...), custom_call_target="tpu_custom_call" | custom-call | flops 8000000000 | tf_op jit(solution)/shard_map/local/pallas_call | solution.py:637
  44.6 0.0 copy-start.3
  44.6 0.8 %copy-done.3 = bf16[368,640]{1,0:T(8,128)(2,1)} copy-done((bf16[368,640]{1,0:T(8,128)(2,1)}, bf16[368,640]{1,0:T(8,128)(2,1)S(1)}, u32[]{:S(2)}) %copy-start.3) | copy-done | bytes 471064
  45.4 11.4 %all-to-all-done.1 = bf16[16,40,512]{2,1,0:T(8,128)(2,1)S(1)} async-done(((bf16[16,40,512]{2,1,0:T(8,128)(2,1)}), bf16[16,40,512]{2,1,0:T(8,128)(2,1)S(1)}, u32[]{:S(2)}, u32[]{:S(2)}) %all-to-all-start.1) | async-done | bytes 655392 | tf_op jit(solution)/shard_map/all_to_all | solution.py:650
  56.8 0.0 collective-permute-start.9
  56.8 0.0 collective-permute-done.7.mix_b_ref
  56.8 0.0 collective-permute-done.8.mix_d_ref
  56.8 0.0 copy-done.2
  56.8 0.0 copy-start
  56.8 0.0 copy-start.1
  56.8 0.0 copy-start.4
  56.8 1.0 %stage.1 = (f32[2,368,640]{2,1,0:T(8,128)S(1)}, bf16[2,640,640]{2,1,0:T(8,128)(2,1)S(1)}) custom-call(s32[1]{0:T(128)} %bitcast.place_ref, bf16[640,512]{1,0:T(8,128)(2,1)S(1)} %bitcast.40, bf16[2,368,256]{2,1,0:T(8,128)(2,1)S(1)} %dynamic-slice_bitcast_fusion.2.table_ref, bf16[2,160,640]{2,1,0:T(8,128)(2,1)S(1)} %bitcast.43, ...), custom_call_target="tpu_custom_call" | custom-call | flops 12000000000 | tf_op jit(solution)/shard_map/stage/pallas_call | solution.py:656
  57.8 1.0 %collective-permute-done.9.other_ref = bf16[640,512]{1,0:T(8,128)(2,1)S(1)} collective-permute-done((bf16[640,512]{1,0:T(8,128)(2,1)S(1)}, bf16[640,512]{1,0:T(8,128)(2,1)S(1)}, u32[]{:S(2)}, u32[]{:S(2)}) %collective-permute-start.9) | collective-permute-done | bytes 655392 | tf_op jit(solution)/shard_map/ppermute | solution.py:654
  58.9 0.0 copy-done
  58.9 0.0 copy-done.1
  58.9 0.0 copy-done.4
  58.9 3.2 %finish.1 = bf16[2,180,640]{2,1,0:T(8,128)(2,1)S(1)} custom-call(f32[2,368,640]{2,1,0:T(8,128)S(1)} %get-tuple-element.39.field_ref, bf16[640,512]{1,0:T(8,128)(2,1)S(1)} %collective-permute-done.9.other_ref, bf16[368,640]{1,0:T(8,128)(2,1)S(1)} %copy-done.4, f32[1,640]{1,0:T(1,128)S(1)} %broadcast_in_dim.55.gain_ref, ...), custom_call_target="tpu_custom_call" | custom-call | flops 3000000000 | tf_op jit(solution)/shard_map/finish/pallas_call | solution.py:673
  62.1 1.1 %copy.15 = bf16[2,180,640]{2,0,1:T(2,128)(2,1)} copy(bf16[2,180,640]{2,1,0:T(8,128)(2,1)S(1)} %finish.1) | data formatting | bytes 921600 | tf_op jit(solution)/shard_map/finish/pallas_call | solution.py:673
  (9 shorter events, 0.1 us)
Async XLA Ops:
  0.0 19.4 %collective-permute-start = (bf16[2,160,640]{2,1,0:T(8,128)(2,1)}, bf16[2,160,640]{2,1,0:T(8,128)(2,1)S(1)}, u32[]{:S(2)}, u32[]{:S(2)}) collective-permute-start(bf16[2,160,640]{2,1,0:T(8,128)(2,1)} %bitcast.41), channel_id=1, source_target_pairs={{0,2},{2,0},{1,3},{3,1},{4,6},{6,4},{5,7},{7,5},{8,10},{10,8},{9,1... | collective-permute-start | bytes 1228808 | tf_op jit(solution)/shard_map/ppermute | solution.py:578
  2.9 53.8 %collective-permute-start.7 = (bf16[2,160,640]{2,1,0:T(8,128)(2,1)}, bf16[2,160,640]{2,1,0:T(8,128)(2,1)S(1)}, u32[]{:S(2)}, u32[]{:S(2)}) collective-permute-start(bf16[2,160,640]{2,1,0:T(8,128)(2,1)} %bitcast.42), channel_id=1, source_target_pairs={{0,1},{1,0},{2,3},{3,2},{4,5},{5,4},{6,7},{7,6},{8,9},{9,8},{10,11... | collective-permute-start | bytes 1228808 | tf_op jit(solution)/shard_map/ppermute | solution.py:627
  4.0 13.1 %copy-start.6 = (f32[3,3,640]{2,1,0:T(4,128)S(1)}, f32[3,3,640]{2,1,0:T(4,128)}, u32[]{:S(2)}) copy-start(f32[3,3,640]{2,1,0:T(4,128)} %param.11) | copy-start | bytes 69124
  5.2 21.1 %all-to-all-start = ((bf16[16,120,128]{2,1,0:T(8,128)(2,1)}), bf16[16,120,128]{2,1,0:T(8,128)(2,1)S(1)}, u32[]{:S(2)}, u32[]{:S(2)}) async-start(bf16[16,120,128]{2,1,0:T(8,128)(2,1)} %pack.1), calls=%async_computation | async-start | bytes 983040 | tf_op jit(solution)/shard_map/all_to_all | solution.py:573
  11.1 8.3 %copy-start.5 = (bf16[2,180,640]{2,0,1:T(2,128)(2,1)S(1)}, bf16[2,180,640]{2,0,1:T(2,128)(2,1)}, u32[]{:S(2)}) copy-start(bf16[2,180,640]{2,0,1:T(2,128)(2,1)} %param.10) | copy-start | bytes 1382404
  11.9 22.8 %collective-permute-start.3 = (bf16[180,640]{1,0:T(8,128)(2,1)}, bf16[180,640]{1,0:T(8,128)(2,1)S(1)}, u32[]{:S(2)}, u32[]{:S(2)}) collective-permute-start(bf16[180,640]{1,0:T(8,128)(2,1)} %get-tuple-element.44), channel_id=1, source_target_pairs={{0,4},{4,8},{8,12},{12,16},{16,20},{20,24},{24,28},{1,5},{5,9},{9,... | collective-permute-start | bytes 691208 | tf_op jit(solution)/shard_map/ppermute | solution.py:606
  15.8 19.0 %collective-permute-start.4 = (bf16[180,640]{1,0:T(8,128)(2,1)}, bf16[180,640]{1,0:T(8,128)(2,1)S(1)}, u32[]{:S(2)}, u32[]{:S(2)}) collective-permute-start(bf16[180,640]{1,0:T(8,128)(2,1)} %get-tuple-element.43), channel_id=1, source_target_pairs={{4,0},{8,4},{12,8},{16,12},{20,16},{24,20},{28,24},{5,1},{9,5},{13... | collective-permute-start | bytes 691208 | tf_op jit(solution)/shard_map/ppermute | solution.py:607
  20.3 6.0 %collective-permute-start.2 = (bf16[2,40,256]{2,1,0:T(8,128)(2,1)S(1)}, bf16[2,40,256]{2,1,0:T(8,128)(2,1)S(1)}, u32[]{:S(2)}, u32[]{:S(2)}) collective-permute-start(bf16[2,40,256]{2,1,0:T(8,128)(2,1)S(1)} %dynamic-slice_bitcast_fusion.3), channel_id=1, source_target_pairs={{0,1},{1,0},{2,3},{3,2},{4,5},{5,4},{6,7},{7,6},{8,9},{9,8},{10,11... | collective-permute-start | bytes 122888 | tf_op jit(solution)/shard_map/ppermute | solution.py:584
  26.3 1.9 %collective-permute-start.1 = (bf16[16,120,128]{2,1,0:T(8,128)(2,1)S(1)}, bf16[16,120,128]{2,1,0:T(8,128)(2,1)S(1)}, u32[]{:S(2)}, u32[]{:S(2)}) collective-permute-start(bf16[16,120,128]{2,1,0:T(8,128)(2,1)S(1)} %all-to-all-done.own_ref), channel_id=1, source_target_pairs={{0,1},{1,0},{2,3},{3,2},{4,5},{5,4},{6,7},{7,6},{8,9},{9,8},{10,11... | collective-permute-start | bytes 1474568 | tf_op jit(solution)/shard_map/ppermute | solution.py:605
  34.8 6.3 %copy-start.7 = (f32[640]{0:T(1024)S(1)}, f32[640]{0:T(1024)}, u32[]{:S(2)}) copy-start(f32[640]{0:T(1024)} %param.14) | copy-start | bytes 7684
  34.8 22.0 %all-to-all-start.1 = ((bf16[16,40,512]{2,1,0:T(8,128)(2,1)}), bf16[16,40,512]{2,1,0:T(8,128)(2,1)S(1)}, u32[]{:S(2)}, u32[]{:S(2)}) async-start(bf16[16,40,512]{2,1,0:T(8,128)(2,1)} %bitcast.10), calls=%async_computation.1 | async-start | bytes 1310720 | tf_op jit(solution)/shard_map/all_to_all | solution.py:650
  38.8 3.5 %collective-permute-start.6 = (bf16[4,640]{1,0:T(4,128)(2,1)S(1)}, bf16[4,640]{1,0:T(4,128)(2,1)S(1)}, u32[]{:S(2)}, u32[]{:S(2)}) collective-permute-start(bf16[4,640]{1,0:T(4,128)(2,1)S(1)} %pad_maximum_fusion.2), channel_id=1, source_target_pairs={{1,0},{2,1},{3,2},{0,3},{5,4},{6,5},{7,6},{4,7},{9,8},{10,9},{11,1... | collective-permute-start | bytes 15368 | tf_op jit(solution)/shard_map/ppermute | solution.py:634
  39.9 3.1 %collective-permute-start.5 = (bf16[4,640]{1,0:T(4,128)(2,1)S(1)}, bf16[4,640]{1,0:T(4,128)(2,1)S(1)}, u32[]{:S(2)}, u32[]{:S(2)}) collective-permute-start(bf16[4,640]{1,0:T(4,128)(2,1)S(1)} %pad_maximum_fusion.1), channel_id=1, source_target_pairs={{0,1},{1,2},{2,3},{3,0},{4,5},{5,6},{6,7},{7,4},{8,9},{9,10},{10,1... | collective-permute-start | bytes 15368 | tf_op jit(solution)/shard_map/ppermute | solution.py:631
  41.1 15.7 %copy-start.2 = (bf16[2,640,160]{1,2,0:T(8,128)(2,1)S(1)}, bf16[2,640,160]{1,2,0:T(8,128)(2,1)}, u32[]{:S(2)}) copy-start(bf16[2,640,160]{1,2,0:T(8,128)(2,1)} %param.13) | copy-start | bytes 1228804
  41.1 15.6 %collective-permute-start.8 = (bf16[2,160,640]{2,1,0:T(8,128)(2,1)S(1)}, bf16[2,160,640]{2,1,0:T(8,128)(2,1)S(1)}, u32[]{:S(2)}, u32[]{:S(2)}) collective-permute-start(bf16[2,160,640]{2,1,0:T(8,128)(2,1)S(1)} %collective-permute-done.mix_c_ref), channel_id=1, source_target_pairs={{0,1},{1,0},{2,3},{3,2},{4,5},{5,4},{6,7},{7,6},{8,9},{9,8},{10,11... | collective-permute-start | bytes 1228808 | tf_op jit(solution)/shard_map/ppermute | solution.py:628
  44.6 0.8 %copy-start.3 = (bf16[368,640]{1,0:T(8,128)(2,1)}, bf16[368,640]{1,0:T(8,128)(2,1)S(1)}, u32[]{:S(2)}) copy-start(bf16[368,640]{1,0:T(8,128)(2,1)S(1)} %get-tuple-element.40.first_ref) | copy-start | bytes 1413124
  56.8 2.1 %collective-permute-start.9 = (bf16[640,512]{1,0:T(8,128)(2,1)S(1)}, bf16[640,512]{1,0:T(8,128)(2,1)S(1)}, u32[]{:S(2)}, u32[]{:S(2)}) collective-permute-start(bf16[640,512]{1,0:T(8,128)(2,1)S(1)} %bitcast.39), channel_id=1, source_target_pairs={{0,1},{1,0},{2,3},{3,2},{4,5},{5,4},{6,7},{7,6},{8,9},{9,8},{10,11... | collective-permute-start | bytes 1966088 | tf_op jit(solution)/shard_map/ppermute | solution.py:654
  56.8 2.1 %copy-start = (bf16[640,1280]{1,0:T(8,128)(2,1)S(1)}, bf16[640,1280]{1,0:T(8,128)(2,1)}, u32[]{:S(2)}) copy-start(bf16[640,1280]{1,0:T(8,128)(2,1)} %expand_ref.1) | copy-start | bytes 4915204
  56.8 2.1 %copy-start.1 = (bf16[1280,640]{1,0:T(8,128)(2,1)S(1)}, bf16[1280,640]{1,0:T(8,128)(2,1)}, u32[]{:S(2)}) copy-start(bf16[1280,640]{1,0:T(8,128)(2,1)} %reduce_ref.1) | copy-start | bytes 4915204
  56.8 2.1 %copy-start.4 = (bf16[368,640]{1,0:T(8,128)(2,1)S(1)}, bf16[368,640]{1,0:T(8,128)(2,1)}, u32[]{:S(2)}) copy-start(bf16[368,640]{1,0:T(8,128)(2,1)} %copy-done.3) | copy-start | bytes 1413124

commit v7 on v6

--- a/solution.py
+++ b/solution.py
@@ -271,6 +271,11 @@
     return out.reshape(sectors, 2, 2 * padded, mode_count).astype(jnp.bfloat16)
 
 
+def gelu_of_double(half):
+    inner = half * (1.5957691216057308 + (8 * 0.7978845608028654 * 0.044715) * (half * half))
+    return half + half * jnp.tanh(inner)
+
+
 def gelu(value):
     inner = value * (0.7978845608028654 + (0.7978845608028654 * 0.044715) * (value * value))
     half = 0.5 * value
@@ -363,7 +368,7 @@
             held, total, ahead = None, None, None
 
             def finish(t, value, sum_):
-                first_ref[sector, pl.ds(pl.multiple_of(t * share + tile * 8, 8), 8), :] = value + gelu(sum_)
+                first_ref[sector, pl.ds(pl.multiple_of(t * share + tile * 8, 8), 8), :] = value + gelu_of_double(sum_)
 
             for t in range(lat_total):
                 value = field_ref[sector, t, rows, :]
@@ -385,7 +390,8 @@
 
         return lax.fori_loop(0, share // 8, filter_rows, unused)
 
-    lax.fori_loop(0, sectors, filter_sector, 0)
+    for sector in range(sectors):
+        filter_sector(sector, 0)
 
     modes = None
     for sector in range(sectors):
@@ -595,7 +601,7 @@
     ).astype(jnp.bfloat16)
     chip = column * lat_count + lat_at
     taps = lax.dynamic_slice_in_dim(conv_weight.reshape(9, channels), chip * share, share, axis=1)
-    taps = jnp.broadcast_to(taps[:, :, None], (9, share, LANES))
+    taps = jnp.broadcast_to(0.5 * taps[:, :, None], (9, share, LANES))
 
     legendre = own_part(parity_tables(lat_total, M), core)
     analysis = own_part(analysis_constant(sectors, width, span, M), core)

time: 63.9 us -> 63.8 us (level)
  no operation moved by 1% of the time
where the time goes in v7:
time: 63.8 us; the launch traced here: 63.2 us
  starting transfers between devices  20.2 us (32%)
  waiting for transfers between devices  20.2 us (32%)
  Pallas kernels  13.4 us (21%)
  local copies, waits for them, and re-layouts  8.13 us (13%)
  other arithmetic  1.05 us (2%)
    all_to_all x1, waiting for transfers between devices, chip_shards(): lax.all_to_all(bands.reshape(chips, share, 2 * M), over_chips, split_axis...  11.4 us
    pallas_call x1, Pallas kernels, chip_shards(): pl.pallas_call(functools.partial(spectral_body, lat_count, columns, share...  6.43 us
    all_to_all x1, starting transfers between devices, chip_shards(): lax.all_to_all(packed, over_chips, split_axis=0, concat_axis=0, tiled=True)  5.94 us
    all_to_all x1, waiting for transfers between devices, chip_shards(): lax.all_to_all(packed, over_chips, split_axis=0, concat_axis=0, tiled=True)  5.91 us
    all_to_all x1, starting transfers between devices, chip_shards(): lax.all_to_all(bands.reshape(chips, share, 2 * M), over_chips, split_axis...  3.94 us
    ppermute x1, starting transfers between devices, chip_shards(): lax.ppermute(grid_first[1], 'lat', [(i, i + 1) for i in range(lat_count -...  3.83 us
    pallas_call x1, Pallas kernels, chip_shards(): pl.pallas_call(functools.partial(finish_body, width, padded), out_shape=j...  3.25 us
    squeeze x3, local copies, waits for them, and re-layouts, own_part(): lax.dynamic_index_in_dim(jnp.asarray(constant), at, 0, keepdims=False)  3.18 us
  transfers between devices with their start and end apart: 12, of which 6 were waited for; matrix products, arithmetic and copies ran while one was open for 11% of the time, Pallas kernels for 16%

profile of v7, /device:TPU:0, one launch (start us, length us, event | category | flops | bytes accessed | tf_op | source)
XLA Modules:
  0.0 63.2 jit_solution(2651614257492978749)
XLA Ops:
  0.0 2.9 %collective-permute-start = (bf16[2,160,640]{2,1,0:T(8,128)(2,1)}, bf16[2,160,640]{2,1,0:T(8,128)(2,1)S(1)}, u32[]{:S(2)}, u32[]{:S(2)}) collective-permute-start(bf16[2,160,640]{2,1,0:T(8,128)(2,1)} %bitcast.41), channel_id=1, source_target_pairs={{0,2},{2,0},{1,3},{3,1},{4,6},{6,4},{5,7},{7,5},{8,10},{10,8},{9,1... | collective-permute-start | bytes 1228808 | tf_op jit(solution)/shard_map/ppermute | solution.py:584
  2.9 0.0 collective-permute-start.7
  2.9 1.1 %copy.11.grid_ref = bf16[2,180,640]{2,1,0:T(8,128)(2,1)S(1)} copy(bf16[2,180,640]{2,0,1:T(2,128)(2,1)} %param.10) | data formatting | bytes 921600 | tf_op args[0]
  4.0 0.0 copy-start.6
  4.0 1.1 %pack.1 = bf16[16,120,128]{2,1,0:T(8,128)(2,1)} custom-call(bf16[2,180,640]{2,1,0:T(8,128)(2,1)S(1)} %copy.11.grid_ref), custom_call_target="tpu_custom_call" | custom-call | tf_op jit(solution)/shard_map/pack/pallas_call | solution.py:565
  5.2 5.9 %all-to-all-start = ((bf16[16,120,128]{2,1,0:T(8,128)(2,1)}), bf16[16,120,128]{2,1,0:T(8,128)(2,1)S(1)}, u32[]{:S(2)}, u32[]{:S(2)}) async-start(bf16[16,120,128]{2,1,0:T(8,128)(2,1)} %pack.1), calls=%async_computation | async-start | bytes 983040 | tf_op jit(solution)/shard_map/all_to_all | solution.py:579
  11.1 0.0 copy-start.5
  11.1 0.8 %slice_bitcast_fusion = (bf16[180,640]{1,0:T(8,128)(2,1)}, bf16[180,640]{1,0:T(8,128)(2,1)}) fusion(bf16[2,180,640]{2,1,0:T(8,128)(2,1)S(1)} %copy.11.grid_ref), kind=kLoop, calls=%fused_computation.3 | loop fusion | bytes 921600 | tf_op jit(solution)/shard_map/squeeze | solution.py:613
  11.9 3.8 %collective-permute-start.3 = (bf16[180,640]{1,0:T(8,128)(2,1)}, bf16[180,640]{1,0:T(8,128)(2,1)S(1)}, u32[]{:S(2)}, u32[]{:S(2)}) collective-permute-start(bf16[180,640]{1,0:T(8,128)(2,1)} %get-tuple-element.44), channel_id=1, source_target_pairs={{0,4},{4,8},{8,12},{12,16},{16,20},{20,24},{24,28},{1,5},{5,9},{9,... | collective-permute-start | bytes 691208 | tf_op jit(solution)/shard_map/ppermute | solution.py:612
  15.8 1.3 %collective-permute-start.4 = (bf16[180,640]{1,0:T(8,128)(2,1)}, bf16[180,640]{1,0:T(8,128)(2,1)S(1)}, u32[]{:S(2)}, u32[]{:S(2)}) collective-permute-start(bf16[180,640]{1,0:T(8,128)(2,1)} %get-tuple-element.43), channel_id=1, source_target_pairs={{4,0},{8,4},{12,8},{16,12},{20,16},{24,20},{28,24},{5,1},{9,5},{13... | collective-permute-start | bytes 691208 | tf_op jit(solution)/shard_map/ppermute | solution.py:613
  17.1 0.0 copy-done.6
  17.1 1.1 %dynamic-slice_bitcast_fusion.table_ref = bf16[4,256,256]{2,1,0:T(8,128)(2,1)S(1)} fusion(bf16[2,4,256,256]{3,2,1,0:T(8,128)(2,1)} %constant.84.clone, s32[]{:T(128)S(6)} %select_n.76), kind=kLoop, calls=%fused_computation | loop fusion | bytes 1048580 | tf_op jit(solution)/shard_map/jit(dynamic_index_in_dim)/squeeze | solution.py:539
  18.2 0.1 dynamic-slice_multiply_fusion
  18.3 1.1 %dynamic-slice_bitcast_fusion.1.legendre_ref = bf16[8,256,128]{2,1,0:T(8,128)(2,1)S(1)} fusion(bf16[2,8,256,128]{3,2,1,0:T(8,128)(2,1)} %constant.83.clone, s32[]{:T(128)S(6)} %select_n.76), kind=kLoop, calls=%fused_computation.1 | loop fusion | bytes 1048580 | tf_op jit(solution)/shard_map/jit(dynamic_index_in_dim)/squeeze | solution.py:539
  19.4 0.0 copy-done.5
  19.4 0.0 collective-permute-done.mix_c_ref
  19.4 0.9 %dynamic-slice_bitcast_fusion.3 = bf16[2,40,256]{2,1,0:T(8,128)(2,1)S(1)} fusion(f32[2,256,160]{1,2,0:T(8,128)} %param.12, s32[]{:T(128)S(6)} %select_n.69), kind=kLoop, calls=%fused_computation.6 | loop fusion | bytes 81924 | tf_op jit(solution)/shard_map/transpose | solution.py:589
  20.3 0.0 collective-permute-start.2
  20.4 5.9 %all-to-all-done.own_ref = bf16[16,120,128]{2,1,0:T(8,128)(2,1)S(1)} async-done(((bf16[16,120,128]{2,1,0:T(8,128)(2,1)}), bf16[16,120,128]{2,1,0:T(8,128)(2,1)S(1)}, u32[]{:S(2)}, u32[]{:S(2)}) %all-to-all-start) | async-done | bytes 491552 | tf_op jit(solution)/shard_map/all_to_all | solution.py:579
  26.3 0.0 collective-permute-start.1
  26.3 0.0 collective-permute-done.2
  26.3 0.9 %broadcast_select_fusion = bf16[2,40,256]{2,1,0:T(8,128)(2,1)S(1)} fusion(bf16[2,40,256]{2,1,0:T(8,128)(2,1)S(1)} %collective-permute-done.2, pred[]{:T(512)S(6)} %eq.22, f32[2,256,160]{1,2,0:T(8,128)} %param.12, s32[]{:T(128)S(6)} %select_n.69), kind=kLoop, calls=%fused_computation.13 | loop fusion | flops 20480 | bytes 122885 | tf_op jit(solution)/shard_map/jit(_where)/select_n | solution.py:591
  27.2 0.9 %collective-permute-done.1.other_ref = bf16[16,120,128]{2,1,0:T(8,128)(2,1)S(1)} collective-permute-done((bf16[16,120,128]{2,1,0:T(8,128)(2,1)S(1)}, bf16[16,120,128]{2,1,0:T(8,128)(2,1)S(1)}, u32[]{:S(2)}, u32[]{:S(2)}) %collective-permute-start.1) | collective-permute-done | bytes 491552 | tf_op jit(solution)/shard_map/ppermute | solution.py:611
  28.1 0.1 broadcast_in_dim.54.tap_ref
  28.3 6.4 %spectral.1 = bf16[2,8,40,512]{3,2,1,0:T(8,128)(2,1)} custom-call(s32[1]{0:T(128)} %bitcast.1.parity_ref, bf16[16,120,128]{2,1,0:T(8,128)(2,1)S(1)} %all-to-all-done.own_ref, bf16[16,120,128]{2,1,0:T(8,128)(2,1)S(1)} %collective-permute-done.1.other_ref, bf16[160,256]{1,0:T(8,128)(2,1)S(1)} %pad_maximum_fusion.gain_ref, ...), custom_call_target="tpu_custom_call" | custom-call | flops 8999999488 | tf_op jit(solution)/shard_map/spectral/pallas_call | solution.py:615
  34.7 0.0 copy-start.7
  34.7 0.0 collective-permute-done.3.above_ref
  34.7 0.0 collective-permute-done.4.below_ref
  34.7 3.9 %all-to-all-start.1 = ((bf16[16,40,512]{2,1,0:T(8,128)(2,1)}), bf16[16,40,512]{2,1,0:T(8,128)(2,1)S(1)}, u32[]{:S(2)}, u32[]{:S(2)}) async-start(bf16[16,40,512]{2,1,0:T(8,128)(2,1)} %bitcast.10), calls=%async_computation.1 | async-start | bytes 1310720 | tf_op jit(solution)/shard_map/all_to_all | solution.py:656
  38.7 1.1 %collective-permute-start.6 = (bf16[4,640]{1,0:T(4,128)(2,1)S(1)}, bf16[4,640]{1,0:T(4,128)(2,1)S(1)}, u32[]{:S(2)}, u32[]{:S(2)}) collective-permute-start(bf16[4,640]{1,0:T(4,128)(2,1)S(1)} %pad_maximum_fusion.2), channel_id=1, source_target_pairs={{1,0},{2,1},{3,2},{0,3},{5,4},{6,5},{7,6},{4,7},{9,8},{10,9},{11,1... | collective-permute-start | bytes 15368 | tf_op jit(solution)/shard_map/ppermute | solution.py:640
  39.9 0.1 collective-permute-start.5
  39.9 1.0 %dynamic-slice_bitcast_fusion.2.table_ref = bf16[2,368,256]{2,1,0:T(8,128)(2,1)S(1)} fusion(bf16[4,2,368,256]{3,2,1,0:T(8,128)(2,1)} %constant.85.clone, s32[]{:T(128)S(6)} %select_n.77), kind=kLoop, calls=%fused_computation.2 | loop fusion | bytes 753668 | tf_op jit(solution)/shard_map/jit(dynamic_index_in_dim)/squeeze | solution.py:539
  41.0 0.1 copy.14.grid_ref
  41.0 0.0 copy-done.7
  41.0 0.0 copy-start.2
  41.1 1.0 %collective-permute-start.8 = (bf16[2,160,640]{2,1,0:T(8,128)(2,1)S(1)}, bf16[2,160,640]{2,1,0:T(8,128)(2,1)S(1)}, u32[]{:S(2)}, u32[]{:S(2)}) collective-permute-start(bf16[2,160,640]{2,1,0:T(8,128)(2,1)S(1)} %collective-permute-done.mix_c_ref), channel_id=1, source_target_pairs={{0,1},{1,0},{2,3},{3,2},{4,5},{5,4},{6,7},{7,6},{8,9},{9,8},{10,11... | collective-permute-start | bytes 1228808 | tf_op jit(solution)/shard_map/ppermute | solution.py:634
  42.1 0.1 collective-permute-done.6.east_ref
  42.2 0.8 %collective-permute-done.5.west_ref = bf16[4,640]{1,0:T(4,128)(2,1)S(1)} collective-permute-done((bf16[4,640]{1,0:T(4,128)(2,1)S(1)}, bf16[4,640]{1,0:T(4,128)(2,1)S(1)}, u32[]{:S(2)}, u32[]{:S(2)}) %collective-permute-start.5) | collective-permute-done | bytes 5152 | tf_op jit(solution)/shard_map/ppermute | solution.py:637
  43.0 1.5 %local.1 = (bf16[368,640]{1,0:T(8,128)(2,1)S(1)}, f32[8,128]{1,0:T(8,128)S(1)}) custom-call(bf16[180,640]{1,0:T(8,128)(2,1)S(1)} %collective-permute-done.3.above_ref, bf16[2,180,640]{2,1,0:T(8,128)(2,1)S(1)} %copy.14.grid_ref, bf16[180,640]{1,0:T(8,128)(2,1)S(1)} %collective-permute-done.4.below_ref, bf16[4,640]{1,0:T(4,128)(2,1)S(1)} %collective-permute-done.5.west_ref, ...), custom_call_target="tpu_custom_call" | custom-call | flops 8000000000 | tf_op jit(solution)/shard_map/local/pallas_call | solution.py:643
  44.5 0.0 copy-start.3
  44.5 0.8 %copy-done.3 = bf16[368,640]{1,0:T(8,128)(2,1)} copy-done((bf16[368,640]{1,0:T(8,128)(2,1)}, bf16[368,640]{1,0:T(8,128)(2,1)S(1)}, u32[]{:S(2)}) %copy-start.3) | copy-done | bytes 471064
  45.3 11.4 %all-to-all-done.1 = bf16[16,40,512]{2,1,0:T(8,128)(2,1)S(1)} async-done(((bf16[16,40,512]{2,1,0:T(8,128)(2,1)}), bf16[16,40,512]{2,1,0:T(8,128)(2,1)S(1)}, u32[]{:S(2)}, u32[]{:S(2)}) %all-to-all-start.1) | async-done | bytes 655392 | tf_op jit(solution)/shard_map/all_to_all | solution.py:656
  56.7 0.0 collective-permute-start.9
  56.7 0.0 collective-permute-done.7.mix_b_ref
  56.7 0.0 collective-permute-done.8.mix_d_ref
  56.7 0.0 copy-done.2
  56.7 0.0 copy-start
  56.7 0.0 copy-start.1
  56.7 0.0 copy-start.4
  56.7 1.0 %stage.1 = (f32[2,368,640]{2,1,0:T(8,128)S(1)}, bf16[2,640,640]{2,1,0:T(8,128)(2,1)S(1)}) custom-call(s32[1]{0:T(128)} %bitcast.place_ref, bf16[640,512]{1,0:T(8,128)(2,1)S(1)} %bitcast.40, bf16[2,368,256]{2,1,0:T(8,128)(2,1)S(1)} %dynamic-slice_bitcast_fusion.2.table_ref, bf16[2,160,640]{2,1,0:T(8,128)(2,1)S(1)} %bitcast.43, ...), custom_call_target="tpu_custom_call" | custom-call | flops 12000000000 | tf_op jit(solution)/shard_map/stage/pallas_call | solution.py:662
  57.7 1.0 %collective-permute-done.9.other_ref = bf16[640,512]{1,0:T(8,128)(2,1)S(1)} collective-permute-done((bf16[640,512]{1,0:T(8,128)(2,1)S(1)}, bf16[640,512]{1,0:T(8,128)(2,1)S(1)}, u32[]{:S(2)}, u32[]{:S(2)}) %collective-permute-start.9) | collective-permute-done | bytes 655392 | tf_op jit(solution)/shard_map/ppermute | solution.py:660
  58.8 0.0 copy-done
  58.8 0.0 copy-done.1
  58.8 0.0 copy-done.4
  58.8 3.2 %finish.1 = bf16[2,180,640]{2,1,0:T(8,128)(2,1)S(1)} custom-call(f32[2,368,640]{2,1,0:T(8,128)S(1)} %get-tuple-element.39.field_ref, bf16[640,512]{1,0:T(8,128)(2,1)S(1)} %collective-permute-done.9.other_ref, bf16[368,640]{1,0:T(8,128)(2,1)S(1)} %copy-done.4, f32[1,640]{1,0:T(1,128)S(1)} %broadcast_in_dim.55.gain_ref, ...), custom_call_target="tpu_custom_call" | custom-call | flops 3000000000 | tf_op jit(solution)/shard_map/finish/pallas_call | solution.py:679
  62.0 1.1 %copy.15 = bf16[2,180,640]{2,0,1:T(2,128)(2,1)} copy(bf16[2,180,640]{2,1,0:T(8,128)(2,1)S(1)} %finish.1) | data formatting | bytes 921600 | tf_op jit(solution)/shard_map/finish/pallas_call | solution.py:679
  (9 shorter events, 0.1 us)
Async XLA Ops:
  0.0 19.4 %collective-permute-start = (bf16[2,160,640]{2,1,0:T(8,128)(2,1)}, bf16[2,160,640]{2,1,0:T(8,128)(2,1)S(1)}, u32[]{:S(2)}, u32[]{:S(2)}) collective-permute-start(bf16[2,160,640]{2,1,0:T(8,128)(2,1)} %bitcast.41), channel_id=1, source_target_pairs={{0,2},{2,0},{1,3},{3,1},{4,6},{6,4},{5,7},{7,5},{8,10},{10,8},{9,1... | collective-permute-start | bytes 1228808 | tf_op jit(solution)/shard_map/ppermute | solution.py:584
  2.9 53.7 %collective-permute-start.7 = (bf16[2,160,640]{2,1,0:T(8,128)(2,1)}, bf16[2,160,640]{2,1,0:T(8,128)(2,1)S(1)}, u32[]{:S(2)}, u32[]{:S(2)}) collective-permute-start(bf16[2,160,640]{2,1,0:T(8,128)(2,1)} %bitcast.42), channel_id=1, source_target_pairs={{0,1},{1,0},{2,3},{3,2},{4,5},{5,4},{6,7},{7,6},{8,9},{9,8},{10,11... | collective-permute-start | bytes 1228808 | tf_op jit(solution)/shard_map/ppermute | solution.py:633
  4.0 13.1 %copy-start.6 = (f32[3,3,640]{2,1,0:T(4,128)S(1)}, f32[3,3,640]{2,1,0:T(4,128)}, u32[]{:S(2)}) copy-start(f32[3,3,640]{2,1,0:T(4,128)} %param.11) | copy-start | bytes 69124
  5.2 21.1 %all-to-all-start = ((bf16[16,120,128]{2,1,0:T(8,128)(2,1)}), bf16[16,120,128]{2,1,0:T(8,128)(2,1)S(1)}, u32[]{:S(2)}, u32[]{:S(2)}) async-start(bf16[16,120,128]{2,1,0:T(8,128)(2,1)} %pack.1), calls=%async_computation | async-start | bytes 983040 | tf_op jit(solution)/shard_map/all_to_all | solution.py:579
  11.1 8.3 %copy-start.5 = (bf16[2,180,640]{2,0,1:T(2,128)(2,1)S(1)}, bf16[2,180,640]{2,0,1:T(2,128)(2,1)}, u32[]{:S(2)}) copy-start(bf16[2,180,640]{2,0,1:T(2,128)(2,1)} %param.10) | copy-start | bytes 1382404
  11.9 22.8 %collective-permute-start.3 = (bf16[180,640]{1,0:T(8,128)(2,1)}, bf16[180,640]{1,0:T(8,128)(2,1)S(1)}, u32[]{:S(2)}, u32[]{:S(2)}) collective-permute-start(bf16[180,640]{1,0:T(8,128)(2,1)} %get-tuple-element.44), channel_id=1, source_target_pairs={{0,4},{4,8},{8,12},{12,16},{16,20},{20,24},{24,28},{1,5},{5,9},{9,... | collective-permute-start | bytes 691208 | tf_op jit(solution)/shard_map/ppermute | solution.py:612
  15.8 18.9 %collective-permute-start.4 = (bf16[180,640]{1,0:T(8,128)(2,1)}, bf16[180,640]{1,0:T(8,128)(2,1)S(1)}, u32[]{:S(2)}, u32[]{:S(2)}) collective-permute-start(bf16[180,640]{1,0:T(8,128)(2,1)} %get-tuple-element.43), channel_id=1, source_target_pairs={{4,0},{8,4},{12,8},{16,12},{20,16},{24,20},{28,24},{5,1},{9,5},{13... | collective-permute-start | bytes 691208 | tf_op jit(solution)/shard_map/ppermute | solution.py:613
  20.3 6.0 %collective-permute-start.2 = (bf16[2,40,256]{2,1,0:T(8,128)(2,1)S(1)}, bf16[2,40,256]{2,1,0:T(8,128)(2,1)S(1)}, u32[]{:S(2)}, u32[]{:S(2)}) collective-permute-start(bf16[2,40,256]{2,1,0:T(8,128)(2,1)S(1)} %dynamic-slice_bitcast_fusion.3), channel_id=1, source_target_pairs={{0,1},{1,0},{2,3},{3,2},{4,5},{5,4},{6,7},{7,6},{8,9},{9,8},{10,11... | collective-permute-start | bytes 122888 | tf_op jit(solution)/shard_map/ppermute | solution.py:590
  26.3 1.9 %collective-permute-start.1 = (bf16[16,120,128]{2,1,0:T(8,128)(2,1)S(1)}, bf16[16,120,128]{2,1,0:T(8,128)(2,1)S(1)}, u32[]{:S(2)}, u32[]{:S(2)}) collective-permute-start(bf16[16,120,128]{2,1,0:T(8,128)(2,1)S(1)} %all-to-all-done.own_ref), channel_id=1, source_target_pairs={{0,1},{1,0},{2,3},{3,2},{4,5},{5,4},{6,7},{7,6},{8,9},{9,8},{10,11... | collective-permute-start | bytes 1474568 | tf_op jit(solution)/shard_map/ppermute | solution.py:611
  34.7 6.3 %copy-start.7 = (f32[640]{0:T(1024)S(1)}, f32[640]{0:T(1024)}, u32[]{:S(2)}) copy-start(f32[640]{0:T(1024)} %param.14) | copy-start | bytes 7684
  34.7 22.0 %all-to-all-start.1 = ((bf16[16,40,512]{2,1,0:T(8,128)(2,1)}), bf16[16,40,512]{2,1,0:T(8,128)(2,1)S(1)}, u32[]{:S(2)}, u32[]{:S(2)}) async-start(bf16[16,40,512]{2,1,0:T(8,128)(2,1)} %bitcast.10), calls=%async_computation.1 | async-start | bytes 1310720 | tf_op jit(solution)/shard_map/all_to_all | solution.py:656
  38.7 3.5 %collective-permute-start.6 = (bf16[4,640]{1,0:T(4,128)(2,1)S(1)}, bf16[4,640]{1,0:T(4,128)(2,1)S(1)}, u32[]{:S(2)}, u32[]{:S(2)}) collective-permute-start(bf16[4,640]{1,0:T(4,128)(2,1)S(1)} %pad_maximum_fusion.2), channel_id=1, source_target_pairs={{1,0},{2,1},{3,2},{0,3},{5,4},{6,5},{7,6},{4,7},{9,8},{10,9},{11,1... | collective-permute-start | bytes 15368 | tf_op jit(solution)/shard_map/ppermute | solution.py:640
  39.9 3.1 %collective-permute-start.5 = (bf16[4,640]{1,0:T(4,128)(2,1)S(1)}, bf16[4,640]{1,0:T(4,128)(2,1)S(1)}, u32[]{:S(2)}, u32[]{:S(2)}) collective-permute-start(bf16[4,640]{1,0:T(4,128)(2,1)S(1)} %pad_maximum_fusion.1), channel_id=1, source_target_pairs={{0,1},{1,2},{2,3},{3,0},{4,5},{5,6},{6,7},{7,4},{8,9},{9,10},{10,1... | collective-permute-start | bytes 15368 | tf_op jit(solution)/shard_map/ppermute | solution.py:637
  41.0 15.7 %copy-start.2 = (bf16[2,640,160]{1,2,0:T(8,128)(2,1)S(1)}, bf16[2,640,160]{1,2,0:T(8,128)(2,1)}, u32[]{:S(2)}) copy-start(bf16[2,640,160]{1,2,0:T(8,128)(2,1)} %param.13) | copy-start | bytes 1228804
  41.1 15.6 %collective-permute-start.8 = (bf16[2,160,640]{2,1,0:T(8,128)(2,1)S(1)}, bf16[2,160,640]{2,1,0:T(8,128)(2,1)S(1)}, u32[]{:S(2)}, u32[]{:S(2)}) collective-permute-start(bf16[2,160,640]{2,1,0:T(8,128)(2,1)S(1)} %collective-permute-done.mix_c_ref), channel_id=1, source_target_pairs={{0,1},{1,0},{2,3},{3,2},{4,5},{5,4},{6,7},{7,6},{8,9},{9,8},{10,11... | collective-permute-start | bytes 1228808 | tf_op jit(solution)/shard_map/ppermute | solution.py:634
  44.5 0.8 %copy-start.3 = (bf16[368,640]{1,0:T(8,128)(2,1)}, bf16[368,640]{1,0:T(8,128)(2,1)S(1)}, u32[]{:S(2)}) copy-start(bf16[368,640]{1,0:T(8,128)(2,1)S(1)} %get-tuple-element.40.first_ref) | copy-start | bytes 1413124
  56.7 2.1 %collective-permute-start.9 = (bf16[640,512]{1,0:T(8,128)(2,1)S(1)}, bf16[640,512]{1,0:T(8,128)(2,1)S(1)}, u32[]{:S(2)}, u32[]{:S(2)}) collective-permute-start(bf16[640,512]{1,0:T(8,128)(2,1)S(1)} %bitcast.39), channel_id=1, source_target_pairs={{0,1},{1,0},{2,3},{3,2},{4,5},{5,4},{6,7},{7,6},{8,9},{9,8},{10,11... | collective-permute-start | bytes 1966088 | tf_op jit(solution)/shard_map/ppermute | solution.py:660
  56.7 2.1 %copy-start = (bf16[640,1280]{1,0:T(8,128)(2,1)S(1)}, bf16[640,1280]{1,0:T(8,128)(2,1)}, u32[]{:S(2)}) copy-start(bf16[640,1280]{1,0:T(8,128)(2,1)} %expand_ref.1) | copy-start | bytes 4915204
  56.7 2.1 %copy-start.1 = (bf16[1280,640]{1,0:T(8,128)(2,1)S(1)}, bf16[1280,640]{1,0:T(8,128)(2,1)}, u32[]{:S(2)}) copy-start(bf16[1280,640]{1,0:T(8,128)(2,1)} %reduce_ref.1) | copy-start | bytes 4915204
  56.7 2.1 %copy-start.4 = (bf16[368,640]{1,0:T(8,128)(2,1)S(1)}, bf16[368,640]{1,0:T(8,128)(2,1)}, u32[]{:S(2)}) copy-start(bf16[368,640]{1,0:T(8,128)(2,1)} %copy-done.3) | copy-start | bytes 1413124
